TPU v7x, 512 devices: a whole 4x4x16 slice. The times are simulated.
512 devices in a mesh: row: 16 (over x_lo, y, core), col: 32 (over x_hi, z).
Axes of the slice: x: 4 (x_hi: 2, x_lo: 2; x = x_hi * 2 + x_lo), y: 4, z: 16, core: 2. Of those that a mesh axis runs over, the one named last changes fastest.
Arguments:
- seq_ids: int32 [1024], replicated, may hold values from 0 to 3, never falling along the last dimension, each value on 1 to 512 neighbouring positions
- query_inputs: bfloat16 [1024, 8192], P('col', 'row'), may hold values from -6 to 6
- query_grads: bfloat16 [1024, 8192], P('row', 'col'), may hold values from -0.25 to 0.25
- query_act_basis: bfloat16 [8192, 8192], P('row', 'col'), may hold values from -0.0625 to 0.0625
- query_grad_basis: bfloat16 [8192, 8192], P('col', 'row'), may hold values from -0.0625 to 0.0625
- output_inputs: bfloat16 [1024, 8192], P('col', 'row'), may hold values from -6 to 6
- output_grads: bfloat16 [1024, 8192], P('row', 'col'), may hold values from -0.25 to 0.25
- output_act_basis: bfloat16 [8192, 8192], P('row', 'col'), may hold values from -0.0625 to 0.0625
- output_grad_basis: bfloat16 [8192, 8192], P('col', 'row'), may hold values from -0.0625 to 0.0625
Outputs:
- query_corr: float32 [8192, 8192], P('row', 'col')
- output_corr: float32 [8192, 8192], P('row', 'col')
Inputs may be any that keep to these rules, and one draw needn't show every extreme that they name: seq_ids never falls along the tokens; each of the 4 sequences holds 1 to 512 tokens, and one holds exactly 512.
All inputs are finite; a program needn't handle non-finite values.
Results may differ from a plain program's by a relative error of at most 0.0003.
Values may be sent and summed in bfloat16 or wider, within the bound.
No kernel may reach another device: no remote copies, remote signals or barrier semaphores. Data moves between devices by JAX's collectives and lax.ppermute only.
A program may use at most 64 MiB of HBM per device.

v0:
```python
import jax
import jax.numpy as jnp
from jax import lax
from jax.sharding import PartitionSpec as P

SEQS = 4
MOST = 512


def gather_act(inputs_now):
    return lax.all_gather(inputs_now, "col", axis=0, tiled=True)


def gather_grad(grads_now):
    return lax.all_gather(grads_now, "row", axis=0, tiled=True)


def reduce_act(partial_value):
    return lax.psum(partial_value, "row")


def reduce_grad(partial_value):
    return lax.psum(partial_value, "col")


def correct(act_rot, grad_rot, seq_ids):
    numbers = jnp.arange(SEQS, dtype=jnp.int32)
    counts = jnp.sum((seq_ids[None, :] == numbers[:, None]).astype(jnp.int32), axis=1)
    starts = jnp.cumsum(counts) - counts
    padded_act = jnp.concatenate([act_rot, jnp.zeros((MOST, act_rot.shape[1]), act_rot.dtype)], 0)
    padded_grad = jnp.concatenate(
        [grad_rot, jnp.zeros((MOST, grad_rot.shape[1]), grad_rot.dtype)], 0
    )
    offsets = jnp.arange(MOST, dtype=jnp.int32)
    running = jnp.zeros((grad_rot.shape[1], act_rot.shape[1]), jnp.float32)
    for seq_index in range(SEQS):
        act_rows = lax.dynamic_slice_in_dim(padded_act, starts[seq_index], MOST, 0)
        grad_rows = lax.dynamic_slice_in_dim(padded_grad, starts[seq_index], MOST, 0)
        inside = offsets < counts[seq_index]
        grad_rows = jnp.where(inside[:, None], grad_rows, jnp.zeros_like(grad_rows))
        product = lax.dot_general(
            grad_rows, act_rows, (((0,), (0,)), ((), ())), precision=lax.Precision.HIGHEST
        )
        running = running + product * product
    return running / SEQS


def act_term(gathered_act, act_eigen):
    return jnp.dot(gathered_act, act_eigen, preferred_element_type=jnp.float32)


def grad_term(gathered_grad, grad_eigen):
    return jnp.dot(gathered_grad, grad_eigen, preferred_element_type=jnp.float32)


def finish(seq_ids, gathered_act, gathered_grad, act_eigen, grad_eigen):
    act_rot = reduce_act(act_term(gathered_act, act_eigen))
    grad_rot = reduce_grad(grad_term(gathered_grad, grad_eigen))
    return correct(act_rot, grad_rot, seq_ids)


def per_device(
    seq_ids,
    query_inputs,
    query_grads,
    query_act_basis,
    query_grad_basis,
    output_inputs,
    output_grads,
    output_act_basis,
    output_grad_basis,
):
    projections = (
        (query_inputs, query_grads, query_act_basis, query_grad_basis),
        (output_inputs, output_grads, output_act_basis, output_grad_basis),
    )
    results = []
    for inputs_now, grads_now, act_eigen, grad_eigen in projections:
        results.append(
            finish(seq_ids, gather_act(inputs_now), gather_grad(grads_now), act_eigen, grad_eigen)
        )
    return (results[0], results[1])


def solution(mesh):
    in_specs = (
        P(),
        P("col", "row"),
        P("row", "col"),
        P("row", "col"),
        P("col", "row"),
        P("col", "row"),
        P("row", "col"),
        P("row", "col"),
        P("col", "row"),
    )
    out_specs = (P("row", "col"), P("row", "col"))
    return jax.shard_map(
        per_device, mesh=mesh, in_specs=in_specs, out_specs=out_specs, check_vma=False
    )
```

profile of v0, /device:TPU:6, one launch (start us, length us, event | category | flops | bytes accessed | tf_op | source)
XLA Modules:
  0.0 779.2 jit_solution(2244642291569405733)
XLA Ops:
  7.2 0.0 copy-start
  7.2 0.0 copy-start.5
  7.2 0.0 all-gather.3.cloned.1.call-start
  7.2 0.7 all-gather.3.cloned.1.call-update
  7.9 0.0 all-gather.5.cloned.1.call-start
  8.0 0.7 all-gather.5.cloned.1.call-update
  8.7 0.0 all-reduce.11.cloned.1.call-start
  8.7 148.3 %all-gather.3.cloned.1.call-done = bf16[1024,512]{1,0:T(8,128)(2,1)} async-done(((bf16[32,512]{1,0:T(8,128)(2,1)}), bf16[1024,512]{1,0:T(8,128)(2,1)}) %all-gather.3.cloned.1.call-update) | async-done | bytes 1048592 | tf_op jit(solution)/shard_map/all_gather | solution.py:11
  157.0 2.7 fusion.59
  159.7 137.7 %all-gather.5.cloned.1.call-done = bf16[1024,512]{1,0:T(8,128)(2,1)} async-done(((bf16[32,512]{1,0:T(8,128)(2,1)}), bf16[1024,512]{1,0:T(8,128)(2,1)}) %all-gather.5.cloned.1.call-update) | async-done | bytes 1048592 | tf_op jit(solution)/shard_map/all_gather | solution.py:11
  297.5 0.0 copy-done.5
  297.5 2.7 fusion.61
  300.1 0.0 all-reduce.11.cloned.1.call-update
  300.1 0.0 copy-start.6
  300.2 0.0 all-reduce.9.cloned.1.call-start
  300.2 0.0 copy-done.7
  300.2 19.8 %all_gather.12 = bf16[1024,256]{1,0:T(8,128)(2,1)S(1)} all-gather(bf16[64,256]{1,0:T(8,128)(2,1)S(1)} %copy-done.7), channel_id=1, replica_groups=mesh['row'=16,'col'=32] {'row'}, dimensions={0}, use_global_device_ids=true | all-gather | bytes 557056 | tf_op jit(solution)/shard_map/all_gather | solution.py:15
  320.0 0.0 copy-done.8
  320.0 17.7 %all_gather.14 = bf16[1024,256]{1,0:T(8,128)(2,1)S(1)} all-gather(bf16[64,256]{1,0:T(8,128)(2,1)S(1)} %copy-done.8), channel_id=1, replica_groups=mesh['row'=16,'col'=32] {'row'}, dimensions={0}, use_global_device_ids=true | all-gather | bytes 557056 | tf_op jit(solution)/shard_map/all_gather | solution.py:15
  337.7 0.0 copy-done
  337.7 1.8 fusion.58
  339.5 1.8 fusion.60
  341.3 0.0 all-reduce.9.cloned.1.call-update
  341.3 0.7 copy-done.9
  341.9 0.1 convert_reduce_fusion
  342.1 0.2 reduce-window.9
  342.2 0.7 fusion.57
  350.8 0.7 fusion.56
  351.4 0.6 iota_compare_fusion.3
  352.0 0.7 iota_compare_fusion.4
  352.8 0.7 iota_compare_fusion.2
  353.4 0.7 iota_compare_fusion.1
  354.1 81.2 %all-reduce.11.cloned.1.call-done = (f32[1024,256]{1,0:T(8,128)}, f32[1024,256]{1,0:T(8,128)}) async-done(((f32[1024,256]{1,0:T(8,128)}, f32[1024,256]{1,0:T(8,128)}), (f32[1024,256]{1,0:T(8,128)}, f32[1024,256]{1,0:T(8,128)})) %all-reduce.11.cloned.1.call-update) | async-done | bytes 2097168 | tf_op jit(solution)/shard_map/psum | solution.py:19
  435.3 318.5 %all-reduce.9.cloned.1.call-done = (f32[1024,512]{1,0:T(8,128)}, f32[1024,512]{1,0:T(8,128)}) async-done(((f32[1024,512]{1,0:T(8,128)}, f32[1024,512]{1,0:T(8,128)}), (f32[1024,512]{1,0:T(8,128)}, f32[1024,512]{1,0:T(8,128)})) %all-reduce.9.cloned.1.call-update) | async-done | bytes 4194320 | tf_op jit(solution)/shard_map/psum | solution.py:23
  753.8 3.4 convolution_multiply_fusion.6
  757.2 0.0 copy-start.2
  757.2 0.0 copy-start.4
  757.2 0.0 copy-done.3
  757.2 0.0 copy-done.1
  757.2 2.0 convolution_multiply_fusion.2
  759.2 0.0 copy-done.2
  759.2 0.0 copy-done.4
  759.2 1.9 fusion
  761.2 1.9 fusion.3
  763.1 1.9 fusion.1
  765.1 2.1 fusion.4
  767.2 2.7 fusion.7
  770.0 2.7 fusion.6
  (7 shorter events, 0.0 us)
Async XLA Ops:
  7.2 330.5 %copy-start = (bf16[256,512]{1,0:T(8,128)(2,1)S(1)}, bf16[256,512]{1,0:T(8,128)(2,1)}, u32[]{:S(2)}) copy-start(bf16[256,512]{1,0:T(8,128)(2,1)} %param.13) | copy-start | bytes 786436
  7.2 290.3 %copy-start.5 = (bf16[512,256]{1,0:T(8,128)(2,1)S(1)}, bf16[512,256]{1,0:T(8,128)(2,1)}, u32[]{:S(2)}) copy-start(bf16[512,256]{1,0:T(8,128)(2,1)} %param.16) | copy-start | bytes 786436
  7.2 149.8 %all-gather.3.cloned.1.call-start = ((), (), s32[]{:S(2)}) async-start(), calls=%async_computation | async-start | bytes 1081344 | tf_op jit(solution)/shard_map/all_gather | solution.py:11
  7.9 289.5 %all-gather.5.cloned.1.call-start = ((), (), s32[]{:S(2)}) async-start(), calls=%async_computation.1 | async-start | bytes 1081344 | tf_op jit(solution)/shard_map/all_gather | solution.py:11
  8.7 426.6 %all-reduce.11.cloned.1.call-start = ((), (), s32[]{:S(2)}) async-start(), calls=%async_computation.3 | async-start | bytes 4194304 | tf_op jit(solution)/shard_map/psum | solution.py:19
  159.7 140.5 %copy-start.7 = (bf16[64,256]{1,0:T(8,128)(2,1)S(1)}, bf16[64,256]{1,0:T(8,128)(2,1)}, u32[]{:S(2)}) copy-start(bf16[64,256]{1,0:T(8,128)(2,1)} %param.11) | copy-start | bytes 98308
  159.7 160.3 %copy-start.8 = (bf16[64,256]{1,0:T(8,128)(2,1)S(1)}, bf16[64,256]{1,0:T(8,128)(2,1)}, u32[]{:S(2)}) copy-start(bf16[64,256]{1,0:T(8,128)(2,1)} %param.15) | copy-start | bytes 98308
  300.1 39.3 %copy-start.6 = (bf16[256,512]{1,0:T(8,128)(2,1)S(1)}, bf16[256,512]{1,0:T(8,128)(2,1)}, u32[]{:S(2)}) copy-start(bf16[256,512]{1,0:T(8,128)(2,1)} %param.17) | copy-start | bytes 786436
  300.2 453.6 %all-reduce.9.cloned.1.call-start = ((), (), s32[]{:S(2)}) async-start(), calls=%async_computation.2 | async-start | bytes 8388608 | tf_op jit(solution)/shard_map/psum | solution.py:23
  341.3 0.7 copy-start.9
  435.3 321.9 %copy-start.3 = (f32[1024,256]{1,0:T(8,128)S(1)}, f32[1024,256]{1,0:T(8,128)}, u32[]{:S(2)}) copy-start(f32[1024,256]{1,0:T(8,128)} %get-tuple-element.5) | copy-start | bytes 3145732
  753.8 3.5 copy-start.1
  757.2 2.0 copy-start.2
  757.2 2.0 copy-start.4
Sparse Core Ops, SparseCore 0:
  11.1 145.8 all-gather.2
  160.1 137.2 all-gather.4
  300.4 134.7 all-reduce.10
  438.1 315.5 all-reduce.8
where the time goes:
time: 781 us; the launch traced here: 779 us
  waiting for transfers between devices  687 us (88%)
  blocking collectives  37.5 us (5%)
  matrix products  27.7 us (4%)
  between operations  21.8 us (3%)
    psum x1, waiting for transfers between devices, reduce_grad(): return lax.psum(partial_value, 'col')  318 us
    all_gather x2, waiting for transfers between devices, gather_act(): return lax.all_gather(inputs_now, 'col', axis=0, tiled=True)  286 us
    psum x1, waiting for transfers between devices, reduce_act(): return lax.psum(partial_value, 'row')  81.2 us
    all_gather x2, blocking collectives, gather_grad(): return lax.all_gather(grads_now, 'row', axis=0, tiled=True)  37.5 us
    dot_general x8, matrix products, correct(): lax.dot_general(grad_rows, act_rows, (((0,), (0,)), ((), ())), precision=...  18.8 us
  transfers between devices with their start and end apart: 4, of which 4 were waited for; matrix products, arithmetic and copies ran while one was open for 1% of the time, Pallas kernels for 0%

commit v1 on v0

v1 whole, which is shorter than its diff:
```python
import jax
import jax.numpy as jnp
from jax import lax
from jax.sharding import Mesh, PartitionSpec as P

SEQS = 4
ROW = ("xl", "y", "c")
Z = ("zh", "zl")
PLANE = ("xh", "xl", "y", "c")
NZ = 16
NEAR = (0, 1, -1, 2)
FAR = (0, 4, -4, 8)
TOP = 32000.0


def shift(x, by):
    if by == 0:
        return x
    return lax.ppermute(x, Z, [(i, (i + by) % NZ) for i in range(NZ)])


def swap_half(x):
    return lax.ppermute(x, "xh", [(0, 1), (1, 0)])


def pack(x):
    b, p, t, n = x.shape
    most = jnp.max(jnp.abs(x), axis=(2, 3), keepdims=True)
    step = jnp.ceil(jnp.log2(jnp.maximum(most, 1e-30)) * 64.0)
    codes = jnp.round(x * (TOP * jnp.exp2(step * (-1.0 / 64.0)))).astype(jnp.int16)
    head = jnp.broadcast_to(step.astype(jnp.int16), (b, p, 4, n))
    return jnp.concatenate([codes.reshape(b, p * t, n), head.reshape(b, 8, n)], axis=1)


def unpack(w):
    b, rows, n = w.shape
    t = (rows - 8) // 2
    step = jnp.stack([w[:, rows - 8, :1], w[:, rows - 4, :1]], axis=1).astype(jnp.float32)
    scale = jnp.exp2(step * (1.0 / 64.0)) * (1.0 / TOP)
    return w[:, : 2 * t].reshape(b, 2, t, n).astype(jnp.float32) * scale[..., None]


def roll_blocks(x, by):
    return lax.dynamic_slice_in_dim(jnp.concatenate([x, x], 0), by, x.shape[0], 0)


def reduce_scatter_z(part):
    def group(near):
        return jnp.stack([part[(near + far) % NZ] for far in FAR])

    total = group(0)
    for near in NEAR[1:]:
        total = total + unpack(shift(pack(group(near)), near))
    result = total[0]
    for index, far in enumerate(FAR[1:]):
        result = result + unpack(shift(pack(total[index + 1:index + 2]), far))[0]
    return result


def gather_z(w):
    level = jnp.concatenate([shift(w, far) for far in FAR], 0)
    both = jnp.concatenate([shift(level, near) for near in NEAR], 0)
    offsets = [(near + far) % NZ for near in NEAR for far in FAR]
    order = [offsets.index(i) for i in range(NZ)]
    return jnp.concatenate([both[k:k + 1] for k in order], 0)


def correct(act_rot, grad_rot, seq_ids):
    running = jnp.zeros((grad_rot.shape[1], act_rot.shape[1]), jnp.float32)
    for seq in range(SEQS):
        grad_rows = jnp.where((seq_ids == seq)[:, None], grad_rot, 0.0)
        product = lax.dot_general(
            grad_rows, act_rot, (((0,), (0,)), ((), ())), precision=lax.Precision.HIGH
        )
        running = running + product * product
    return running / SEQS


def dot(a, b):
    return jnp.dot(a, b, preferred_element_type=jnp.float32)


def per_device(seq_ids, qx, qg, qa, qb, ox, og, oa, ob):
    z = lax.axis_index(Z)
    xh = lax.axis_index("xh")
    mine_first = xh == 0

    grads = jnp.stack([qg, og])
    sent = jnp.transpose(grads.reshape(2, 2, 32, 256), (1, 0, 2, 3))
    sent = jnp.broadcast_to(sent[:, None], (2, 16, 2, 32, 256)).reshape(32, 2, 32, 256)
    got = lax.all_to_all(sent, PLANE, split_axis=0, concat_axis=0, tiled=True)
    grad_basis = jnp.stack([qb, ob])
    grad_other = swap_half(grad_basis)
    inputs = lax.all_gather(jnp.stack([qx, ox])[None], Z, axis=0, tiled=True)
    act_basis = jnp.stack([qa, oa])
    act_other = swap_half(act_basis)

    got = got.reshape(2, 16, 2, 32, 256)
    g0 = roll_blocks(got[0], z)
    g1 = roll_blocks(got[1], z)
    b0 = jnp.where(mine_first, grad_basis, grad_other)
    b1 = jnp.where(mine_first, grad_other, grad_basis)
    parts = []
    for p in range(2):
        part = dot(g0[:, p].reshape(512, 256), b0[p]) + dot(g1[:, p].reshape(512, 256), b1[p])
        parts.append(part.reshape(16, 32, 512))
    part = jnp.stack(parts, 1)
    grad_mine = reduce_scatter_z(part)
    words = gather_z(pack(grad_mine[None]))
    others = swap_half(words)

    a0 = jnp.where(mine_first, act_basis, act_other)
    a1 = jnp.where(mine_first, act_other, act_basis)
    parts = []
    for p in range(2):
        rows = inputs[:, p].reshape(512, 512)
        part = jnp.concatenate([dot(rows, a0[p]), dot(rows, a1[p])], 1)
        parts.append(part.reshape(16, 32, 512))
    act_words = pack(jnp.stack(parts, 1))
    act_words = lax.all_to_all(act_words, ROW, split_axis=0, concat_axis=0, tiled=True)
    act_mine = jnp.sum(unpack(act_words), axis=0)
    act_sent = pack(jnp.stack([act_mine[:, :, :256], act_mine[:, :, 256:]]))
    act_sent = jnp.broadcast_to(act_sent[:, None], (2, 16, 72, 256)).reshape(32, 72, 256)
    act_words = lax.all_to_all(act_sent, PLANE, split_axis=0, concat_axis=0, tiled=True)
    act = jnp.transpose(unpack(act_words), (1, 0, 2, 3)).reshape(2, 1024, 256)

    low = jnp.where(mine_first, words, others)
    high = jnp.where(mine_first, others, words)
    both = jnp.stack([low, high])
    both = lax.rev(both, (1,))
    both = lax.dynamic_slice_in_dim(jnp.concatenate([both, both], 1), NZ - 1 - z, NZ, 1)
    grad = unpack(both.reshape(32, 72, 512)).reshape(2, 16, 2, 32, 512)
    grad = jnp.transpose(grad, (2, 1, 0, 3, 4)).reshape(2, 1024, 512)
    return correct(act[0], grad[0], seq_ids), correct(act[1], grad[1], seq_ids)


def solution(mesh):
    fine = Mesh(mesh.devices.reshape(2, 4, 2, 2, 4, 4), ("xl", "y", "c", "xh", "zh", "zl"))
    row, col = ROW, ("xh",) + Z
    in_specs = (P(), P(col, row), P(row, col), P(row, col), P(col, row)) + (
        P(col, row),
        P(row, col),
        P(row, col),
        P(col, row),
    )
    out_specs = (P(row, col), P(row, col))
    return jax.shard_map(
        per_device, mesh=fine, in_specs=in_specs, out_specs=out_specs, check_vma=False
    )
```

time: 781 us -> 299 us (0.38)
  waiting for transfers between devices: 687 us -> 89 us
  starting transfers between devices: 0.16 us -> 96 us
  local copies, waits for them, and re-layouts: 2.01 us -> 48.1 us
  blocking collectives: 37.5 us -> 0 us
  other arithmetic: 2.94 us -> 27.5 us
  matrix products: 27.7 us -> 19.3 us
    psum x2 -> x0, waiting for transfers between devices: 400 us -> none  [the longest x1 318 us: reduce_grad(): return lax.psum(partial_value, 'col')]
    all_gather x2 -> x1, waiting for transfers between devices: 286 us -> 39.8 us  [per_device(): inputs = lax.all_gather(jnp.stack([qx, ox])[None], Z, axis=0, tiled=True)]
    ppermute x0 -> x15, starting transfers between devices: none -> 74 us  [the longest x12 62.6 us: shift(): return lax.ppermute(x, Z, [(i, (i + by) % NZ) for i in range(NZ)])]
    ppermute x0 -> x15, waiting for transfers between devices: none -> 44.2 us  [the longest x12 27.1 us: shift(): return lax.ppermute(x, Z, [(i, (i + by) % NZ) for i in range(NZ)])]
    all_gather x2 -> x0, blocking collectives: 37.5 us -> none  [gather_grad(): return lax.all_gather(grads_now, 'row', axis=0, tiled=True)]
    all_to_all x0 -> x3, starting transfers between devices: none -> 22 us  [the longest x1 9.59 us: per_device(): got = lax.all_to_all(sent, PLANE, split_axis=0, concat_axis=0, tiled=True)]
    select_n x0 -> x8, local copies, waits for them, and re-layouts: none -> 11.3 us  [correct(): grad_rows = jnp.where((seq_ids == seq)[:, None], grad_rot, 0.0)]
    slice x2 -> x23, local copies, waits for them, and re-layouts: 1.31 us -> 10.8 us  [the longest x9 6.35 us: unpack(): w[:, rows - 8, :1]]
  transfers between devices with their start and end apart: 4 -> 19, of which waited for: 4 -> 11; matrix products, arithmetic and copies ran while one was open for 1% -> 23% of each run, Pallas kernels for 0% -> 0%
where the time goes in v1:
time: 299 us; the launch traced here: 295 us
  starting transfers between devices  96 us (32%)
  waiting for transfers between devices  89 us (30%)
  local copies, waits for them, and re-layouts  48.1 us (16%)
  other arithmetic  27.5 us (9%)
  matrix products  19.3 us (6%)
  between operations  15 us (5%)
    ppermute x12, starting transfers between devices, shift(): return lax.ppermute(x, Z, [(i, (i + by) % NZ) for i in range(NZ)])  62.6 us
    all_gather x1, waiting for transfers between devices, per_device(): inputs = lax.all_gather(jnp.stack([qx, ox])[None], Z, axis=0, tiled=True)  39.8 us
    ppermute x12, waiting for transfers between devices, shift(): return lax.ppermute(x, Z, [(i, (i + by) % NZ) for i in range(NZ)])  27.1 us
    ppermute x3, waiting for transfers between devices, swap_half(): return lax.ppermute(x, 'xh', [(0, 1), (1, 0)])  17.1 us
    dot_general x8, matrix products, correct(): lax.dot_general(grad_rows, act_rot, (((0,), (0,)), ((), ())), precision=l...  16.8 us
    ppermute x3, starting transfers between devices, swap_half(): return lax.ppermute(x, 'xh', [(0, 1), (1, 0)])  11.3 us
    select_n x8, local copies, waits for them, and re-layouts, correct(): grad_rows = jnp.where((seq_ids == seq)[:, None], grad_rot, 0.0)  11.3 us
    all_to_all x1, starting transfers between devices, per_device(): got = lax.all_to_all(sent, PLANE, split_axis=0, concat_axis=0, tiled=True)  9.59 us
  transfers between devices with their start and end apart: 19, of which 11 were waited for; matrix products, arithmetic and copies ran while one was open for 23% of the time, Pallas kernels for 0%

profile of v1, /device:TPU:6, one launch (start us, length us, event | category | flops | bytes accessed | tf_op | source)
XLA Modules:
  0.0 295.0 jit_solution(14725430089309707744)
XLA Ops:
  9.2 9.6 %all-to-all-start = ((bf16[32,2,32,256]{3,2,1,0:T(8,128)(2,1)}), bf16[32,2,32,256]{3,2,1,0:T(8,128)(2,1)S(1)}, u32[]{:S(2)}, u32[]{:S(2)}) async-start(bf16[32,2,32,256]{3,2,1,0:T(8,128)(2,1)} %bitcast.3), calls=%async_computation | async-start | bytes 2097152 | tf_op jit(solution)/shard_map/all_to_all | solution.py:91
  18.9 3.3 %collective-permute-start = (bf16[2,256,512]{2,1,0:T(8,128)(2,1)S(1)}, bf16[2,256,512]{2,1,0:T(8,128)(2,1)}, u32[]{:S(2)}, u32[]{:S(2)}) collective-permute-start(bf16[2,256,512]{2,1,0:T(8,128)(2,1)S(1)} %pad_maximum_fusion.3), channel_id=1, source_target_pairs={{0,16},{16,0},{1,17},{17,1},{2,18},{18,2},{3,19},{19,3},{4,20},{20... | collective-permute-start | bytes 1572872 | tf_op jit(solution)/shard_map/ppermute | solution.py:23
  23.0 4.1 %collective-permute-start.14 = (bf16[2,512,256]{2,1,0:T(8,128)(2,1)}, bf16[2,512,256]{2,1,0:T(8,128)(2,1)}, u32[]{:S(2)}, u32[]{:S(2)}) collective-permute-start(bf16[2,512,256]{2,1,0:T(8,128)(2,1)} %pad_maximum_fusion.4), channel_id=1, source_target_pairs={{0,16},{16,0},{1,17},{17,1},{2,18},{18,2},{3,19},{19,3},{4,20},{20... | collective-permute-start | bytes 1572872 | tf_op jit(solution)/shard_map/ppermute | solution.py:23
  27.1 17.1 %collective-permute-done = bf16[2,256,512]{2,1,0:T(8,128)(2,1)} collective-permute-done((bf16[2,256,512]{2,1,0:T(8,128)(2,1)S(1)}, bf16[2,256,512]{2,1,0:T(8,128)(2,1)}, u32[]{:S(2)}, u32[]{:S(2)}) %collective-permute-start) | collective-permute-done | bytes 524320 | tf_op jit(solution)/shard_map/ppermute | solution.py:23
  48.1 3.3 %collective-permute-start.3 = (s16[4,72,512]{2,1,0:T(8,128)(2,1)S(1)}, s16[4,72,512]{2,1,0:T(8,128)(2,1)S(1)}, u32[]{:S(2)}, u32[]{:S(2)}) collective-permute-start(s16[4,72,512]{2,1,0:T(8,128)(2,1)S(1)} %pad_add_fusion.4), channel_id=1, source_target_pairs={{0,2},{1,3},{2,4},{3,5},{4,6},{5,7},{6,8},{7,9},{8,10},{9,11},{10,... | collective-permute-start | bytes 884744 | tf_op jit(solution)/shard_map/ppermute | solution.py:19
  52.1 8.1 %collective-permute-start.2 = (s16[4,72,512]{2,1,0:T(8,128)(2,1)S(1)}, s16[4,72,512]{2,1,0:T(8,128)(2,1)S(1)}, u32[]{:S(2)}, u32[]{:S(2)}) collective-permute-start(s16[4,72,512]{2,1,0:T(8,128)(2,1)S(1)} %pad_add_fusion.3), channel_id=1, source_target_pairs={{0,15},{1,0},{2,1},{3,2},{4,3},{5,4},{6,5},{7,6},{8,7},{9,8},{10,9... | collective-permute-start | bytes 884744 | tf_op jit(solution)/shard_map/ppermute | solution.py:19
  61.0 1.9 collective-permute-start.1
  62.9 4.5 %collective-permute-done.3 = s16[4,72,512]{2,1,0:T(8,128)(2,1)S(1)} collective-permute-done((s16[4,72,512]{2,1,0:T(8,128)(2,1)S(1)}, s16[4,72,512]{2,1,0:T(8,128)(2,1)S(1)}, u32[]{:S(2)}, u32[]{:S(2)}) %collective-permute-start.3) | collective-permute-done | bytes 294944 | tf_op jit(solution)/shard_map/ppermute | solution.py:19
  68.1 8.5 %collective-permute-done.1 = s16[4,72,512]{2,1,0:T(8,128)(2,1)} collective-permute-done((s16[4,72,512]{2,1,0:T(8,128)(2,1)S(1)}, s16[4,72,512]{2,1,0:T(8,128)(2,1)}, u32[]{:S(2)}, u32[]{:S(2)}) %collective-permute-start.1) | collective-permute-done | bytes 294944 | tf_op jit(solution)/shard_map/ppermute | solution.py:19
  79.8 9.6 %collective-permute-start.6 = (s16[1,72,512]{2,1,0:T(8,128)(2,1)S(1)}, s16[1,72,512]{2,1,0:T(8,128)(2,1)S(1)}, u32[]{:S(2)}, u32[]{:S(2)}) collective-permute-start(s16[1,72,512]{2,1,0:T(8,128)(2,1)S(1)} %pad_add_fusion.8), channel_id=1, source_target_pairs={{0,8},{1,9},{2,10},{3,11},{4,12},{5,13},{6,14},{7,15},{8,0},{9,1},... | collective-permute-start | bytes 221192 | tf_op jit(solution)/shard_map/ppermute | solution.py:19
  89.8 1.9 collective-permute-start.5
  92.0 7.8 %collective-permute-start.4 = (s16[1,72,512]{2,1,0:T(8,128)(2,1)S(1)}, s16[1,72,512]{2,1,0:T(8,128)(2,1)S(1)}, u32[]{:S(2)}, u32[]{:S(2)}) collective-permute-start(s16[1,72,512]{2,1,0:T(8,128)(2,1)S(1)} %pad_add_fusion.6), channel_id=1, source_target_pairs={{0,4},{1,5},{2,6},{3,7},{4,8},{5,9},{6,10},{7,11},{8,12},{9,13},{1... | collective-permute-start | bytes 221192 | tf_op jit(solution)/shard_map/ppermute | solution.py:19
  108.7 9.3 %collective-permute-start.9 = (s16[1,72,512]{2,1,0:T(8,128)(2,1)S(1)}, s16[1,72,512]{2,1,0:T(8,128)(2,1)S(1)}, u32[]{:S(2)}, u32[]{:S(2)}) collective-permute-start(s16[1,72,512]{2,1,0:T(8,128)(2,1)S(1)} %get-tuple-element.74), channel_id=1, source_target_pairs={{0,8},{1,9},{2,10},{3,11},{4,12},{5,13},{6,14},{7,15},{8,0},{9,1},... | collective-permute-start | bytes 221192 | tf_op jit(solution)/shard_map/ppermute | solution.py:19
  118.0 4.2 %collective-permute-start.8 = (s16[1,72,512]{2,1,0:T(8,128)(2,1)S(1)}, s16[1,72,512]{2,1,0:T(8,128)(2,1)S(1)}, u32[]{:S(2)}, u32[]{:S(2)}) collective-permute-start(s16[1,72,512]{2,1,0:T(8,128)(2,1)S(1)} %get-tuple-element.74), channel_id=1, source_target_pairs={{0,12},{1,13},{2,14},{3,15},{4,0},{5,1},{6,2},{7,3},{8,4},{9,5},{1... | collective-permute-start | bytes 221192 | tf_op jit(solution)/shard_map/ppermute | solution.py:19
  122.2 5.5 %collective-permute-start.7 = (s16[1,72,512]{2,1,0:T(8,128)(2,1)S(1)}, s16[1,72,512]{2,1,0:T(8,128)(2,1)S(1)}, u32[]{:S(2)}, u32[]{:S(2)}) collective-permute-start(s16[1,72,512]{2,1,0:T(8,128)(2,1)S(1)} %get-tuple-element.74), channel_id=1, source_target_pairs={{0,4},{1,5},{2,6},{3,7},{4,8},{5,9},{6,10},{7,11},{8,12},{9,13},{1... | collective-permute-start | bytes 221192 | tf_op jit(solution)/shard_map/ppermute | solution.py:19
  127.8 3.1 %collective-permute-done.8 = s16[1,72,512]{2,1,0:T(8,128)(2,1)S(1)} collective-permute-done((s16[1,72,512]{2,1,0:T(8,128)(2,1)S(1)}, s16[1,72,512]{2,1,0:T(8,128)(2,1)S(1)}, u32[]{:S(2)}, u32[]{:S(2)}) %collective-permute-start.8) | collective-permute-done | bytes 73760 | tf_op jit(solution)/shard_map/ppermute | solution.py:19
  130.9 1.9 collective-permute-done.7
  132.8 4.3 %collective-permute-start.10 = (s16[4,72,512]{2,1,0:T(8,128)(2,1)S(1)}, s16[4,72,512]{2,1,0:T(8,128)(2,1)S(1)}, u32[]{:S(2)}, u32[]{:S(2)}) collective-permute-start(s16[4,72,512]{2,1,0:T(8,128)(2,1)S(1)} %pad_add_fusion.5), channel_id=1, source_target_pairs={{0,1},{1,2},{2,3},{3,4},{4,5},{5,6},{6,7},{7,8},{8,9},{9,10},{10,1... | collective-permute-start | bytes 884744 | tf_op jit(solution)/shard_map/ppermute | solution.py:19
  137.9 1.9 collective-permute-start.11
  140.9 4.6 %collective-permute-start.12 = (s16[4,72,512]{2,1,0:T(8,128)(2,1)S(1)}, s16[4,72,512]{2,1,0:T(8,128)(2,1)S(1)}, u32[]{:S(2)}, u32[]{:S(2)}) collective-permute-start(s16[4,72,512]{2,1,0:T(8,128)(2,1)S(1)} %pad_add_fusion.5), channel_id=1, source_target_pairs={{0,15},{1,0},{2,1},{3,2},{4,3},{5,4},{6,5},{7,6},{8,7},{9,8},{10,9... | collective-permute-start | bytes 884744 | tf_op jit(solution)/shard_map/ppermute | solution.py:19
  145.5 4.1 %collective-permute-done.10 = s16[4,72,512]{2,1,0:T(8,128)(2,1)S(1)} collective-permute-done((s16[4,72,512]{2,1,0:T(8,128)(2,1)S(1)}, s16[4,72,512]{2,1,0:T(8,128)(2,1)S(1)}, u32[]{:S(2)}, u32[]{:S(2)}) %collective-permute-start.10) | collective-permute-done | bytes 294944 | tf_op jit(solution)/shard_map/ppermute | solution.py:19
  150.3 3.1 %collective-permute-done.11 = s16[4,72,512]{2,1,0:T(8,128)(2,1)S(1)} collective-permute-done((s16[4,72,512]{2,1,0:T(8,128)(2,1)S(1)}, s16[4,72,512]{2,1,0:T(8,128)(2,1)S(1)}, u32[]{:S(2)}, u32[]{:S(2)}) %collective-permute-start.11) | collective-permute-done | bytes 294944 | tf_op jit(solution)/shard_map/ppermute | solution.py:19
  162.3 4.0 %collective-permute-start.13 = (s16[16,72,512]{2,1,0:T(8,128)(2,1)}, s16[16,72,512]{2,1,0:T(8,128)(2,1)}, u32[]{:S(2)}, u32[]{:S(2)}) collective-permute-start(s16[16,72,512]{2,1,0:T(8,128)(2,1)} %slice_dynamic-update-slice_fusion), channel_id=1, source_target_pairs={{0,16},{16,0},{1,17},{17,1},{2,18},{18,2},{3,19},{19,3},{4,20},{20... | collective-permute-start | bytes 3538952 | tf_op jit(solution)/shard_map/ppermute | solution.py:23
  166.3 39.8 %all-gather.3.cloned.1.call-done = bf16[32,32,512]{2,1,0:T(8,128)(2,1)} async-done(((bf16[2,32,512]{2,1,0:T(8,128)(2,1)}), bf16[32,32,512]{2,1,0:T(8,128)(2,1)}) %all-gather.3.cloned.1.call-update) | async-done | bytes 1048592 | tf_op jit(solution)/shard_map/all_gather | solution.py:94
  214.1 2.0 fusion.3
  217.2 5.8 %all-to-all-start.1 = ((s16[16,72,512]{2,1,0:T(8,128)(2,1)}), s16[16,72,512]{2,1,0:T(8,128)(2,1)S(1)}, u32[]{:S(2)}, u32[]{:S(2)}) async-start(s16[16,72,512]{2,1,0:T(8,128)(2,1)} %pad_add_fusion.1), calls=%async_computation.1 | async-start | bytes 2359296 | tf_op jit(solution)/shard_map/all_to_all | solution.py:120
  225.7 2.1 select_bitcast_fusion.1
  228.0 1.6 rev.3
  229.6 2.7 fusion.1
  234.7 4.9 %all-to-all-done.1 = s16[16,72,512]{2,1,0:T(8,128)(2,1)S(1)} async-done(((s16[16,72,512]{2,1,0:T(8,128)(2,1)}), s16[16,72,512]{2,1,0:T(8,128)(2,1)S(1)}, u32[]{:S(2)}, u32[]{:S(2)}) %all-to-all-start.1) | async-done | bytes 1179680 | tf_op jit(solution)/shard_map/all_to_all | solution.py:120
  245.4 6.7 %all-to-all-start.2 = ((s16[32,72,256]{2,1,0:T(8,128)(2,1)}), s16[32,72,256]{2,1,0:T(8,128)(2,1)S(1)}, u32[]{:S(2)}, u32[]{:S(2)}) async-start(s16[32,72,256]{2,1,0:T(8,128)(2,1)} %bitcast.72), calls=%async_computation.2 | async-start | bytes 2359296 | tf_op jit(solution)/shard_map/all_to_all | solution.py:124
  252.1 1.6 slice.404
  253.8 2.3 fusion
  256.2 1.6 slice_select_fusion
  258.0 1.6 copy.117
  259.6 1.6 copy.108
  262.8 1.6 copy.124
  264.3 1.6 copy.123
  265.9 1.6 copy.122
  267.5 1.6 copy.125
  271.1 1.9 convolution_multiply_fusion.5
  273.0 1.9 convolution_multiply_fusion.6
  274.9 1.9 convolution_multiply_fusion.1
  276.8 1.9 convolution_multiply_fusion.2
  278.7 1.9 fusion.6
  280.6 2.9 fusion.8
  283.6 1.9 fusion.10
  285.4 2.7 fusion.12
  (217 shorter events, 56.6 us)
Async XLA Ops:
  7.2 11.6 %copy-start.7 = (bf16[256,512]{1,0:T(8,128)(2,1)S(1)}, bf16[256,512]{1,0:T(8,128)(2,1)}, u32[]{:S(2)}) copy-start(bf16[256,512]{1,0:T(8,128)(2,1)} %param.17) | copy-start | bytes 786436
  7.2 11.6 %copy-start.8 = (bf16[256,512]{1,0:T(8,128)(2,1)S(1)}, bf16[256,512]{1,0:T(8,128)(2,1)}, u32[]{:S(2)}) copy-start(bf16[256,512]{1,0:T(8,128)(2,1)} %param.13) | copy-start | bytes 786436
  8.0 14.1 %copy-start.9 = (bf16[512,256]{1,0:T(8,128)(2,1)S(1)}, bf16[512,256]{1,0:T(8,128)(2,1)}, u32[]{:S(2)}) copy-start(bf16[512,256]{1,0:T(8,128)(2,1)} %param.16) | copy-start | bytes 786436
  8.0 14.1 %copy-start.10 = (bf16[512,256]{1,0:T(8,128)(2,1)S(1)}, bf16[512,256]{1,0:T(8,128)(2,1)}, u32[]{:S(2)}) copy-start(bf16[512,256]{1,0:T(8,128)(2,1)} %param.12) | copy-start | bytes 786436
  9.2 36.2 %all-to-all-start = ((bf16[32,2,32,256]{3,2,1,0:T(8,128)(2,1)}), bf16[32,2,32,256]{3,2,1,0:T(8,128)(2,1)S(1)}, u32[]{:S(2)}, u32[]{:S(2)}) async-start(bf16[32,2,32,256]{3,2,1,0:T(8,128)(2,1)} %bitcast.3), calls=%async_computation | async-start | bytes 2097152 | tf_op jit(solution)/shard_map/all_to_all | solution.py:91
  18.8 187.4 %all-gather.3.cloned.1.call-start = ((), (), s32[]{:S(2)}) async-start(), calls=%async_computation.3 | async-start | bytes 1114112 | tf_op jit(solution)/shard_map/all_gather | solution.py:94
  18.9 25.4 %collective-permute-start = (bf16[2,256,512]{2,1,0:T(8,128)(2,1)S(1)}, bf16[2,256,512]{2,1,0:T(8,128)(2,1)}, u32[]{:S(2)}, u32[]{:S(2)}) collective-permute-start(bf16[2,256,512]{2,1,0:T(8,128)(2,1)S(1)} %pad_maximum_fusion.3), channel_id=1, source_target_pairs={{0,16},{16,0},{1,17},{17,1},{2,18},{18,2},{3,19},{19,3},{4,20},{20... | collective-permute-start | bytes 1572872 | tf_op jit(solution)/shard_map/ppermute | solution.py:23
  23.0 116.8 %collective-permute-start.14 = (bf16[2,512,256]{2,1,0:T(8,128)(2,1)}, bf16[2,512,256]{2,1,0:T(8,128)(2,1)}, u32[]{:S(2)}, u32[]{:S(2)}) collective-permute-start(bf16[2,512,256]{2,1,0:T(8,128)(2,1)} %pad_maximum_fusion.4), channel_id=1, source_target_pairs={{0,16},{16,0},{1,17},{17,1},{2,18},{18,2},{3,19},{19,3},{4,20},{20... | collective-permute-start | bytes 1572872 | tf_op jit(solution)/shard_map/ppermute | solution.py:23
  48.1 19.3 %collective-permute-start.3 = (s16[4,72,512]{2,1,0:T(8,128)(2,1)S(1)}, s16[4,72,512]{2,1,0:T(8,128)(2,1)S(1)}, u32[]{:S(2)}, u32[]{:S(2)}) collective-permute-start(s16[4,72,512]{2,1,0:T(8,128)(2,1)S(1)} %pad_add_fusion.4), channel_id=1, source_target_pairs={{0,2},{1,3},{2,4},{3,5},{4,6},{5,7},{6,8},{7,9},{8,10},{9,11},{10,... | collective-permute-start | bytes 884744 | tf_op jit(solution)/shard_map/ppermute | solution.py:19
  52.1 15.7 %collective-permute-start.2 = (s16[4,72,512]{2,1,0:T(8,128)(2,1)S(1)}, s16[4,72,512]{2,1,0:T(8,128)(2,1)S(1)}, u32[]{:S(2)}, u32[]{:S(2)}) collective-permute-start(s16[4,72,512]{2,1,0:T(8,128)(2,1)S(1)} %pad_add_fusion.3), channel_id=1, source_target_pairs={{0,15},{1,0},{2,1},{3,2},{4,3},{5,4},{6,5},{7,6},{8,7},{9,8},{10,9... | collective-permute-start | bytes 884744 | tf_op jit(solution)/shard_map/ppermute | solution.py:19
  61.0 15.7 %collective-permute-start.1 = (s16[4,72,512]{2,1,0:T(8,128)(2,1)S(1)}, s16[4,72,512]{2,1,0:T(8,128)(2,1)}, u32[]{:S(2)}, u32[]{:S(2)}) collective-permute-start(s16[4,72,512]{2,1,0:T(8,128)(2,1)S(1)} %pad_add_fusion.2), channel_id=1, source_target_pairs={{0,1},{1,2},{2,3},{3,4},{4,5},{5,6},{6,7},{7,8},{8,9},{9,10},{10,1... | collective-permute-start | bytes 884744 | tf_op jit(solution)/shard_map/ppermute | solution.py:19
  79.2 58.0 %copy-start.11 = (bf16[32,512]{1,0:T(8,128)(2,1)S(1)}, bf16[32,512]{1,0:T(8,128)(2,1)}, u32[]{:S(2)}) copy-start(bf16[32,512]{1,0:T(8,128)(2,1)} %param.14) | copy-start | bytes 98308
  79.2 58.0 %copy-start.12 = (bf16[32,512]{1,0:T(8,128)(2,1)S(1)}, bf16[32,512]{1,0:T(8,128)(2,1)}, u32[]{:S(2)}) copy-start(bf16[32,512]{1,0:T(8,128)(2,1)} %param.10) | copy-start | bytes 98308
  79.8 20.1 %collective-permute-start.6 = (s16[1,72,512]{2,1,0:T(8,128)(2,1)S(1)}, s16[1,72,512]{2,1,0:T(8,128)(2,1)S(1)}, u32[]{:S(2)}, u32[]{:S(2)}) collective-permute-start(s16[1,72,512]{2,1,0:T(8,128)(2,1)S(1)} %pad_add_fusion.8), channel_id=1, source_target_pairs={{0,8},{1,9},{2,10},{3,11},{4,12},{5,13},{6,14},{7,15},{8,0},{9,1},... | collective-permute-start | bytes 221192 | tf_op jit(solution)/shard_map/ppermute | solution.py:19
  89.8 13.0 %collective-permute-start.5 = (s16[1,72,512]{2,1,0:T(8,128)(2,1)S(1)}, s16[1,72,512]{2,1,0:T(8,128)(2,1)S(1)}, u32[]{:S(2)}, u32[]{:S(2)}) collective-permute-start(s16[1,72,512]{2,1,0:T(8,128)(2,1)S(1)} %pad_add_fusion.7), channel_id=1, source_target_pairs={{0,12},{1,13},{2,14},{3,15},{4,0},{5,1},{6,2},{7,3},{8,4},{9,5},{1... | collective-permute-start | bytes 221192 | tf_op jit(solution)/shard_map/ppermute | solution.py:19
  92.0 13.5 %collective-permute-start.4 = (s16[1,72,512]{2,1,0:T(8,128)(2,1)S(1)}, s16[1,72,512]{2,1,0:T(8,128)(2,1)S(1)}, u32[]{:S(2)}, u32[]{:S(2)}) collective-permute-start(s16[1,72,512]{2,1,0:T(8,128)(2,1)S(1)} %pad_add_fusion.6), channel_id=1, source_target_pairs={{0,4},{1,5},{2,6},{3,7},{4,8},{5,9},{6,10},{7,11},{8,12},{9,13},{1... | collective-permute-start | bytes 221192 | tf_op jit(solution)/shard_map/ppermute | solution.py:19
  108.7 19.1 %collective-permute-start.9 = (s16[1,72,512]{2,1,0:T(8,128)(2,1)S(1)}, s16[1,72,512]{2,1,0:T(8,128)(2,1)S(1)}, u32[]{:S(2)}, u32[]{:S(2)}) collective-permute-start(s16[1,72,512]{2,1,0:T(8,128)(2,1)S(1)} %get-tuple-element.74), channel_id=1, source_target_pairs={{0,8},{1,9},{2,10},{3,11},{4,12},{5,13},{6,14},{7,15},{8,0},{9,1},... | collective-permute-start | bytes 221192 | tf_op jit(solution)/shard_map/ppermute | solution.py:19
  118.0 12.9 %collective-permute-start.8 = (s16[1,72,512]{2,1,0:T(8,128)(2,1)S(1)}, s16[1,72,512]{2,1,0:T(8,128)(2,1)S(1)}, u32[]{:S(2)}, u32[]{:S(2)}) collective-permute-start(s16[1,72,512]{2,1,0:T(8,128)(2,1)S(1)} %get-tuple-element.74), channel_id=1, source_target_pairs={{0,12},{1,13},{2,14},{3,15},{4,0},{5,1},{6,2},{7,3},{8,4},{9,5},{1... | collective-permute-start | bytes 221192 | tf_op jit(solution)/shard_map/ppermute | solution.py:19
  122.2 10.6 %collective-permute-start.7 = (s16[1,72,512]{2,1,0:T(8,128)(2,1)S(1)}, s16[1,72,512]{2,1,0:T(8,128)(2,1)S(1)}, u32[]{:S(2)}, u32[]{:S(2)}) collective-permute-start(s16[1,72,512]{2,1,0:T(8,128)(2,1)S(1)} %get-tuple-element.74), channel_id=1, source_target_pairs={{0,4},{1,5},{2,6},{3,7},{4,8},{5,9},{6,10},{7,11},{8,12},{9,13},{1... | collective-permute-start | bytes 221192 | tf_op jit(solution)/shard_map/ppermute | solution.py:19
  132.8 16.8 %collective-permute-start.10 = (s16[4,72,512]{2,1,0:T(8,128)(2,1)S(1)}, s16[4,72,512]{2,1,0:T(8,128)(2,1)S(1)}, u32[]{:S(2)}, u32[]{:S(2)}) collective-permute-start(s16[4,72,512]{2,1,0:T(8,128)(2,1)S(1)} %pad_add_fusion.5), channel_id=1, source_target_pairs={{0,1},{1,2},{2,3},{3,4},{4,5},{5,6},{6,7},{7,8},{8,9},{9,10},{10,1... | collective-permute-start | bytes 884744 | tf_op jit(solution)/shard_map/ppermute | solution.py:19
  137.9 15.5 %collective-permute-start.11 = (s16[4,72,512]{2,1,0:T(8,128)(2,1)S(1)}, s16[4,72,512]{2,1,0:T(8,128)(2,1)S(1)}, u32[]{:S(2)}, u32[]{:S(2)}) collective-permute-start(s16[4,72,512]{2,1,0:T(8,128)(2,1)S(1)} %pad_add_fusion.5), channel_id=1, source_target_pairs={{0,2},{1,3},{2,4},{3,5},{4,6},{5,7},{6,8},{7,9},{8,10},{9,11},{10,... | collective-permute-start | bytes 884744 | tf_op jit(solution)/shard_map/ppermute | solution.py:19
  140.9 13.1 %collective-permute-start.12 = (s16[4,72,512]{2,1,0:T(8,128)(2,1)S(1)}, s16[4,72,512]{2,1,0:T(8,128)(2,1)S(1)}, u32[]{:S(2)}, u32[]{:S(2)}) collective-permute-start(s16[4,72,512]{2,1,0:T(8,128)(2,1)S(1)} %pad_add_fusion.5), channel_id=1, source_target_pairs={{0,15},{1,0},{2,1},{3,2},{4,3},{5,4},{6,5},{7,6},{8,7},{9,8},{10,9... | collective-permute-start | bytes 884744 | tf_op jit(solution)/shard_map/ppermute | solution.py:19
  162.3 63.5 %collective-permute-start.13 = (s16[16,72,512]{2,1,0:T(8,128)(2,1)}, s16[16,72,512]{2,1,0:T(8,128)(2,1)}, u32[]{:S(2)}, u32[]{:S(2)}) collective-permute-start(s16[16,72,512]{2,1,0:T(8,128)(2,1)} %slice_dynamic-update-slice_fusion), channel_id=1, source_target_pairs={{0,16},{16,0},{1,17},{17,1},{2,18},{18,2},{3,19},{19,3},{4,20},{20... | collective-permute-start | bytes 3538952 | tf_op jit(solution)/shard_map/ppermute | solution.py:23
  216.1 6.9 %copy-start.17 = (s32[1024]{0:T(1024)S(1)}, s32[1024]{0:T(1024)}, u32[]{:S(2)}) copy-start(s32[1024]{0:T(1024)} %param.9) | copy-start | bytes 12292
  217.2 22.4 %all-to-all-start.1 = ((s16[16,72,512]{2,1,0:T(8,128)(2,1)}), s16[16,72,512]{2,1,0:T(8,128)(2,1)S(1)}, u32[]{:S(2)}, u32[]{:S(2)}) async-start(s16[16,72,512]{2,1,0:T(8,128)(2,1)} %pad_add_fusion.1), calls=%async_computation.1 | async-start | bytes 2359296 | tf_op jit(solution)/shard_map/all_to_all | solution.py:120
  243.6 8.4 %copy-start.18 = (s16[2,16,1]{1,0,2:T(2,128)(2,1)S(1)}, s16[2,16,1]{1,0,2:T(2,128)(2,1)}, u32[]{:S(2)}) copy-start(s16[2,16,1]{1,0,2:T(2,128)(2,1)} %stack.221) | copy-start | bytes 196
  243.6 8.4 %copy-start.19 = (s16[2,16,1]{1,0,2:T(2,128)(2,1)S(1)}, s16[2,16,1]{1,0,2:T(2,128)(2,1)}, u32[]{:S(2)}) copy-start(s16[2,16,1]{1,0,2:T(2,128)(2,1)} %stack.220) | copy-start | bytes 196
  245.4 23.7 %all-to-all-start.2 = ((s16[32,72,256]{2,1,0:T(8,128)(2,1)}), s16[32,72,256]{2,1,0:T(8,128)(2,1)S(1)}, u32[]{:S(2)}, u32[]{:S(2)}) async-start(s16[32,72,256]{2,1,0:T(8,128)(2,1)} %bitcast.72), calls=%async_computation.2 | async-start | bytes 2359296 | tf_op jit(solution)/shard_map/all_to_all | solution.py:124
  253.8 2.3 copy-start.13
  253.8 2.3 copy-start.14
  253.8 2.3 copy-start.15
  253.8 2.3 copy-start.16
  271.1 1.9 copy-start
  273.0 1.9 copy-start.1
  274.9 1.9 copy-start.2
  276.8 1.9 copy-start.5
  278.7 1.9 copy-start.3
  280.6 2.9 copy-start.6
  283.6 1.9 copy-start.4
Sparse Core Ops, SparseCore 0:
  138.0 68.0 all-gather.2

commit v2 on v1

v2 whole, which is shorter than its diff:
```python
import jax
import jax.numpy as jnp
from jax import lax
from jax.experimental import pallas as pl
from jax.experimental.pallas import tpu as pltpu
from jax.sharding import Mesh, PartitionSpec as P

SEQS = 4
ROW = ("xl", "y", "c")
Z = ("zh", "zl")
PLANE = ("xh", "xl", "y", "c")
NZ = 16
NEAR = (0, 1, -1, 2)
TOP = 32000.0
F32 = jnp.float32
BF16 = jnp.bfloat16
S16 = jnp.int16


def shift(x, by):
    return lax.ppermute(x, Z, [(i, (i + by) % NZ) for i in range(NZ)])


def swap_half(x):
    return lax.ppermute(x, "xh", [(0, 1), (1, 0)])


def whole(kernel, outs, args, scratch=(), scalars=1, flops=0):
    specs = [
        pl.BlockSpec(memory_space=pltpu.SMEM if i < scalars else pltpu.VMEM)
        for i in range(len(args))
    ]
    moved = sum(a.size * a.dtype.itemsize for a in args) + sum(
        o.size * o.dtype.itemsize for o in outs
    )
    return pl.pallas_call(
        kernel,
        out_shape=outs,
        in_specs=specs,
        out_specs=[pl.BlockSpec(memory_space=pltpu.VMEM) for _ in outs],
        scratch_shapes=list(scratch),
        compiler_params=pltpu.CompilerParams(vmem_limit_bytes=40 * 2**20),
        cost_estimate=pl.CostEstimate(flops=flops, bytes_accessed=moved, transcendentals=0),
    )(*args)


def coded(x):
    most = jnp.max(jnp.max(jnp.abs(x), axis=1, keepdims=True), axis=0, keepdims=True)
    step = jnp.ceil(jnp.log2(jnp.maximum(most, 1e-30)) * 64.0)
    return jnp.round(x * (TOP * jnp.exp2(step * (-1.0 / 64.0)))), step


def message(x0, x1):
    (c0, s0), (c1, s1) = coded(x0), coded(x1)
    n = x0.shape[1]
    head = jnp.where(lax.broadcasted_iota(jnp.int32, (8, n), 0) < 4, s0, s1)
    return jnp.concatenate([c0, c1, head], axis=0).astype(jnp.int32).astype(S16)


def opened(w, t):
    x = w.astype(F32)
    scale = jnp.exp2(x[2 * t:] * (1.0 / 64.0)) * (1.0 / TOP)
    return x[:t] * scale[0:1], x[t:2 * t] * scale[4:5]


def rotate_grad_kernel(where, got, qb, ob, other, keep, *sends):
    z, xh = where[0], where[1]
    for index, near in enumerate(NEAR):
        residue = lax.rem(z + near + NZ, 4)
        done = []
        for p in range(2):
            basis = (qb, ob)[p]
            rows = [
                jnp.concatenate([got[side, 4 * j + residue, p] for j in range(4)], axis=0)
                for side in (xh, 1 - xh)
            ]
            done.append(
                jnp.dot(rows[0], basis[...], preferred_element_type=F32)
                + jnp.dot(rows[1], other[p], preferred_element_type=F32)
            )
        for j in range(4):
            parts = [d[32 * j:32 * j + 32] for d in done]
            if near == 0:
                keep[j, 0], keep[j, 1] = parts
            else:
                sends[index - 1][j] = message(*parts)


def near_sum_kernel(keep, w1, w2, w3, out):
    for j in range(4):
        total = [keep[j, 0], keep[j, 1]]
        for w in (w1, w2, w3):
            parts = opened(w[j], 32)
            total = [total[0] + parts[0], total[1] + parts[1]]
        out[j] = message(*total)


def far_sum_kernel(w, out):
    total = opened(w[0], 32)
    for j in range(1, 4):
        parts = opened(w[j], 32)
        total = [total[0] + parts[0], total[1] + parts[1]]
    out[0] = message(*total)


def rotate_act_kernel(x0, x1, x2, x3, qa, oa, other, out):
    for index, x in enumerate((x0, x1, x2, x3)):
        done = []
        for p in range(2):
            rows = jnp.concatenate([x[j, p] for j in range(4)], axis=0)
            basis = (qa, oa)[p]
            done.append(
                jnp.concatenate(
                    [
                        jnp.dot(rows, basis[...], preferred_element_type=F32),
                        jnp.dot(rows, other[p], preferred_element_type=F32),
                    ],
                    axis=1,
                )
            )
        for j in range(4):
            out[4 * index + j] = message(*[d[32 * j:32 * j + 32] for d in done])


def act_sum_kernel(where, w, out):
    xh = where[1]
    total = opened(w[0], 32)
    for e in range(1, 16):
        parts = opened(w[e], 32)
        total = [total[0] + parts[0], total[1] + parts[1]]
    out[xh] = message(total[0][:, :256], total[1][:, :256])
    out[1 - xh] = message(total[0][:, 256:], total[1][:, 256:])


def correct_kernel(where, act_w, *rest):
    grads, (q_out, o_out, act, high, low, acc) = rest[:8], rest[8:]
    z, xh = where[0], where[1]
    for p in range(2):
        out = (q_out, o_out)[p]

        def place_act(e, carry, p=p):
            side, r = e // 16, lax.rem(e, 16)
            near = jnp.where(r // 4 == 2, -1, jnp.where(r // 4 == 3, 2, r // 4))
            block = 4 * lax.rem(r, 4) + lax.rem(z - near + NZ, 4)
            at = pl.multiple_of(512 * side + 32 * block, 32)
            act[pl.ds(at, 32), :] = opened(act_w[e], 32)[p]
            return carry

        lax.fori_loop(0, 32, place_act, 0)
        for side in range(2):
            half = xh if side == 0 else 1 - xh
            for index, near in enumerate(NEAR):
                words = grads[4 * side + index]

                def place_grad(j, carry, p=p, near=near, half=half, words=words):
                    block = 4 * j + lax.rem(z - near + NZ, 4)
                    at = pl.multiple_of(64 * block + 32 * half, 32)
                    x = opened(words[j], 32)[p]
                    top = x.astype(BF16)
                    high[pl.ds(at, 32), :] = top
                    low[pl.ds(at, 32), :] = (x - top.astype(F32)).astype(BF16)
                    return carry

                lax.fori_loop(0, 4, place_grad, 0)
        for seq in range(SEQS):
            first, last = where[2 + seq], where[3 + seq]
            acc[...] = jnp.zeros_like(acc)

            def chunk(k, carry, first=first, last=last):
                at = pl.multiple_of(256 * k, 256)
                token = at + lax.broadcasted_iota(jnp.int32, (256, 256), 0)
                a = jnp.where((token >= first) & (token < last), act[pl.ds(at, 256), :], 0.0)
                a_high = a.astype(BF16)
                a_low = (a - a_high.astype(F32)).astype(BF16)
                g_high, g_low = high[pl.ds(at, 256), :], low[pl.ds(at, 256), :]
                dims = (((0,), (0,)), ((), ()))
                acc[...] += (
                    lax.dot_general(g_high, a_high, dims, preferred_element_type=F32)
                    + lax.dot_general(g_high, a_low, dims, preferred_element_type=F32)
                    + lax.dot_general(g_low, a_high, dims, preferred_element_type=F32)
                )
                return carry

            lax.fori_loop(first // 256, (last + 255) // 256, chunk, 0)
            square = acc[...] * acc[...]
            if seq == 0:
                out[...] = square
            elif seq < SEQS - 1:
                out[...] += square
            else:
                out[...] = (out[...] + square) * (1.0 / SEQS)


def shape(*dims, dtype=S16):
    return jax.ShapeDtypeStruct(dims, dtype)


def per_device(seq_ids, qx, qg, qa, qb, ox, og, oa, ob):
    z = lax.axis_index(Z)
    xh = lax.axis_index("xh")
    bounds = jnp.sum(
        (seq_ids[None, :] < jnp.arange(SEQS + 1, dtype=jnp.int32)[:, None]).astype(jnp.int32), axis=1
    )
    where = jnp.concatenate([jnp.stack([z, xh]).astype(jnp.int32), bounds, jnp.zeros(1, jnp.int32)])

    grads = jnp.stack([qg, og])
    sent = jnp.transpose(grads.reshape(2, 2, 32, 256), (1, 0, 2, 3))
    sent = jnp.broadcast_to(sent[:, None], (2, 16, 2, 32, 256)).reshape(32, 2, 32, 256)
    got = lax.all_to_all(sent, PLANE, split_axis=0, concat_axis=0, tiled=True)
    got = got.reshape(2, 16, 2, 32, 256)
    grad_other = swap_half(jnp.stack([qb, ob]))
    level = lax.all_gather(jnp.stack([qx, ox])[None], "zh", axis=0, tiled=True)
    inputs = [level] + [shift(level, near) for near in NEAR[1:]]
    act_other = swap_half(jnp.stack([qa, oa]))

    keep, *sends = whole(
        rotate_grad_kernel,
        [shape(4, 2, 32, 512, dtype=F32)] + [shape(4, 72, 512)] * 3,
        [where, got, qb, ob, grad_other],
        flops=2 * 2 * 512 * 512 * 512,
    )
    sends = [shift(w, near) for w, near in zip(sends, NEAR[1:])]
    [words] = whole(near_sum_kernel, [shape(4, 72, 512)], [keep] + sends, scalars=0)
    words = lax.all_to_all(words, "zh", split_axis=0, concat_axis=0, tiled=True)
    [words] = whole(far_sum_kernel, [shape(1, 72, 512)], [words], scalars=0)
    words = lax.all_gather(words, "zh", axis=0, tiled=True)
    mine = [words] + [shift(words, near) for near in NEAR[1:]]
    others = [swap_half(w) for w in mine]

    [act_words] = whole(
        rotate_act_kernel,
        [shape(16, 72, 512)],
        inputs + [qa, oa, act_other],
        scalars=0,
        flops=2 * 2 * 512 * 512 * 512,
    )
    act_words = lax.all_to_all(act_words, ROW, split_axis=0, concat_axis=0, tiled=True)
    [act_words] = whole(act_sum_kernel, [shape(2, 72, 256)], [where, act_words])
    act_words = jnp.broadcast_to(act_words[:, None], (2, 16, 72, 256)).reshape(32, 72, 256)
    act_words = lax.all_to_all(act_words, PLANE, split_axis=0, concat_axis=0, tiled=True)

    return tuple(
        whole(
            correct_kernel,
            [shape(512, 256, dtype=F32)] * 2,
            [where, act_words] + mine + others,
            scratch=[
                pltpu.VMEM((1024, 256), F32),
                pltpu.VMEM((1024, 512), BF16),
                pltpu.VMEM((1024, 512), BF16),
                pltpu.VMEM((512, 256), F32),
            ],
            flops=2 * 2 * 7 * 3 * 256 * 512 * 256,
        )
    )


def solution(mesh):
    fine = Mesh(mesh.devices.reshape(2, 4, 2, 2, 4, 4), ("xl", "y", "c", "xh", "zh", "zl"))
    row, col = ROW, ("xh",) + Z
    one = (P(col, row), P(row, col), P(row, col), P(col, row))
    out_specs = (P(row, col), P(row, col))
    return jax.shard_map(
        per_device, mesh=fine, in_specs=(P(),) + one + one, out_specs=out_specs, check_vma=False
    )
```

time: 299 us -> 228 us (0.76)
  local copies, waits for them, and re-layouts: 48.1 us -> 2.24 us
  blocking collectives: 0 us -> 44.5 us
  other arithmetic: 27.5 us -> 1.89 us
  matrix products: 19.3 us -> 0 us
  starting transfers between devices: 96 us -> 78.1 us
  Pallas kernels: 0 us -> 15.9 us
  between operations: 15 us -> 0.92 us
  waiting for transfers between devices: 89 us -> 81.3 us
    all_gather x0 -> x2, blocking collectives: none -> 44.5 us  [the longest x1 25.1 us: per_device(): level = lax.all_gather(jnp.stack([qx, ox])[None], 'zh', axis=0, tiled=True)]
    all_gather x1 -> x0, waiting for transfers between devices: 39.8 us -> none  [per_device(): inputs = lax.all_gather(jnp.stack([qx, ox])[None], Z, axis=0, tiled=True)]
    ppermute x12 -> x9, starting transfers between devices: 62.6 us -> 28.7 us  [shift(): return lax.ppermute(x, Z, [(i, (i + by) % NZ) for i in range(NZ)])]
    dot_general x16 -> x0, matrix products: 19.3 us -> none  [the longest x8 16.8 us: correct(): lax.dot_general(grad_rows, act_rot, (((0,), (0,)), ((), ())), precision=l...]
    ppermute x3 -> x6, waiting for transfers between devices: 17.1 us -> 36.1 us  [swap_half(): return lax.ppermute(x, 'xh', [(0, 1), (1, 0)])]
    pallas_call x0 -> x6, Pallas kernels: none -> 15.9 us  [whole(): pl.pallas_call(kernel, out_shape=outs, in_specs=specs, out_specs=[pl.Bloc...]
    all_to_all x1 -> x2, waiting for transfers between devices: 0.01 us -> 15.5 us  [the longest x1 15.5 us: per_device(): words = lax.all_to_all(words, 'zh', split_axis=0, concat_axis=0, tiled=True)]
    select_n x8 -> x0, local copies, waits for them, and re-layouts: 11.3 us -> none  [correct(): grad_rows = jnp.where((seq_ids == seq)[:, None], grad_rot, 0.0)]
  transfers between devices with their start and end apart: 19 -> 19, of which waited for: 11 -> 12; matrix products, arithmetic and copies ran while one was open for 23% -> 0% of each run, Pallas kernels for 0% -> 2%
where the time goes in v2:
time: 228 us; the launch traced here: 225 us
  waiting for transfers between devices  81.3 us (36%)
  starting transfers between devices  78.1 us (34%)
  blocking collectives  44.5 us (20%)
  Pallas kernels  15.9 us (7%)
    ppermute x6, waiting for transfers between devices, swap_half(): return lax.ppermute(x, 'xh', [(0, 1), (1, 0)])  36.1 us
    ppermute x9, waiting for transfers between devices, shift(): return lax.ppermute(x, Z, [(i, (i + by) % NZ) for i in range(NZ)])  29.6 us
    ppermute x9, starting transfers between devices, shift(): return lax.ppermute(x, Z, [(i, (i + by) % NZ) for i in range(NZ)])  28.7 us
    all_gather x1, blocking collectives, per_device(): level = lax.all_gather(jnp.stack([qx, ox])[None], 'zh', axis=0, tiled=True)  25.1 us
    ppermute x6, starting transfers between devices, swap_half(): return lax.ppermute(x, 'xh', [(0, 1), (1, 0)])  20 us
    all_gather x1, blocking collectives, per_device(): words = lax.all_gather(words, 'zh', axis=0, tiled=True)  19.4 us
    pallas_call x6, Pallas kernels, whole(): pl.pallas_call(kernel, out_shape=outs, in_specs=specs, out_specs=[pl.Bloc...  15.9 us
    all_to_all x1, waiting for transfers between devices, per_device(): words = lax.all_to_all(words, 'zh', split_axis=0, concat_axis=0, tiled=True)  15.5 us
  transfers between devices with their start and end apart: 19, of which 12 were waited for; matrix products, arithmetic and copies ran while one was open for 0% of the time, Pallas kernels for 2%

profile of v2, /device:TPU:6, one launch (start us, length us, event | category | flops | bytes accessed | tf_op | source)
XLA Modules:
  0.0 224.8 jit_solution(18398746826430739813)
XLA Ops:
  0.6 0.8 maximum_bitcast_fusion
  1.4 1.1 broadcast_in_dim.8
  2.5 9.7 %all-to-all-start.2 = ((bf16[32,2,32,256]{3,2,1,0:T(8,128)(2,1)}), bf16[32,2,32,256]{3,2,1,0:T(8,128)(2,1)S(1)}, u32[]{:S(2)}, u32[]{:S(2)}) async-start(bf16[32,2,32,256]{3,2,1,0:T(8,128)(2,1)} %bitcast.11), calls=%async_computation.2 | async-start | bytes 2097152 | tf_op jit(solution)/shard_map/all_to_all | solution.py:209
  12.3 0.1 pad_maximum_fusion
  12.3 3.3 %collective-permute-start.3 = (bf16[2,512,256]{2,1,0:T(8,128)(2,1)S(1)}, bf16[2,512,256]{2,1,0:T(8,128)(2,1)S(1)}, u32[]{:S(2)}, u32[]{:S(2)}) collective-permute-start(bf16[2,512,256]{2,1,0:T(8,128)(2,1)S(1)} %pad_maximum_fusion), channel_id=1, source_target_pairs={{0,16},{16,0},{1,17},{17,1},{2,18},{18,2},{3,19},{19,3},{4,20},{20... | collective-permute-start | bytes 1572872 | tf_op jit(solution)/shard_map/ppermute | solution.py:25
  15.6 25.1 %all-gather = bf16[8,32,512]{2,1,0:T(8,128)(2,1)S(1)} all-gather(bf16[2,32,512]{2,1,0:T(8,128)(2,1)S(1)} %pad_maximum_fusion.2), channel_id=2, replica_groups=mesh['xl'=2,'y'=4,'c'=2,'xh'=2,'zh'=4,'zl'=4] {'zh'}, dimensions={0}, use_global_device_ids=true | all-gather | bytes 327680 | tf_op jit(solution)/shard_map/all_gather | solution.py:212
  40.7 2.9 %collective-permute-start = (bf16[4,2,32,512]{3,2,1,0:T(8,128)(2,1)S(1)}, bf16[4,2,32,512]{3,2,1,0:T(8,128)(2,1)S(1)}, u32[]{:S(2)}, u32[]{:S(2)}) collective-permute-start(bf16[4,2,32,512]{3,2,1,0:T(8,128)(2,1)S(1)} %bitcast.17), channel_id=1, source_target_pairs={{0,1},{1,2},{2,3},{3,4},{4,5},{5,6},{6,7},{7,8},{8,9},{9,10},{10,1... | collective-permute-start | bytes 786440 | tf_op jit(solution)/shard_map/ppermute | solution.py:21
  43.6 4.2 %collective-permute-start.1 = (bf16[4,2,32,512]{3,2,1,0:T(8,128)(2,1)S(1)}, bf16[4,2,32,512]{3,2,1,0:T(8,128)(2,1)S(1)}, u32[]{:S(2)}, u32[]{:S(2)}) collective-permute-start(bf16[4,2,32,512]{3,2,1,0:T(8,128)(2,1)S(1)} %bitcast.18), channel_id=1, source_target_pairs={{0,15},{1,0},{2,1},{3,2},{4,3},{5,4},{6,5},{7,6},{8,7},{9,8},{10,9... | collective-permute-start | bytes 786440 | tf_op jit(solution)/shard_map/ppermute | solution.py:21
  47.8 2.1 collective-permute-start.2
  49.9 0.9 collective-permute-done.x1
  50.7 1.1 collective-permute-done.1.x2
  51.8 10.0 %collective-permute-done.2.x3 = bf16[4,2,32,512]{3,2,1,0:T(8,128)(2,1)S(1)} collective-permute-done((bf16[4,2,32,512]{3,2,1,0:T(8,128)(2,1)S(1)}, bf16[4,2,32,512]{3,2,1,0:T(8,128)(2,1)S(1)}, u32[]{:S(2)}, u32[]{:S(2)}) %collective-permute-start.2) | collective-permute-done | bytes 262176 | tf_op jit(solution)/shard_map/ppermute | solution.py:21
  61.8 0.0 collective-permute-done.3.other
  61.8 1.9 shard_map.104
  63.8 0.0 all-to-all-done.2
  63.8 5.8 %all-to-all-start = ((s16[16,72,512]{2,1,0:T(8,128)(2,1)}), s16[16,72,512]{2,1,0:T(8,128)(2,1)S(1)}, u32[]{:S(2)}, u32[]{:S(2)}) async-start(s16[16,72,512]{2,1,0:T(8,128)(2,1)} %shard_map.104), calls=%async_computation | async-start | bytes 2359296 | tf_op jit(solution)/shard_map/all_to_all | solution.py:237
  69.6 0.8 pad_maximum_fusion.1
  70.4 4.0 %collective-permute-start.4 = (bf16[2,256,512]{2,1,0:T(8,128)(2,1)}, bf16[2,256,512]{2,1,0:T(8,128)(2,1)S(1)}, u32[]{:S(2)}, u32[]{:S(2)}) collective-permute-start(bf16[2,256,512]{2,1,0:T(8,128)(2,1)} %pad_maximum_fusion.1), channel_id=1, source_target_pairs={{0,16},{16,0},{1,17},{17,1},{2,18},{18,2},{3,19},{19,3},{4,20},{20... | collective-permute-start | bytes 1572872 | tf_op jit(solution)/shard_map/ppermute | solution.py:25
  74.5 0.1 convert_reduce_fusion
  74.6 0.1 pad_add_fusion.where
  74.7 22.2 %collective-permute-done.4.other = bf16[2,256,512]{2,1,0:T(8,128)(2,1)S(1)} collective-permute-done((bf16[2,256,512]{2,1,0:T(8,128)(2,1)}, bf16[2,256,512]{2,1,0:T(8,128)(2,1)S(1)}, u32[]{:S(2)}, u32[]{:S(2)}) %collective-permute-start.4) | collective-permute-done | bytes 524320 | tf_op jit(solution)/shard_map/ppermute | solution.py:25
  96.8 1.4 shard_map.106
  98.3 2.3 %collective-permute-start.5 = (s16[4,72,512]{2,1,0:T(8,128)(2,1)S(1)}, s16[4,72,512]{2,1,0:T(8,128)(2,1)S(1)}, u32[]{:S(2)}, u32[]{:S(2)}) collective-permute-start(s16[4,72,512]{2,1,0:T(8,128)(2,1)S(1)} %get-tuple-element.7), channel_id=1, source_target_pairs={{0,1},{1,2},{2,3},{3,4},{4,5},{5,6},{6,7},{7,8},{8,9},{9,10},{10,1... | collective-permute-start | bytes 884744 | tf_op jit(solution)/shard_map/ppermute | solution.py:21
  100.6 4.7 %collective-permute-start.6 = (s16[4,72,512]{2,1,0:T(8,128)(2,1)S(1)}, s16[4,72,512]{2,1,0:T(8,128)(2,1)S(1)}, u32[]{:S(2)}, u32[]{:S(2)}) collective-permute-start(s16[4,72,512]{2,1,0:T(8,128)(2,1)S(1)} %get-tuple-element.8), channel_id=1, source_target_pairs={{0,15},{1,0},{2,1},{3,2},{4,3},{5,4},{6,5},{7,6},{8,7},{9,8},{10,9... | collective-permute-start | bytes 884744 | tf_op jit(solution)/shard_map/ppermute | solution.py:21
  105.3 1.9 collective-permute-start.7
  107.3 3.7 %collective-permute-done.5.w1 = s16[4,72,512]{2,1,0:T(8,128)(2,1)S(1)} collective-permute-done((s16[4,72,512]{2,1,0:T(8,128)(2,1)S(1)}, s16[4,72,512]{2,1,0:T(8,128)(2,1)S(1)}, u32[]{:S(2)}, u32[]{:S(2)}) %collective-permute-start.5) | collective-permute-done | bytes 294944 | tf_op jit(solution)/shard_map/ppermute | solution.py:21
  111.0 0.1 collective-permute-done.6.w2
  111.1 11.5 %collective-permute-done.7.w3 = s16[4,72,512]{2,1,0:T(8,128)(2,1)S(1)} collective-permute-done((s16[4,72,512]{2,1,0:T(8,128)(2,1)S(1)}, s16[4,72,512]{2,1,0:T(8,128)(2,1)S(1)}, u32[]{:S(2)}, u32[]{:S(2)}) %collective-permute-start.7) | collective-permute-done | bytes 294944 | tf_op jit(solution)/shard_map/ppermute | solution.py:21
  122.6 1.1 shard_map.107
  123.7 6.7 %all-to-all-start.3 = ((s16[4,72,512]{2,1,0:T(8,128)(2,1)}), s16[4,72,512]{2,1,0:T(8,128)(2,1)S(1)}, u32[]{:S(2)}, u32[]{:S(2)}) async-start(s16[4,72,512]{2,1,0:T(8,128)(2,1)} %shard_map.107), calls=%async_computation.3 | async-start | bytes 589824 | tf_op jit(solution)/shard_map/all_to_all | solution.py:224
  130.4 1.0 shard_map.105
  131.4 15.5 %all-to-all-done.3.w = s16[4,72,512]{2,1,0:T(8,128)(2,1)S(1)} async-done(((s16[4,72,512]{2,1,0:T(8,128)(2,1)}), s16[4,72,512]{2,1,0:T(8,128)(2,1)S(1)}, u32[]{:S(2)}, u32[]{:S(2)}) %all-to-all-start.3) | async-done | bytes 294944 | tf_op jit(solution)/shard_map/all_to_all | solution.py:224
  146.9 1.1 broadcast_in_dim.7
  148.0 7.2 %all-to-all-start.1 = ((s16[32,72,256]{2,1,0:T(8,128)(2,1)}), s16[32,72,256]{2,1,0:T(8,128)(2,1)S(1)}, u32[]{:S(2)}, u32[]{:S(2)}) async-start(s16[32,72,256]{2,1,0:T(8,128)(2,1)} %bitcast.7), calls=%async_computation.1 | async-start | bytes 2359296 | tf_op jit(solution)/shard_map/all_to_all | solution.py:240
  155.3 0.2 shard_map.108
  155.4 19.4 %all_gather.7.rest_0_ = s16[4,72,512]{2,1,0:T(8,128)(2,1)S(1)} all-gather(s16[1,72,512]{2,1,0:T(8,128)(2,1)S(1)} %shard_map.108), channel_id=1, replica_groups=mesh['xl'=2,'y'=4,'c'=2,'xh'=2,'zh'=4,'zl'=4] {'zh'}, dimensions={0}, use_global_device_ids=true | all-gather | bytes 368640 | tf_op jit(solution)/shard_map/all_gather | solution.py:226
  174.9 4.9 %collective-permute-start.8 = (s16[4,72,512]{2,1,0:T(8,128)(2,1)S(1)}, s16[4,72,512]{2,1,0:T(8,128)(2,1)S(1)}, u32[]{:S(2)}, u32[]{:S(2)}) collective-permute-start(s16[4,72,512]{2,1,0:T(8,128)(2,1)S(1)} %all_gather.7.rest_0_), channel_id=1, source_target_pairs={{0,1},{1,2},{2,3},{3,4},{4,5},{5,6},{6,7},{7,8},{8,9},{9,10},{10,1... | collective-permute-start | bytes 884744 | tf_op jit(solution)/shard_map/ppermute | solution.py:21
  179.8 2.1 collective-permute-start.9
  181.9 3.5 %collective-permute-start.10 = (s16[4,72,512]{2,1,0:T(8,128)(2,1)S(1)}, s16[4,72,512]{2,1,0:T(8,128)(2,1)S(1)}, u32[]{:S(2)}, u32[]{:S(2)}) collective-permute-start(s16[4,72,512]{2,1,0:T(8,128)(2,1)S(1)} %all_gather.7.rest_0_), channel_id=1, source_target_pairs={{0,2},{1,3},{2,4},{3,5},{4,6},{5,7},{6,8},{7,9},{8,10},{9,11},{10,... | collective-permute-start | bytes 884744 | tf_op jit(solution)/shard_map/ppermute | solution.py:21
  185.5 3.4 %collective-permute-start.11 = (s16[4,72,512]{2,1,0:T(8,128)(2,1)S(1)}, s16[4,72,512]{2,1,0:T(8,128)(2,1)S(1)}, u32[]{:S(2)}, u32[]{:S(2)}) collective-permute-start(s16[4,72,512]{2,1,0:T(8,128)(2,1)S(1)} %all_gather.7.rest_0_), channel_id=1, source_target_pairs={{0,16},{16,0},{1,17},{17,1},{2,18},{18,2},{3,19},{19,3},{4,20},{20... | collective-permute-start | bytes 884744 | tf_op jit(solution)/shard_map/ppermute | solution.py:25
  188.9 3.9 %collective-permute-start.12 = (s16[4,72,512]{2,1,0:T(8,128)(2,1)S(1)}, s16[4,72,512]{2,1,0:T(8,128)(2,1)S(1)}, u32[]{:S(2)}, u32[]{:S(2)}) collective-permute-start(s16[4,72,512]{2,1,0:T(8,128)(2,1)S(1)} %collective-permute-done.8.rest_1_), channel_id=1, source_target_pairs={{0,16},{16,0},{1,17},{17,1},{2,18},{18,2},{3,19},{19,3},{4,20},{20... | collective-permute-start | bytes 884744 | tf_op jit(solution)/shard_map/ppermute | solution.py:25
  192.8 3.4 %collective-permute-start.13 = (s16[4,72,512]{2,1,0:T(8,128)(2,1)S(1)}, s16[4,72,512]{2,1,0:T(8,128)(2,1)S(1)}, u32[]{:S(2)}, u32[]{:S(2)}) collective-permute-start(s16[4,72,512]{2,1,0:T(8,128)(2,1)S(1)} %collective-permute-done.9.rest_2_), channel_id=1, source_target_pairs={{0,16},{16,0},{1,17},{17,1},{2,18},{18,2},{3,19},{19,3},{4,20},{20... | collective-permute-start | bytes 884744 | tf_op jit(solution)/shard_map/ppermute | solution.py:25
  196.3 2.4 %collective-permute-done.10.rest_3_ = s16[4,72,512]{2,1,0:T(8,128)(2,1)S(1)} collective-permute-done((s16[4,72,512]{2,1,0:T(8,128)(2,1)S(1)}, s16[4,72,512]{2,1,0:T(8,128)(2,1)S(1)}, u32[]{:S(2)}, u32[]{:S(2)}) %collective-permute-start.10) | collective-permute-done | bytes 294944 | tf_op jit(solution)/shard_map/ppermute | solution.py:21
  198.6 1.9 collective-permute-start.14
  200.6 4.5 %collective-permute-done.12.rest_5_ = s16[4,72,512]{2,1,0:T(8,128)(2,1)S(1)} collective-permute-done((s16[4,72,512]{2,1,0:T(8,128)(2,1)S(1)}, s16[4,72,512]{2,1,0:T(8,128)(2,1)S(1)}, u32[]{:S(2)}, u32[]{:S(2)}) %collective-permute-start.12) | collective-permute-done | bytes 294944 | tf_op jit(solution)/shard_map/ppermute | solution.py:25
  205.1 6.2 %collective-permute-done.13.rest_6_ = s16[4,72,512]{2,1,0:T(8,128)(2,1)S(1)} collective-permute-done((s16[4,72,512]{2,1,0:T(8,128)(2,1)S(1)}, s16[4,72,512]{2,1,0:T(8,128)(2,1)S(1)}, u32[]{:S(2)}, u32[]{:S(2)}) %collective-permute-start.13) | collective-permute-done | bytes 294944 | tf_op jit(solution)/shard_map/ppermute | solution.py:25
  211.2 3.3 %collective-permute-done.14.rest_7_ = s16[4,72,512]{2,1,0:T(8,128)(2,1)} collective-permute-done((s16[4,72,512]{2,1,0:T(8,128)(2,1)S(1)}, s16[4,72,512]{2,1,0:T(8,128)(2,1)}, u32[]{:S(2)}, u32[]{:S(2)}) %collective-permute-start.14) | collective-permute-done | bytes 294944 | tf_op jit(solution)/shard_map/ppermute | solution.py:25
  214.5 10.3 %shard_map.109 = (f32[512,256]{1,0:T(8,128)}, f32[512,256]{1,0:T(8,128)}) custom-call(s32[8]{0:T(128)S(1)} %pad_add_fusion.where, s16[32,72,256]{2,1,0:T(8,128)(2,1)S(1)} %all-to-all-done.1.act_w, s16[4,72,512]{2,1,0:T(8,128)(2,1)S(1)} %all_gather.7.rest_0_, s16[4,72,512]{2,1,0:T(8,128)(2,1)S(1)} %collective-permute-done.8.rest_1_, ...), custom_call_target="tpu_custom_call" | custom-call | flops 2818572288 | bytes 4587552 | tf_op jit(solution)/shard_map/pallas_call | solution.py:36
  (21 shorter events, 0.1 us)
Async XLA Ops:
  2.5 9.8 %copy-start = (bf16[512,256]{1,0:T(8,128)(2,1)S(1)}, bf16[512,256]{1,0:T(8,128)(2,1)}, u32[]{:S(2)}) copy-start(bf16[512,256]{1,0:T(8,128)(2,1)} %qa.1) | copy-start | bytes 786436
  2.5 9.8 %copy-start.1 = (bf16[512,256]{1,0:T(8,128)(2,1)S(1)}, bf16[512,256]{1,0:T(8,128)(2,1)}, u32[]{:S(2)}) copy-start(bf16[512,256]{1,0:T(8,128)(2,1)} %oa.1) | copy-start | bytes 786436
  2.5 13.1 %copy-start.4 = (bf16[32,512]{1,0:T(8,128)(2,1)S(1)}, bf16[32,512]{1,0:T(8,128)(2,1)}, u32[]{:S(2)}) copy-start(bf16[32,512]{1,0:T(8,128)(2,1)} %param.14) | copy-start | bytes 98308
  2.5 13.1 %copy-start.5 = (bf16[32,512]{1,0:T(8,128)(2,1)S(1)}, bf16[32,512]{1,0:T(8,128)(2,1)}, u32[]{:S(2)}) copy-start(bf16[32,512]{1,0:T(8,128)(2,1)} %param.10) | copy-start | bytes 98308
  2.5 61.3 %all-to-all-start.2 = ((bf16[32,2,32,256]{3,2,1,0:T(8,128)(2,1)}), bf16[32,2,32,256]{3,2,1,0:T(8,128)(2,1)S(1)}, u32[]{:S(2)}, u32[]{:S(2)}) async-start(bf16[32,2,32,256]{3,2,1,0:T(8,128)(2,1)} %bitcast.11), calls=%async_computation.2 | async-start | bytes 2097152 | tf_op jit(solution)/shard_map/all_to_all | solution.py:209
  12.3 49.5 %collective-permute-start.3 = (bf16[2,512,256]{2,1,0:T(8,128)(2,1)S(1)}, bf16[2,512,256]{2,1,0:T(8,128)(2,1)S(1)}, u32[]{:S(2)}, u32[]{:S(2)}) collective-permute-start(bf16[2,512,256]{2,1,0:T(8,128)(2,1)S(1)} %pad_maximum_fusion), channel_id=1, source_target_pairs={{0,16},{16,0},{1,17},{17,1},{2,18},{18,2},{3,19},{19,3},{4,20},{20... | collective-permute-start | bytes 1572872 | tf_op jit(solution)/shard_map/ppermute | solution.py:25
  40.7 10.0 %collective-permute-start = (bf16[4,2,32,512]{3,2,1,0:T(8,128)(2,1)S(1)}, bf16[4,2,32,512]{3,2,1,0:T(8,128)(2,1)S(1)}, u32[]{:S(2)}, u32[]{:S(2)}) collective-permute-start(bf16[4,2,32,512]{3,2,1,0:T(8,128)(2,1)S(1)} %bitcast.17), channel_id=1, source_target_pairs={{0,1},{1,2},{2,3},{3,4},{4,5},{5,6},{6,7},{7,8},{8,9},{9,10},{10,1... | collective-permute-start | bytes 786440 | tf_op jit(solution)/shard_map/ppermute | solution.py:21
  43.6 8.3 %collective-permute-start.1 = (bf16[4,2,32,512]{3,2,1,0:T(8,128)(2,1)S(1)}, bf16[4,2,32,512]{3,2,1,0:T(8,128)(2,1)S(1)}, u32[]{:S(2)}, u32[]{:S(2)}) collective-permute-start(bf16[4,2,32,512]{3,2,1,0:T(8,128)(2,1)S(1)} %bitcast.18), channel_id=1, source_target_pairs={{0,15},{1,0},{2,1},{3,2},{4,3},{5,4},{6,5},{7,6},{8,7},{9,8},{10,9... | collective-permute-start | bytes 786440 | tf_op jit(solution)/shard_map/ppermute | solution.py:21
  47.8 14.1 %collective-permute-start.2 = (bf16[4,2,32,512]{3,2,1,0:T(8,128)(2,1)S(1)}, bf16[4,2,32,512]{3,2,1,0:T(8,128)(2,1)S(1)}, u32[]{:S(2)}, u32[]{:S(2)}) collective-permute-start(bf16[4,2,32,512]{3,2,1,0:T(8,128)(2,1)S(1)} %bitcast.19), channel_id=1, source_target_pairs={{0,2},{1,3},{2,4},{3,5},{4,6},{5,7},{6,8},{7,9},{8,10},{9,11},{10,... | collective-permute-start | bytes 786440 | tf_op jit(solution)/shard_map/ppermute | solution.py:21
  63.8 5.8 %copy-start.2 = (bf16[256,512]{1,0:T(8,128)(2,1)S(1)}, bf16[256,512]{1,0:T(8,128)(2,1)}, u32[]{:S(2)}) copy-start(bf16[256,512]{1,0:T(8,128)(2,1)} %qb.1) | copy-start | bytes 786436
  63.8 5.8 %copy-start.3 = (bf16[256,512]{1,0:T(8,128)(2,1)S(1)}, bf16[256,512]{1,0:T(8,128)(2,1)}, u32[]{:S(2)}) copy-start(bf16[256,512]{1,0:T(8,128)(2,1)} %ob.1) | copy-start | bytes 786436
  63.8 10.7 %copy-start.6 = (s32[1024]{0:T(1024)S(1)}, s32[1024]{0:T(1024)}, u32[]{:S(2)}) copy-start(s32[1024]{0:T(1024)} %param.9) | copy-start | bytes 12292
  63.8 59.9 %all-to-all-start = ((s16[16,72,512]{2,1,0:T(8,128)(2,1)}), s16[16,72,512]{2,1,0:T(8,128)(2,1)S(1)}, u32[]{:S(2)}, u32[]{:S(2)}) async-start(s16[16,72,512]{2,1,0:T(8,128)(2,1)} %shard_map.104), calls=%async_computation | async-start | bytes 2359296 | tf_op jit(solution)/shard_map/all_to_all | solution.py:237
  70.4 26.4 %collective-permute-start.4 = (bf16[2,256,512]{2,1,0:T(8,128)(2,1)}, bf16[2,256,512]{2,1,0:T(8,128)(2,1)S(1)}, u32[]{:S(2)}, u32[]{:S(2)}) collective-permute-start(bf16[2,256,512]{2,1,0:T(8,128)(2,1)} %pad_maximum_fusion.1), channel_id=1, source_target_pairs={{0,16},{16,0},{1,17},{17,1},{2,18},{18,2},{3,19},{19,3},{4,20},{20... | collective-permute-start | bytes 1572872 | tf_op jit(solution)/shard_map/ppermute | solution.py:25
  98.3 12.7 %collective-permute-start.5 = (s16[4,72,512]{2,1,0:T(8,128)(2,1)S(1)}, s16[4,72,512]{2,1,0:T(8,128)(2,1)S(1)}, u32[]{:S(2)}, u32[]{:S(2)}) collective-permute-start(s16[4,72,512]{2,1,0:T(8,128)(2,1)S(1)} %get-tuple-element.7), channel_id=1, source_target_pairs={{0,1},{1,2},{2,3},{3,4},{4,5},{5,6},{6,7},{7,8},{8,9},{9,10},{10,1... | collective-permute-start | bytes 884744 | tf_op jit(solution)/shard_map/ppermute | solution.py:21
  100.6 10.5 %collective-permute-start.6 = (s16[4,72,512]{2,1,0:T(8,128)(2,1)S(1)}, s16[4,72,512]{2,1,0:T(8,128)(2,1)S(1)}, u32[]{:S(2)}, u32[]{:S(2)}) collective-permute-start(s16[4,72,512]{2,1,0:T(8,128)(2,1)S(1)} %get-tuple-element.8), channel_id=1, source_target_pairs={{0,15},{1,0},{2,1},{3,2},{4,3},{5,4},{6,5},{7,6},{8,7},{9,8},{10,9... | collective-permute-start | bytes 884744 | tf_op jit(solution)/shard_map/ppermute | solution.py:21
  105.3 17.2 %collective-permute-start.7 = (s16[4,72,512]{2,1,0:T(8,128)(2,1)S(1)}, s16[4,72,512]{2,1,0:T(8,128)(2,1)S(1)}, u32[]{:S(2)}, u32[]{:S(2)}) collective-permute-start(s16[4,72,512]{2,1,0:T(8,128)(2,1)S(1)} %get-tuple-element.9), channel_id=1, source_target_pairs={{0,2},{1,3},{2,4},{3,5},{4,6},{5,7},{6,8},{7,9},{8,10},{9,11},{10,... | collective-permute-start | bytes 884744 | tf_op jit(solution)/shard_map/ppermute | solution.py:21
  123.7 23.3 %all-to-all-start.3 = ((s16[4,72,512]{2,1,0:T(8,128)(2,1)}), s16[4,72,512]{2,1,0:T(8,128)(2,1)S(1)}, u32[]{:S(2)}, u32[]{:S(2)}) async-start(s16[4,72,512]{2,1,0:T(8,128)(2,1)} %shard_map.107), calls=%async_computation.3 | async-start | bytes 589824 | tf_op jit(solution)/shard_map/all_to_all | solution.py:224
  148.0 52.5 %all-to-all-start.1 = ((s16[32,72,256]{2,1,0:T(8,128)(2,1)}), s16[32,72,256]{2,1,0:T(8,128)(2,1)S(1)}, u32[]{:S(2)}, u32[]{:S(2)}) async-start(s16[32,72,256]{2,1,0:T(8,128)(2,1)} %bitcast.7), calls=%async_computation.1 | async-start | bytes 2359296 | tf_op jit(solution)/shard_map/all_to_all | solution.py:240
  174.9 14.0 %collective-permute-start.8 = (s16[4,72,512]{2,1,0:T(8,128)(2,1)S(1)}, s16[4,72,512]{2,1,0:T(8,128)(2,1)S(1)}, u32[]{:S(2)}, u32[]{:S(2)}) collective-permute-start(s16[4,72,512]{2,1,0:T(8,128)(2,1)S(1)} %all_gather.7.rest_0_), channel_id=1, source_target_pairs={{0,1},{1,2},{2,3},{3,4},{4,5},{5,6},{6,7},{7,8},{8,9},{9,10},{10,1... | collective-permute-start | bytes 884744 | tf_op jit(solution)/shard_map/ppermute | solution.py:21
  179.8 13.0 %collective-permute-start.9 = (s16[4,72,512]{2,1,0:T(8,128)(2,1)S(1)}, s16[4,72,512]{2,1,0:T(8,128)(2,1)S(1)}, u32[]{:S(2)}, u32[]{:S(2)}) collective-permute-start(s16[4,72,512]{2,1,0:T(8,128)(2,1)S(1)} %all_gather.7.rest_0_), channel_id=1, source_target_pairs={{0,15},{1,0},{2,1},{3,2},{4,3},{5,4},{6,5},{7,6},{8,7},{9,8},{10,9... | collective-permute-start | bytes 884744 | tf_op jit(solution)/shard_map/ppermute | solution.py:21
  181.9 16.7 %collective-permute-start.10 = (s16[4,72,512]{2,1,0:T(8,128)(2,1)S(1)}, s16[4,72,512]{2,1,0:T(8,128)(2,1)S(1)}, u32[]{:S(2)}, u32[]{:S(2)}) collective-permute-start(s16[4,72,512]{2,1,0:T(8,128)(2,1)S(1)} %all_gather.7.rest_0_), channel_id=1, source_target_pairs={{0,2},{1,3},{2,4},{3,5},{4,6},{5,7},{6,8},{7,9},{8,10},{9,11},{10,... | collective-permute-start | bytes 884744 | tf_op jit(solution)/shard_map/ppermute | solution.py:21
  185.5 15.1 %collective-permute-start.11 = (s16[4,72,512]{2,1,0:T(8,128)(2,1)S(1)}, s16[4,72,512]{2,1,0:T(8,128)(2,1)S(1)}, u32[]{:S(2)}, u32[]{:S(2)}) collective-permute-start(s16[4,72,512]{2,1,0:T(8,128)(2,1)S(1)} %all_gather.7.rest_0_), channel_id=1, source_target_pairs={{0,16},{16,0},{1,17},{17,1},{2,18},{18,2},{3,19},{19,3},{4,20},{20... | collective-permute-start | bytes 884744 | tf_op jit(solution)/shard_map/ppermute | solution.py:25
  188.9 16.2 %collective-permute-start.12 = (s16[4,72,512]{2,1,0:T(8,128)(2,1)S(1)}, s16[4,72,512]{2,1,0:T(8,128)(2,1)S(1)}, u32[]{:S(2)}, u32[]{:S(2)}) collective-permute-start(s16[4,72,512]{2,1,0:T(8,128)(2,1)S(1)} %collective-permute-done.8.rest_1_), channel_id=1, source_target_pairs={{0,16},{16,0},{1,17},{17,1},{2,18},{18,2},{3,19},{19,3},{4,20},{20... | collective-permute-start | bytes 884744 | tf_op jit(solution)/shard_map/ppermute | solution.py:25
  192.8 18.4 %collective-permute-start.13 = (s16[4,72,512]{2,1,0:T(8,128)(2,1)S(1)}, s16[4,72,512]{2,1,0:T(8,128)(2,1)S(1)}, u32[]{:S(2)}, u32[]{:S(2)}) collective-permute-start(s16[4,72,512]{2,1,0:T(8,128)(2,1)S(1)} %collective-permute-done.9.rest_2_), channel_id=1, source_target_pairs={{0,16},{16,0},{1,17},{17,1},{2,18},{18,2},{3,19},{19,3},{4,20},{20... | collective-permute-start | bytes 884744 | tf_op jit(solution)/shard_map/ppermute | solution.py:25
  198.6 15.9 %collective-permute-start.14 = (s16[4,72,512]{2,1,0:T(8,128)(2,1)S(1)}, s16[4,72,512]{2,1,0:T(8,128)(2,1)}, u32[]{:S(2)}, u32[]{:S(2)}) collective-permute-start(s16[4,72,512]{2,1,0:T(8,128)(2,1)S(1)} %collective-permute-done.10.rest_3_), channel_id=1, source_target_pairs={{0,16},{16,0},{1,17},{17,1},{2,18},{18,2},{3,19},{19,3},{4,20},{20... | collective-permute-start | bytes 884744 | tf_op jit(solution)/shard_map/ppermute | solution.py:25

commit v3 on v2

v3 whole, which is shorter than its diff:
```python
import jax
import jax.numpy as jnp
from jax import lax
from jax.experimental import pallas as pl
from jax.experimental.pallas import tpu as pltpu
from jax.sharding import Mesh, PartitionSpec as P

SEQS = 4
ROW = ("xl", "y", "c")
Z = ("zh", "zm", "zl")
Z8 = ("zh", "zm")
ZH = "zh"
PLANE = ("xh", "xl", "y", "c")
NZ = 16
TOP = 32000.0
F32 = jnp.float32
BF16 = jnp.bfloat16
S16 = jnp.int16


def shift(x, by):
    return lax.ppermute(x, Z, [(i, (i + by) % NZ) for i in range(NZ)])


def swap_half(x):
    return lax.ppermute(x, "xh", [(0, 1), (1, 0)])


def whole(kernel, outs, args, scratch=(), scalars=1, flops=0):
    specs = [
        pl.BlockSpec(memory_space=pltpu.SMEM if i < scalars else pltpu.VMEM)
        for i in range(len(args))
    ]
    moved = sum(a.size * a.dtype.itemsize for a in args) + sum(
        o.size * o.dtype.itemsize for o in outs
    )
    return pl.pallas_call(
        kernel,
        out_shape=outs,
        in_specs=specs,
        out_specs=[pl.BlockSpec(memory_space=pltpu.VMEM) for _ in outs],
        scratch_shapes=list(scratch),
        compiler_params=pltpu.CompilerParams(vmem_limit_bytes=40 * 2**20),
        cost_estimate=pl.CostEstimate(flops=flops, bytes_accessed=moved, transcendentals=0),
    )(*args)


def coded(x):
    most = jnp.max(jnp.max(jnp.abs(x), axis=1, keepdims=True), axis=0, keepdims=True)
    step = jnp.ceil(jnp.log2(jnp.maximum(most, 1e-30)) * 64.0)
    return jnp.round(x * (TOP * jnp.exp2(step * (-1.0 / 64.0)))), step


def message(*blocks):
    pieces = [coded(x) for x in blocks]
    head = pieces[0][1]
    if len(blocks) == 2:
        row = lax.broadcasted_iota(jnp.int32, (8, blocks[0].shape[1]), 0)
        head = jnp.where(row < 4, head, pieces[1][1])
    head = jnp.broadcast_to(head, (8, blocks[0].shape[1]))
    return jnp.concatenate([c for c, _ in pieces] + [head], axis=0).astype(jnp.int32).astype(S16)


def opened(w, t):
    x = w.astype(F32)
    blocks = x.shape[0] // t
    scale = jnp.exp2(x[blocks * t:] * (1.0 / 64.0)) * (1.0 / TOP)
    return [x[t * i:t * i + t] * scale[4 * i:4 * i + 1] for i in range(blocks)]


def added(*pairs):
    return [sum(terms[1:], terms[0]) for terms in zip(*pairs)]


def rotate_grad_kernel(where, got, qb, ob, other, keep, near1, near3, two_up, two_down):
    z, xh = where[0], where[1]
    for ahead in (1, 3, 2, 0):
        residue = lax.rem(z + ahead, 4)
        done = []
        for p in range(2):
            basis = (qb, ob)[p]
            rows = [
                jnp.concatenate([got[side, 4 * j + residue, p] for j in range(4)], axis=0)
                for side in (xh, 1 - xh)
            ]
            done.append(
                jnp.dot(rows[0], basis[...], preferred_element_type=F32)
                + jnp.dot(rows[1], other[p], preferred_element_type=F32)
            )
        for j in range(4):
            parts = [d[32 * j:32 * j + 32] for d in done]
            if ahead == 0:
                keep[j, 0], keep[j, 1] = parts
            elif ahead == 2:
                (two_up, two_down)[j // 2][j % 2] = message(*parts)
            else:
                (near1 if ahead == 1 else near3)[j] = message(*parts)


def near_sum_kernel(keep, w1, w3, up, down, out):
    for j in range(4):
        two = up if j < 2 else down
        out[j] = message(
            *added(
                [keep[j, 0], keep[j, 1]],
                opened(w1[j], 32),
                opened(w3[j], 32),
                opened(two[j % 2], 32),
            )
        )


def far_sum_kernel(w, out):
    out[0] = message(*added(*[opened(w[j], 32) for j in range(4)]))


def rotate_act_kernel(where, level, x1, x3, up, down, qa, oa, other, out):
    for behind, x in ((0, level), (1, x1), (3, x3), (2, None)):
        done = []
        for p in range(2):
            basis = (qa, oa)[p]
            if x is None:
                rows = [up[0, p], up[1, p], down[0, p], down[1, p]]
            else:
                rows = [x[j, p] for j in range(4)]
            rows = jnp.concatenate(rows, axis=0)
            done.append(
                jnp.concatenate(
                    [
                        jnp.dot(rows, basis[...], preferred_element_type=F32),
                        jnp.dot(rows, other[p], preferred_element_type=F32),
                    ],
                    axis=1,
                )
            )
        residue = lax.rem(where[0] + 4 - behind, 4)
        for j in range(4):
            out[4 * j + residue] = message(*[d[32 * j:32 * j + 32] for d in done])


def act_sum_kernel(where, w, out):
    xh = where[1]
    total = opened(w[0], 32)
    for e in range(1, 16):
        total = added(total, opened(w[e], 32))
    mine = message(total[0][:, :256], total[1][:, :256])
    other = message(total[0][:, 256:], total[1][:, 256:])
    for r in range(16):
        out[xh, r] = mine
        out[1 - xh, r] = other


def open_act_kernel(w, out):
    for e in range(0, 32, 4):
        blocks = [opened(w[e + i], 32) for i in range(4)]
        for p in range(2):
            out[p, :, 32 * e:32 * e + 128] = jnp.concatenate([b[p] for b in blocks], axis=0).T


def correct_kernel(where, act, *rest):
    grads, (q_out, o_out, high, low, acc, total) = rest[:6], rest[6:]
    zl, xh = lax.rem(where[0], 2), where[1]
    for p in range(2):
        for side in range(2):
            half = xh if side == 0 else 1 - xh
            level, first_w, last_w = grads[3 * side:3 * side + 3]
            for k in range(16):
                w = level[k] if k < 8 else (first_w[k - 8] if k < 12 else last_w[k - 12])
                block = 2 * (k % 8) + (zl if k < 8 else 1 - zl)
                at = pl.multiple_of(64 * block + 32 * half, 32)
                x = opened(w, 32)[p]
                top = x.astype(BF16)
                high[pl.ds(at, 32), :] = top
                low[pl.ds(at, 32), :] = (x - top.astype(F32)).astype(BF16)
        for seq in range(SEQS):
            first, last = where[2 + seq], where[3 + seq]
            acc[...] = jnp.zeros_like(acc)

            def chunk(k, carry, first=first, last=last, p=p):
                at = pl.multiple_of(256 * k, 256)
                token = at + lax.broadcasted_iota(jnp.int32, (256, 256), 1)
                a = jnp.where((token >= first) & (token < last), act[p, :, pl.ds(at, 256)], 0.0)
                a_high = a.astype(BF16)
                a_low = (a - a_high.astype(F32)).astype(BF16)
                g_high, g_low = high[pl.ds(at, 256), :], low[pl.ds(at, 256), :]
                acc[...] += (
                    jnp.dot(a_high, g_high, preferred_element_type=F32)
                    + jnp.dot(a_low, g_high, preferred_element_type=F32)
                    + jnp.dot(a_high, g_low, preferred_element_type=F32)
                )
                return carry

            lax.fori_loop(first // 256, (last + 255) // 256, chunk, 0)
            square = acc[...] * acc[...]
            total[...] = square if seq == 0 else total[...] + square
        out = (q_out, o_out)[p]
        out[...] = total[...].T * (1.0 / SEQS)


def shape(*dims, dtype=S16):
    return jax.ShapeDtypeStruct(dims, dtype)


def per_device(seq_ids, qx, qg, qa, qb, ox, og, oa, ob):
    z = lax.axis_index(Z)
    xh = lax.axis_index("xh")
    bounds = jnp.sum(
        (seq_ids[None, :] < jnp.arange(SEQS + 1, dtype=jnp.int32)[:, None]).astype(jnp.int32), axis=1
    )
    where = jnp.concatenate([jnp.stack([z, xh]).astype(jnp.int32), bounds, jnp.zeros(1, jnp.int32)])

    grads = jnp.stack([qg, og])
    sent = jnp.transpose(grads.reshape(2, 2, 32, 256), (1, 0, 2, 3))
    sent = jnp.broadcast_to(sent[:, None], (2, 16, 2, 32, 256)).reshape(32, 2, 32, 256)
    got = lax.all_to_all(sent, PLANE, split_axis=0, concat_axis=0, tiled=True)
    got = got.reshape(2, 16, 2, 32, 256)
    grad_other = swap_half(jnp.stack([qb, ob]))
    level = lax.all_gather(jnp.stack([qx, ox])[None], ZH, axis=0, tiled=True)

    keep, *sends = whole(
        rotate_grad_kernel,
        [shape(4, 2, 32, 512, dtype=F32)] + [shape(4, 72, 512)] * 2 + [shape(2, 72, 512)] * 2,
        [where, got, qb, ob, grad_other],
        flops=2 * 2 * 512 * 512 * 512,
    )
    *sends, qa, oa, level = lax.optimization_barrier((*sends, qa, oa, level))
    sends = [shift(w, by) for w, by in zip(sends, (1, -1, 2, -2))]
    act_other = swap_half(jnp.stack([qa, oa]))
    [words] = whole(near_sum_kernel, [shape(4, 72, 512)], [keep] + sends, scalars=0)
    words, level = lax.optimization_barrier((words, level))
    inputs = [level] + [
        shift(w, by) for w, by in ((level, 1), (level, -1), (level[:2], 2), (level[2:], -2))
    ]
    words = lax.all_to_all(words, ZH, split_axis=0, concat_axis=0, tiled=True)
    [words] = whole(far_sum_kernel, [shape(1, 72, 512)], [words], scalars=0)

    [act_words] = whole(
        rotate_act_kernel,
        [shape(16, 72, 512)],
        [where] + inputs + [qa, oa, act_other],
        flops=2 * 2 * 512 * 512 * 512,
    )
    words, act_words = lax.optimization_barrier((words, act_words))
    act_words = lax.all_to_all(act_words, ROW, split_axis=0, concat_axis=0, tiled=True)

    words = lax.all_gather(words, Z8, axis=0, tiled=True)
    other = swap_half(words)
    words, act_words = lax.optimization_barrier((words, act_words))
    mine = [words, shift(words[:4], 1), shift(words[4:], -1)]
    others = [other, shift(other[:4], 1), shift(other[4:], -1)]

    [act_words] = whole(act_sum_kernel, [shape(2, 16, 72, 256)], [where, act_words])
    act_words = act_words.reshape(32, 72, 256)
    act_words = lax.all_to_all(act_words, PLANE, split_axis=0, concat_axis=0, tiled=True)
    [act] = whole(open_act_kernel, [shape(2, 256, 1024, dtype=F32)], [act_words], scalars=0)

    return tuple(
        whole(
            correct_kernel,
            [shape(512, 256, dtype=F32)] * 2,
            [where, act] + mine + others,
            scratch=[
                pltpu.VMEM((1024, 512), BF16),
                pltpu.VMEM((1024, 512), BF16),
                pltpu.VMEM((256, 512), F32),
                pltpu.VMEM((256, 512), F32),
            ],
            flops=2 * 2 * 7 * 3 * 256 * 512 * 256,
        )
    )


def solution(mesh):
    fine = Mesh(mesh.devices.reshape(2, 4, 2, 2, 4, 2, 2), ("xl", "y", "c", "xh") + Z)
    row, col = ROW, ("xh",) + Z
    one = (P(col, row), P(row, col), P(row, col), P(col, row))
    out_specs = (P(row, col), P(row, col))
    return jax.shard_map(
        per_device, mesh=fine, in_specs=(P(),) + one + one, out_specs=out_specs, check_vma=False
    )
```

time: 228 us -> 184 us (0.81); the launches traced: 225 us -> 183 us
  waiting for transfers between devices: 81.3 us -> 18.7 us
  blocking collectives: 44.5 us -> 56.4 us
  starting transfers between devices: 78.1 us -> 87.6 us
    ppermute x6 -> x3, waiting for transfers between devices: 36.1 us -> 2.73 us  [swap_half(): return lax.ppermute(x, 'xh', [(0, 1), (1, 0)])]
    ppermute x9 -> x12, starting transfers between devices: 28.7 us -> 46 us  [shift(): return lax.ppermute(x, Z, [(i, (i + by) % NZ) for i in range(NZ)])]
    all_to_all x1, waiting for transfers between devices: 15.5 us -> 0.01 us  [per_device(): words = lax.all_to_all(words, ZH, split_axis=0, concat_axis=0, tiled=True)]
    ppermute x9 -> x12, waiting for transfers between devices: 29.6 us -> 16 us  [shift(): return lax.ppermute(x, Z, [(i, (i + by) % NZ) for i in range(NZ)])]
    all_gather x2, blocking collectives: 44.5 us -> 56.4 us  [the longest x1 31.4 us: per_device(): words = lax.all_gather(words, Z8, axis=0, tiled=True)]
    ppermute x6 -> x3, starting transfers between devices: 20 us -> 10.9 us  [swap_half(): return lax.ppermute(x, 'xh', [(0, 1), (1, 0)])]
    pallas_call x6 -> x7, Pallas kernels: 15.9 us -> 15.6 us  [whole(): pl.pallas_call(kernel, out_shape=outs, in_specs=specs, out_specs=[pl.Bloc...]
  transfers between devices with their start and end apart: 19 -> 19, of which waited for: 12 -> 6; matrix products, arithmetic and copies ran while one was open for 0% -> 1% of each run, Pallas kernels for 2% -> 3%
where the time goes in v3:
time: 184 us; the launch traced here: 183 us
  starting transfers between devices  87.6 us (48%)
  blocking collectives  56.4 us (31%)
  waiting for transfers between devices  18.7 us (10%)
  Pallas kernels  15.6 us (8%)
  local copies, waits for them, and re-layouts  2.9 us (2%)
    ppermute x12, starting transfers between devices, shift(): return lax.ppermute(x, Z, [(i, (i + by) % NZ) for i in range(NZ)])  46 us
    all_gather x1, blocking collectives, per_device(): words = lax.all_gather(words, Z8, axis=0, tiled=True)  31.4 us
    all_gather x1, blocking collectives, per_device(): level = lax.all_gather(jnp.stack([qx, ox])[None], ZH, axis=0, tiled=True)  25.1 us
    ppermute x12, waiting for transfers between devices, shift(): return lax.ppermute(x, Z, [(i, (i + by) % NZ) for i in range(NZ)])  16 us
    pallas_call x7, Pallas kernels, whole(): pl.pallas_call(kernel, out_shape=outs, in_specs=specs, out_specs=[pl.Bloc...  15.6 us
    ppermute x3, starting transfers between devices, swap_half(): return lax.ppermute(x, 'xh', [(0, 1), (1, 0)])  10.9 us
    all_to_all x1, starting transfers between devices, per_device(): got = lax.all_to_all(sent, PLANE, split_axis=0, concat_axis=0, tiled=True)  9.74 us
    all_to_all x1, starting transfers between devices, per_device(): words = lax.all_to_all(words, ZH, split_axis=0, concat_axis=0, tiled=True)  8.28 us
  transfers between devices with their start and end apart: 19, of which 6 were waited for; matrix products, arithmetic and copies ran while one was open for 1% of the time, Pallas kernels for 3%

profile of v3, /device:TPU:6, one launch (start us, length us, event | category | flops | bytes accessed | tf_op | source)
XLA Modules:
  0.0 183.3 jit_solution(17394837853661557497)
XLA Ops:
  0.6 0.8 maximum_bitcast_fusion
  1.4 1.1 broadcast_in_dim.4
  2.5 9.7 %all-to-all-start = ((bf16[32,2,32,256]{3,2,1,0:T(8,128)(2,1)}), bf16[32,2,32,256]{3,2,1,0:T(8,128)(2,1)S(1)}, u32[]{:S(2)}, u32[]{:S(2)}) async-start(bf16[32,2,32,256]{3,2,1,0:T(8,128)(2,1)} %bitcast.5), calls=%async_computation | async-start | bytes 2097152 | tf_op jit(solution)/shard_map/all_to_all | solution.py:215
  12.3 0.0 copy-start.6
  12.3 0.1 pad_maximum_fusion
  12.4 3.3 %collective-permute-start = (bf16[2,256,512]{2,1,0:T(8,128)(2,1)S(1)}, bf16[2,256,512]{2,1,0:T(8,128)(2,1)S(1)}, u32[]{:S(2)}, u32[]{:S(2)}) collective-permute-start(bf16[2,256,512]{2,1,0:T(8,128)(2,1)S(1)} %pad_maximum_fusion), channel_id=1, source_target_pairs={{0,16},{16,0},{1,17},{17,1},{2,18},{18,2},{3,19},{19,3},{4,20},{20... | collective-permute-start | bytes 1572872 | tf_op jit(solution)/shard_map/ppermute | solution.py:26
  15.7 25.1 %all-gather = bf16[8,32,512]{2,1,0:T(8,128)(2,1)S(1)} all-gather(bf16[2,32,512]{2,1,0:T(8,128)(2,1)S(1)} %pad_maximum_fusion.2), channel_id=2, replica_groups=mesh['xl'=2,'y'=4,'c'=2,'xh'=2,'zh'=4,'zm'=2,'zl'=2] {'zh'}, dimensions={0}, use_global_device_ids=true | all-gather | bytes 327680 | tf_op jit(solution)/shard_map/all_gather | solution.py:218
  40.7 0.1 convert_reduce_fusion
  40.9 0.1 pad_add_fusion.where
  41.0 0.0 collective-permute-done.other
  41.0 1.3 shard_map.104
  42.3 0.0 copy-start.2
  42.3 0.0 copy-start.3
  42.3 3.0 %collective-permute-start.1 = (s16[4,72,512]{2,1,0:T(8,128)(2,1)S(1)}, s16[4,72,512]{2,1,0:T(8,128)(2,1)S(1)}, u32[]{:S(2)}, u32[]{:S(2)}) collective-permute-start(s16[4,72,512]{2,1,0:T(8,128)(2,1)S(1)} %get-tuple-element.25), channel_id=1, source_target_pairs={{0,1},{1,2},{2,3},{3,4},{4,5},{5,6},{6,7},{7,8},{8,9},{9,10},{10,1... | collective-permute-start | bytes 884744 | tf_op jit(solution)/shard_map/ppermute | solution.py:22
  45.3 4.8 %collective-permute-start.2 = (s16[4,72,512]{2,1,0:T(8,128)(2,1)S(1)}, s16[4,72,512]{2,1,0:T(8,128)(2,1)S(1)}, u32[]{:S(2)}, u32[]{:S(2)}) collective-permute-start(s16[4,72,512]{2,1,0:T(8,128)(2,1)S(1)} %get-tuple-element.26), channel_id=1, source_target_pairs={{0,15},{1,0},{2,1},{3,2},{4,3},{5,4},{6,5},{7,6},{8,7},{9,8},{10,9... | collective-permute-start | bytes 884744 | tf_op jit(solution)/shard_map/ppermute | solution.py:22
  50.1 1.9 %collective-permute-start.3 = (s16[2,72,512]{2,1,0:T(8,128)(2,1)S(1)}, s16[2,72,512]{2,1,0:T(8,128)(2,1)S(1)}, u32[]{:S(2)}, u32[]{:S(2)}) collective-permute-start(s16[2,72,512]{2,1,0:T(8,128)(2,1)S(1)} %get-tuple-element.27), channel_id=1, source_target_pairs={{0,2},{1,3},{2,4},{3,5},{4,6},{5,7},{6,8},{7,9},{8,10},{9,11},{10,... | collective-permute-start | bytes 442376 | tf_op jit(solution)/shard_map/ppermute | solution.py:22
  52.0 6.0 %collective-permute-start.4 = (s16[2,72,512]{2,1,0:T(8,128)(2,1)S(1)}, s16[2,72,512]{2,1,0:T(8,128)(2,1)S(1)}, u32[]{:S(2)}, u32[]{:S(2)}) collective-permute-start(s16[2,72,512]{2,1,0:T(8,128)(2,1)S(1)} %get-tuple-element.28), channel_id=1, source_target_pairs={{0,14},{1,15},{2,0},{3,1},{4,2},{5,3},{6,4},{7,5},{8,6},{9,7},{10,... | collective-permute-start | bytes 442376 | tf_op jit(solution)/shard_map/ppermute | solution.py:22
  58.0 3.0 %collective-permute-done.3.up = s16[2,72,512]{2,1,0:T(8,128)(2,1)S(1)} collective-permute-done((s16[2,72,512]{2,1,0:T(8,128)(2,1)S(1)}, s16[2,72,512]{2,1,0:T(8,128)(2,1)S(1)}, u32[]{:S(2)}, u32[]{:S(2)}) %collective-permute-start.3) | collective-permute-done | bytes 147488 | tf_op jit(solution)/shard_map/ppermute | solution.py:22
  61.1 2.4 %collective-permute-done.4.down = s16[2,72,512]{2,1,0:T(8,128)(2,1)S(1)} collective-permute-done((s16[2,72,512]{2,1,0:T(8,128)(2,1)S(1)}, s16[2,72,512]{2,1,0:T(8,128)(2,1)S(1)}, u32[]{:S(2)}, u32[]{:S(2)}) %collective-permute-start.4) | collective-permute-done | bytes 147488 | tf_op jit(solution)/shard_map/ppermute | solution.py:22
  63.5 0.0 collective-permute-done.1.w1
  63.5 0.0 collective-permute-done.2.w3
  63.5 1.1 shard_map.105
  64.6 8.3 %all-to-all-start.1 = ((s16[4,72,512]{2,1,0:T(8,128)(2,1)}), s16[4,72,512]{2,1,0:T(8,128)(2,1)S(1)}, u32[]{:S(2)}, u32[]{:S(2)}) async-start(s16[4,72,512]{2,1,0:T(8,128)(2,1)} %shard_map.105), calls=%async_computation.1 | async-start | bytes 589824 | tf_op jit(solution)/shard_map/all_to_all | solution.py:234
  72.8 0.1 pad_maximum_fusion.1
  72.9 4.0 %collective-permute-start.9 = (bf16[2,512,256]{2,1,0:T(8,128)(2,1)S(1)}, bf16[2,512,256]{2,1,0:T(8,128)(2,1)S(1)}, u32[]{:S(2)}, u32[]{:S(2)}) collective-permute-start(bf16[2,512,256]{2,1,0:T(8,128)(2,1)S(1)} %pad_maximum_fusion.1), channel_id=1, source_target_pairs={{0,16},{16,0},{1,17},{17,1},{2,18},{18,2},{3,19},{19,3},{4,20},{20... | collective-permute-start | bytes 1572872 | tf_op jit(solution)/shard_map/ppermute | solution.py:26
  76.9 1.9 %collective-permute-start.5 = (bf16[4,2,32,512]{3,2,1,0:T(8,128)(2,1)S(1)}, bf16[4,2,32,512]{3,2,1,0:T(8,128)(2,1)S(1)}, u32[]{:S(2)}, u32[]{:S(2)}) collective-permute-start(bf16[4,2,32,512]{3,2,1,0:T(8,128)(2,1)S(1)} %bitcast.17), channel_id=1, source_target_pairs={{0,1},{1,2},{2,3},{3,4},{4,5},{5,6},{6,7},{7,8},{8,9},{9,10},{10,1... | collective-permute-start | bytes 786440 | tf_op jit(solution)/shard_map/ppermute | solution.py:22
  78.9 5.8 %collective-permute-start.6 = (bf16[4,2,32,512]{3,2,1,0:T(8,128)(2,1)S(1)}, bf16[4,2,32,512]{3,2,1,0:T(8,128)(2,1)S(1)}, u32[]{:S(2)}, u32[]{:S(2)}) collective-permute-start(bf16[4,2,32,512]{3,2,1,0:T(8,128)(2,1)S(1)} %bitcast.18), channel_id=1, source_target_pairs={{0,15},{1,0},{2,1},{3,2},{4,3},{5,4},{6,5},{7,6},{8,7},{9,8},{10,9... | collective-permute-start | bytes 786440 | tf_op jit(solution)/shard_map/ppermute | solution.py:22
  84.7 3.0 %collective-permute-start.7 = (bf16[2,2,32,512]{3,2,1,0:T(8,128)(2,1)S(1)}, bf16[2,2,32,512]{3,2,1,0:T(8,128)(2,1)S(1)}, u32[]{:S(2)}, u32[]{:S(2)}) collective-permute-start(bf16[2,2,32,512]{3,2,1,0:T(8,128)(2,1)S(1)} %get-tuple-element.43), channel_id=1, source_target_pairs={{0,2},{1,3},{2,4},{3,5},{4,6},{5,7},{6,8},{7,9},{8,10},{9,11},{10,... | collective-permute-start | bytes 393224 | tf_op jit(solution)/shard_map/ppermute | solution.py:22
  87.7 5.5 %collective-permute-start.8 = (bf16[2,2,32,512]{3,2,1,0:T(8,128)(2,1)S(1)}, bf16[2,2,32,512]{3,2,1,0:T(8,128)(2,1)S(1)}, u32[]{:S(2)}, u32[]{:S(2)}) collective-permute-start(bf16[2,2,32,512]{3,2,1,0:T(8,128)(2,1)S(1)} %get-tuple-element.42), channel_id=1, source_target_pairs={{0,14},{1,15},{2,0},{3,1},{4,2},{5,3},{6,4},{7,5},{8,6},{9,7},{10,... | collective-permute-start | bytes 393224 | tf_op jit(solution)/shard_map/ppermute | solution.py:22
  93.2 6.5 %collective-permute-done.7.up = bf16[2,2,32,512]{3,2,1,0:T(8,128)(2,1)S(1)} collective-permute-done((bf16[2,2,32,512]{3,2,1,0:T(8,128)(2,1)S(1)}, bf16[2,2,32,512]{3,2,1,0:T(8,128)(2,1)S(1)}, u32[]{:S(2)}, u32[]{:S(2)}) %collective-permute-start.7) | collective-permute-done | bytes 131104 | tf_op jit(solution)/shard_map/ppermute | solution.py:22
  99.7 2.5 %shard_map.107 = s16[16,72,512]{2,1,0:T(8,128)(2,1)} custom-call(s32[8]{0:T(128)S(1)} %pad_add_fusion.where, bf16[4,2,32,512]{3,2,1,0:T(8,128)(2,1)S(1)} %bitcast.20, bf16[4,2,32,512]{3,2,1,0:T(8,128)(2,1)S(1)} %collective-permute-done.5.x1, bf16[4,2,32,512]{3,2,1,0:T(8,128)(2,1)S(1)} %collective-permute-done.6.x3, ...), custom_call_target="tpu_custom_call" | custom-call | flops 536870912 | bytes 3276832 | tf_op jit(solution)/shard_map/pallas_call | solution.py:37
  102.2 0.2 shard_map.106
  102.4 5.8 %all-to-all-start.2 = ((s16[16,72,512]{2,1,0:T(8,128)(2,1)}), s16[16,72,512]{2,1,0:T(8,128)(2,1)S(1)}, u32[]{:S(2)}, u32[]{:S(2)}) async-start(s16[16,72,512]{2,1,0:T(8,128)(2,1)} %shard_map.107), calls=%async_computation.2 | async-start | bytes 2359296 | tf_op jit(solution)/shard_map/all_to_all | solution.py:244
  108.1 31.4 %all_gather.7.rest_0_ = s16[8,72,512]{2,1,0:T(8,128)(2,1)S(1)} all-gather(s16[1,72,512]{2,1,0:T(8,128)(2,1)S(1)} %shard_map.106), channel_id=1, replica_groups=mesh['xl'=2,'y'=4,'c'=2,'xh'=2,'zh'=4,'zm'=2,'zl'=2] {'zh','zm'}, dimensions={0}, use_global_device_ids=true | all-gather | bytes 663552 | tf_op jit(solution)/shard_map/all_gather | solution.py:246
  139.5 3.6 %collective-permute-start.12 = (s16[8,72,512]{2,1,0:T(8,128)(2,1)S(1)}, s16[8,72,512]{2,1,0:T(8,128)(2,1)S(1)}, u32[]{:S(2)}, u32[]{:S(2)}) collective-permute-start(s16[8,72,512]{2,1,0:T(8,128)(2,1)S(1)} %all_gather.7.rest_0_), channel_id=1, source_target_pairs={{0,16},{16,0},{1,17},{17,1},{2,18},{18,2},{3,19},{19,3},{4,20},{20... | collective-permute-start | bytes 1769480 | tf_op jit(solution)/shard_map/ppermute | solution.py:26
  143.1 2.1 %shard_map.108 = s16[2,16,72,256]{3,2,1,0:T(8,128)(2,1)} custom-call(s32[8]{0:T(128)S(1)} %pad_add_fusion.where, s16[16,72,512]{2,1,0:T(8,128)(2,1)S(1)} %all-to-all-done.2.w), custom_call_target="tpu_custom_call" | custom-call | bytes 2359328 | tf_op jit(solution)/shard_map/pallas_call | solution.py:37
  145.2 6.9 %all-to-all-start.3 = ((s16[32,72,256]{2,1,0:T(8,128)(2,1)}), s16[32,72,256]{2,1,0:T(8,128)(2,1)S(1)}, u32[]{:S(2)}, u32[]{:S(2)}) async-start(s16[32,72,256]{2,1,0:T(8,128)(2,1)} %bitcast.14), calls=%async_computation.3 | async-start | bytes 2359296 | tf_op jit(solution)/shard_map/all_to_all | solution.py:254
  152.1 2.7 %collective-permute-done.12.rest_3_ = s16[8,72,512]{2,1,0:T(8,128)(2,1)S(1)} collective-permute-done((s16[8,72,512]{2,1,0:T(8,128)(2,1)S(1)}, s16[8,72,512]{2,1,0:T(8,128)(2,1)S(1)}, u32[]{:S(2)}, u32[]{:S(2)}) %collective-permute-start.12) | collective-permute-done | bytes 589856 | tf_op jit(solution)/shard_map/ppermute | solution.py:26
  154.9 0.9 fusion
  155.7 3.7 %collective-permute-start.13 = (s16[4,72,512]{2,1,0:T(8,128)(2,1)}, s16[4,72,512]{2,1,0:T(8,128)(2,1)S(1)}, u32[]{:S(2)}, u32[]{:S(2)}) collective-permute-start(s16[4,72,512]{2,1,0:T(8,128)(2,1)} %get-tuple-element.39), channel_id=1, source_target_pairs={{0,1},{1,2},{2,3},{3,4},{4,5},{5,6},{6,7},{7,8},{8,9},{9,10},{10,1... | collective-permute-start | bytes 884744 | tf_op jit(solution)/shard_map/ppermute | solution.py:22
  159.4 3.3 %collective-permute-start.14 = (s16[4,72,512]{2,1,0:T(8,128)(2,1)}, s16[4,72,512]{2,1,0:T(8,128)(2,1)S(1)}, u32[]{:S(2)}, u32[]{:S(2)}) collective-permute-start(s16[4,72,512]{2,1,0:T(8,128)(2,1)} %get-tuple-element.38), channel_id=1, source_target_pairs={{0,15},{1,0},{2,1},{3,2},{4,3},{5,4},{6,5},{7,6},{8,7},{9,8},{10,9... | collective-permute-start | bytes 884744 | tf_op jit(solution)/shard_map/ppermute | solution.py:22
  162.8 0.9 fusion.1
  163.6 2.5 %collective-permute-start.10 = (s16[4,72,512]{2,1,0:T(8,128)(2,1)}, s16[4,72,512]{2,1,0:T(8,128)(2,1)S(1)}, u32[]{:S(2)}, u32[]{:S(2)}) collective-permute-start(s16[4,72,512]{2,1,0:T(8,128)(2,1)} %get-tuple-element.41), channel_id=1, source_target_pairs={{0,1},{1,2},{2,3},{3,4},{4,5},{5,6},{6,7},{7,8},{8,9},{9,10},{10,1... | collective-permute-start | bytes 884744 | tf_op jit(solution)/shard_map/ppermute | solution.py:22
  166.2 4.5 %collective-permute-start.11 = (s16[4,72,512]{2,1,0:T(8,128)(2,1)}, s16[4,72,512]{2,1,0:T(8,128)(2,1)S(1)}, u32[]{:S(2)}, u32[]{:S(2)}) collective-permute-start(s16[4,72,512]{2,1,0:T(8,128)(2,1)} %get-tuple-element.40), channel_id=1, source_target_pairs={{0,15},{1,0},{2,1},{3,2},{4,3},{5,4},{6,5},{7,6},{8,7},{9,8},{10,9... | collective-permute-start | bytes 884744 | tf_op jit(solution)/shard_map/ppermute | solution.py:22
  170.7 0.6 shard_map.109.act
  171.4 2.3 %collective-permute-done.10.rest_1_ = s16[4,72,512]{2,1,0:T(8,128)(2,1)S(1)} collective-permute-done((s16[4,72,512]{2,1,0:T(8,128)(2,1)}, s16[4,72,512]{2,1,0:T(8,128)(2,1)S(1)}, u32[]{:S(2)}, u32[]{:S(2)}) %collective-permute-start.10) | collective-permute-done | bytes 294944 | tf_op jit(solution)/shard_map/ppermute | solution.py:22
  173.7 1.8 collective-permute-done.11.rest_2_
  175.4 7.8 %shard_map.110 = (f32[512,256]{1,0:T(8,128)}, f32[512,256]{1,0:T(8,128)}) custom-call(s32[8]{0:T(128)S(1)} %pad_add_fusion.where, f32[2,256,1024]{2,1,0:T(8,128)S(1)} %shard_map.109.act, s16[8,72,512]{2,1,0:T(8,128)(2,1)S(1)} %all_gather.7.rest_0_, s16[4,72,512]{2,1,0:T(8,128)(2,1)S(1)} %collective-permute-done.10.rest_1_, ...), custom_call_target="tpu_custom_call" | custom-call | flops 2818572288 | bytes 5505056 | tf_op jit(solution)/shard_map/pallas_call | solution.py:37
  (24 shorter events, 0.1 us)
Async XLA Ops:
  2.5 9.8 %copy-start = (bf16[256,512]{1,0:T(8,128)(2,1)S(1)}, bf16[256,512]{1,0:T(8,128)(2,1)}, u32[]{:S(2)}) copy-start(bf16[256,512]{1,0:T(8,128)(2,1)} %qb.1) | copy-start | bytes 786436
  2.5 9.8 %copy-start.1 = (bf16[256,512]{1,0:T(8,128)(2,1)S(1)}, bf16[256,512]{1,0:T(8,128)(2,1)}, u32[]{:S(2)}) copy-start(bf16[256,512]{1,0:T(8,128)(2,1)} %ob.1) | copy-start | bytes 786436
  2.5 13.1 %copy-start.4 = (bf16[32,512]{1,0:T(8,128)(2,1)S(1)}, bf16[32,512]{1,0:T(8,128)(2,1)}, u32[]{:S(2)}) copy-start(bf16[32,512]{1,0:T(8,128)(2,1)} %param.14) | copy-start | bytes 98308
  2.5 13.1 %copy-start.5 = (bf16[32,512]{1,0:T(8,128)(2,1)S(1)}, bf16[32,512]{1,0:T(8,128)(2,1)}, u32[]{:S(2)}) copy-start(bf16[32,512]{1,0:T(8,128)(2,1)} %param.10) | copy-start | bytes 98308
  2.5 38.4 %all-to-all-start = ((bf16[32,2,32,256]{3,2,1,0:T(8,128)(2,1)}), bf16[32,2,32,256]{3,2,1,0:T(8,128)(2,1)S(1)}, u32[]{:S(2)}, u32[]{:S(2)}) async-start(bf16[32,2,32,256]{3,2,1,0:T(8,128)(2,1)} %bitcast.5), calls=%async_computation | async-start | bytes 2097152 | tf_op jit(solution)/shard_map/all_to_all | solution.py:215
  12.3 28.5 %copy-start.6 = (s32[1024]{0:T(1024)S(1)}, s32[1024]{0:T(1024)}, u32[]{:S(2)}) copy-start(s32[1024]{0:T(1024)} %param.9) | copy-start | bytes 12292
  12.4 28.6 %collective-permute-start = (bf16[2,256,512]{2,1,0:T(8,128)(2,1)S(1)}, bf16[2,256,512]{2,1,0:T(8,128)(2,1)S(1)}, u32[]{:S(2)}, u32[]{:S(2)}) collective-permute-start(bf16[2,256,512]{2,1,0:T(8,128)(2,1)S(1)} %pad_maximum_fusion), channel_id=1, source_target_pairs={{0,16},{16,0},{1,17},{17,1},{2,18},{18,2},{3,19},{19,3},{4,20},{20... | collective-permute-start | bytes 1572872 | tf_op jit(solution)/shard_map/ppermute | solution.py:26
  42.3 30.6 %copy-start.2 = (bf16[512,256]{1,0:T(8,128)(2,1)S(1)}, bf16[512,256]{1,0:T(8,128)(2,1)}, u32[]{:S(2)}) copy-start(bf16[512,256]{1,0:T(8,128)(2,1)} %qa) | copy-start | bytes 786436
  42.3 30.6 %copy-start.3 = (bf16[512,256]{1,0:T(8,128)(2,1)S(1)}, bf16[512,256]{1,0:T(8,128)(2,1)}, u32[]{:S(2)}) copy-start(bf16[512,256]{1,0:T(8,128)(2,1)} %oa) | copy-start | bytes 786436
  42.3 21.2 %collective-permute-start.1 = (s16[4,72,512]{2,1,0:T(8,128)(2,1)S(1)}, s16[4,72,512]{2,1,0:T(8,128)(2,1)S(1)}, u32[]{:S(2)}, u32[]{:S(2)}) collective-permute-start(s16[4,72,512]{2,1,0:T(8,128)(2,1)S(1)} %get-tuple-element.25), channel_id=1, source_target_pairs={{0,1},{1,2},{2,3},{3,4},{4,5},{5,6},{6,7},{7,8},{8,9},{9,10},{10,1... | collective-permute-start | bytes 884744 | tf_op jit(solution)/shard_map/ppermute | solution.py:22
  45.3 18.2 %collective-permute-start.2 = (s16[4,72,512]{2,1,0:T(8,128)(2,1)S(1)}, s16[4,72,512]{2,1,0:T(8,128)(2,1)S(1)}, u32[]{:S(2)}, u32[]{:S(2)}) collective-permute-start(s16[4,72,512]{2,1,0:T(8,128)(2,1)S(1)} %get-tuple-element.26), channel_id=1, source_target_pairs={{0,15},{1,0},{2,1},{3,2},{4,3},{5,4},{6,5},{7,6},{8,7},{9,8},{10,9... | collective-permute-start | bytes 884744 | tf_op jit(solution)/shard_map/ppermute | solution.py:22
  50.1 11.0 %collective-permute-start.3 = (s16[2,72,512]{2,1,0:T(8,128)(2,1)S(1)}, s16[2,72,512]{2,1,0:T(8,128)(2,1)S(1)}, u32[]{:S(2)}, u32[]{:S(2)}) collective-permute-start(s16[2,72,512]{2,1,0:T(8,128)(2,1)S(1)} %get-tuple-element.27), channel_id=1, source_target_pairs={{0,2},{1,3},{2,4},{3,5},{4,6},{5,7},{6,8},{7,9},{8,10},{9,11},{10,... | collective-permute-start | bytes 442376 | tf_op jit(solution)/shard_map/ppermute | solution.py:22
  52.0 11.5 %collective-permute-start.4 = (s16[2,72,512]{2,1,0:T(8,128)(2,1)S(1)}, s16[2,72,512]{2,1,0:T(8,128)(2,1)S(1)}, u32[]{:S(2)}, u32[]{:S(2)}) collective-permute-start(s16[2,72,512]{2,1,0:T(8,128)(2,1)S(1)} %get-tuple-element.28), channel_id=1, source_target_pairs={{0,14},{1,15},{2,0},{3,1},{4,2},{5,3},{6,4},{7,5},{8,6},{9,7},{10,... | collective-permute-start | bytes 442376 | tf_op jit(solution)/shard_map/ppermute | solution.py:22
  64.6 37.6 %all-to-all-start.1 = ((s16[4,72,512]{2,1,0:T(8,128)(2,1)}), s16[4,72,512]{2,1,0:T(8,128)(2,1)S(1)}, u32[]{:S(2)}, u32[]{:S(2)}) async-start(s16[4,72,512]{2,1,0:T(8,128)(2,1)} %shard_map.105), calls=%async_computation.1 | async-start | bytes 589824 | tf_op jit(solution)/shard_map/all_to_all | solution.py:234
  72.9 26.8 %collective-permute-start.9 = (bf16[2,512,256]{2,1,0:T(8,128)(2,1)S(1)}, bf16[2,512,256]{2,1,0:T(8,128)(2,1)S(1)}, u32[]{:S(2)}, u32[]{:S(2)}) collective-permute-start(bf16[2,512,256]{2,1,0:T(8,128)(2,1)S(1)} %pad_maximum_fusion.1), channel_id=1, source_target_pairs={{0,16},{16,0},{1,17},{17,1},{2,18},{18,2},{3,19},{19,3},{4,20},{20... | collective-permute-start | bytes 1572872 | tf_op jit(solution)/shard_map/ppermute | solution.py:26
  76.9 22.7 %collective-permute-start.5 = (bf16[4,2,32,512]{3,2,1,0:T(8,128)(2,1)S(1)}, bf16[4,2,32,512]{3,2,1,0:T(8,128)(2,1)S(1)}, u32[]{:S(2)}, u32[]{:S(2)}) collective-permute-start(bf16[4,2,32,512]{3,2,1,0:T(8,128)(2,1)S(1)} %bitcast.17), channel_id=1, source_target_pairs={{0,1},{1,2},{2,3},{3,4},{4,5},{5,6},{6,7},{7,8},{8,9},{9,10},{10,1... | collective-permute-start | bytes 786440 | tf_op jit(solution)/shard_map/ppermute | solution.py:22
  78.9 20.8 %collective-permute-start.6 = (bf16[4,2,32,512]{3,2,1,0:T(8,128)(2,1)S(1)}, bf16[4,2,32,512]{3,2,1,0:T(8,128)(2,1)S(1)}, u32[]{:S(2)}, u32[]{:S(2)}) collective-permute-start(bf16[4,2,32,512]{3,2,1,0:T(8,128)(2,1)S(1)} %bitcast.18), channel_id=1, source_target_pairs={{0,15},{1,0},{2,1},{3,2},{4,3},{5,4},{6,5},{7,6},{8,7},{9,8},{10,9... | collective-permute-start | bytes 786440 | tf_op jit(solution)/shard_map/ppermute | solution.py:22
  84.7 15.0 %collective-permute-start.7 = (bf16[2,2,32,512]{3,2,1,0:T(8,128)(2,1)S(1)}, bf16[2,2,32,512]{3,2,1,0:T(8,128)(2,1)S(1)}, u32[]{:S(2)}, u32[]{:S(2)}) collective-permute-start(bf16[2,2,32,512]{3,2,1,0:T(8,128)(2,1)S(1)} %get-tuple-element.43), channel_id=1, source_target_pairs={{0,2},{1,3},{2,4},{3,5},{4,6},{5,7},{6,8},{7,9},{8,10},{9,11},{10,... | collective-permute-start | bytes 393224 | tf_op jit(solution)/shard_map/ppermute | solution.py:22
  87.7 12.0 %collective-permute-start.8 = (bf16[2,2,32,512]{3,2,1,0:T(8,128)(2,1)S(1)}, bf16[2,2,32,512]{3,2,1,0:T(8,128)(2,1)S(1)}, u32[]{:S(2)}, u32[]{:S(2)}) collective-permute-start(bf16[2,2,32,512]{3,2,1,0:T(8,128)(2,1)S(1)} %get-tuple-element.42), channel_id=1, source_target_pairs={{0,14},{1,15},{2,0},{3,1},{4,2},{5,3},{6,4},{7,5},{8,6},{9,7},{10,... | collective-permute-start | bytes 393224 | tf_op jit(solution)/shard_map/ppermute | solution.py:22
  102.4 40.7 %all-to-all-start.2 = ((s16[16,72,512]{2,1,0:T(8,128)(2,1)}), s16[16,72,512]{2,1,0:T(8,128)(2,1)S(1)}, u32[]{:S(2)}, u32[]{:S(2)}) async-start(s16[16,72,512]{2,1,0:T(8,128)(2,1)} %shard_map.107), calls=%async_computation.2 | async-start | bytes 2359296 | tf_op jit(solution)/shard_map/all_to_all | solution.py:244
  139.5 15.4 %collective-permute-start.12 = (s16[8,72,512]{2,1,0:T(8,128)(2,1)S(1)}, s16[8,72,512]{2,1,0:T(8,128)(2,1)S(1)}, u32[]{:S(2)}, u32[]{:S(2)}) collective-permute-start(s16[8,72,512]{2,1,0:T(8,128)(2,1)S(1)} %all_gather.7.rest_0_), channel_id=1, source_target_pairs={{0,16},{16,0},{1,17},{17,1},{2,18},{18,2},{3,19},{19,3},{4,20},{20... | collective-permute-start | bytes 1769480 | tf_op jit(solution)/shard_map/ppermute | solution.py:26
  145.2 25.5 %all-to-all-start.3 = ((s16[32,72,256]{2,1,0:T(8,128)(2,1)}), s16[32,72,256]{2,1,0:T(8,128)(2,1)S(1)}, u32[]{:S(2)}, u32[]{:S(2)}) async-start(s16[32,72,256]{2,1,0:T(8,128)(2,1)} %bitcast.14), calls=%async_computation.3 | async-start | bytes 2359296 | tf_op jit(solution)/shard_map/all_to_all | solution.py:254
  155.7 15.6 %collective-permute-start.13 = (s16[4,72,512]{2,1,0:T(8,128)(2,1)}, s16[4,72,512]{2,1,0:T(8,128)(2,1)S(1)}, u32[]{:S(2)}, u32[]{:S(2)}) collective-permute-start(s16[4,72,512]{2,1,0:T(8,128)(2,1)} %get-tuple-element.39), channel_id=1, source_target_pairs={{0,1},{1,2},{2,3},{3,4},{4,5},{5,6},{6,7},{7,8},{8,9},{9,10},{10,1... | collective-permute-start | bytes 884744 | tf_op jit(solution)/shard_map/ppermute | solution.py:22
  159.4 11.9 %collective-permute-start.14 = (s16[4,72,512]{2,1,0:T(8,128)(2,1)}, s16[4,72,512]{2,1,0:T(8,128)(2,1)S(1)}, u32[]{:S(2)}, u32[]{:S(2)}) collective-permute-start(s16[4,72,512]{2,1,0:T(8,128)(2,1)} %get-tuple-element.38), channel_id=1, source_target_pairs={{0,15},{1,0},{2,1},{3,2},{4,3},{5,4},{6,5},{7,6},{8,7},{9,8},{10,9... | collective-permute-start | bytes 884744 | tf_op jit(solution)/shard_map/ppermute | solution.py:22
  163.6 10.0 %collective-permute-start.10 = (s16[4,72,512]{2,1,0:T(8,128)(2,1)}, s16[4,72,512]{2,1,0:T(8,128)(2,1)S(1)}, u32[]{:S(2)}, u32[]{:S(2)}) collective-permute-start(s16[4,72,512]{2,1,0:T(8,128)(2,1)} %get-tuple-element.41), channel_id=1, source_target_pairs={{0,1},{1,2},{2,3},{3,4},{4,5},{5,6},{6,7},{7,8},{8,9},{9,10},{10,1... | collective-permute-start | bytes 884744 | tf_op jit(solution)/shard_map/ppermute | solution.py:22
  166.2 9.3 %collective-permute-start.11 = (s16[4,72,512]{2,1,0:T(8,128)(2,1)}, s16[4,72,512]{2,1,0:T(8,128)(2,1)S(1)}, u32[]{:S(2)}, u32[]{:S(2)}) collective-permute-start(s16[4,72,512]{2,1,0:T(8,128)(2,1)} %get-tuple-element.40), channel_id=1, source_target_pairs={{0,15},{1,0},{2,1},{3,2},{4,3},{5,4},{6,5},{7,6},{8,7},{9,8},{10,9... | collective-permute-start | bytes 884744 | tf_op jit(solution)/shard_map/ppermute | solution.py:22

commit v4 on v3

--- a/solution.py
+++ b/solution.py
@@ -74,44 +74,38 @@
 
 def rotate_grad_kernel(where, got, qb, ob, other, keep, near1, near3, two_up, two_down):
     z, xh = where[0], where[1]
+    mine = jnp.where(xh == 0, qb[...], ob[...])
     for ahead in (1, 3, 2, 0):
         residue = lax.rem(z + ahead, 4)
-        done = []
-        for p in range(2):
-            basis = (qb, ob)[p]
-            rows = [
-                jnp.concatenate([got[side, 4 * j + residue, p] for j in range(4)], axis=0)
-                for side in (xh, 1 - xh)
-            ]
-            done.append(
-                jnp.dot(rows[0], basis[...], preferred_element_type=F32)
-                + jnp.dot(rows[1], other[p], preferred_element_type=F32)
-            )
+        rows = [
+            jnp.concatenate([got[side, 4 * j + residue] for j in range(4)], axis=0)
+            for side in (xh, 1 - xh)
+        ]
+        done = jnp.dot(rows[0], mine, preferred_element_type=F32) + jnp.dot(
+            rows[1], other[...], preferred_element_type=F32
+        )
         for j in range(4):
-            parts = [d[32 * j:32 * j + 32] for d in done]
+            part = done[64 * j:64 * j + 64]
             if ahead == 0:
-                keep[j, 0], keep[j, 1] = parts
+                keep[j] = part
             elif ahead == 2:
-                (two_up, two_down)[j // 2][j % 2] = message(*parts)
+                (two_up, two_down)[j // 2][j % 2] = message(part)
             else:
-                (near1 if ahead == 1 else near3)[j] = message(*parts)
+                (near1 if ahead == 1 else near3)[j] = message(part)
 
 
 def near_sum_kernel(keep, w1, w3, up, down, out):
     for j in range(4):
         two = up if j < 2 else down
-        out[j] = message(
-            *added(
-                [keep[j, 0], keep[j, 1]],
-                opened(w1[j], 32),
-                opened(w3[j], 32),
-                opened(two[j % 2], 32),
-            )
-        )
+        total = opened(w1[j], 64)[0] + opened(w3[j], 64)[0] + opened(two[j % 2], 64)[0]
+        out[j] = message(keep[j] + total)
 
 
 def far_sum_kernel(w, out):
-    out[0] = message(*added(*[opened(w[j], 32) for j in range(4)]))
+    total = opened(w[0], 64)[0]
+    for j in range(1, 4):
+        total = total + opened(w[j], 64)[0]
+    out[0] = message(total)
 
 
 def rotate_act_kernel(where, level, x1, x3, up, down, qa, oa, other, out):
@@ -150,51 +144,54 @@
         out[1 - xh, r] = other
 
 
-def open_act_kernel(w, out):
+def open_act_kernel(w, high, low):
     for e in range(0, 32, 4):
         blocks = [opened(w[e + i], 32) for i in range(4)]
         for p in range(2):
-            out[p, :, 32 * e:32 * e + 128] = jnp.concatenate([b[p] for b in blocks], axis=0).T
-
-
-def correct_kernel(where, act, *rest):
+            x = jnp.concatenate([b[p] for b in blocks], axis=0).T
+            top = x.astype(BF16)
+            high[p, :, 32 * e:32 * e + 128] = top
+            low[p, :, 32 * e:32 * e + 128] = (x - top.astype(F32)).astype(BF16)
+
+
+def correct_kernel(where, act_high, act_low, *rest):
     grads, (q_out, o_out, high, low, acc, total) = rest[:6], rest[6:]
     zl, xh = lax.rem(where[0], 2), where[1]
-    for p in range(2):
-        for side in range(2):
-            half = xh if side == 0 else 1 - xh
-            level, first_w, last_w = grads[3 * side:3 * side + 3]
-            for k in range(16):
-                w = level[k] if k < 8 else (first_w[k - 8] if k < 12 else last_w[k - 12])
-                block = 2 * (k % 8) + (zl if k < 8 else 1 - zl)
-                at = pl.multiple_of(64 * block + 32 * half, 32)
-                x = opened(w, 32)[p]
-                top = x.astype(BF16)
-                high[pl.ds(at, 32), :] = top
-                low[pl.ds(at, 32), :] = (x - top.astype(F32)).astype(BF16)
-        for seq in range(SEQS):
-            first, last = where[2 + seq], where[3 + seq]
-            acc[...] = jnp.zeros_like(acc)
-
-            def chunk(k, carry, first=first, last=last, p=p):
-                at = pl.multiple_of(256 * k, 256)
-                token = at + lax.broadcasted_iota(jnp.int32, (256, 256), 1)
-                a = jnp.where((token >= first) & (token < last), act[p, :, pl.ds(at, 256)], 0.0)
-                a_high = a.astype(BF16)
-                a_low = (a - a_high.astype(F32)).astype(BF16)
-                g_high, g_low = high[pl.ds(at, 256), :], low[pl.ds(at, 256), :]
-                acc[...] += (
+    for side in range(2):
+        half = xh if side == 0 else 1 - xh
+        level, first_w, last_w = grads[3 * side:3 * side + 3]
+        for k in range(16):
+            w = level[k] if k < 8 else (first_w[k - 8] if k < 12 else last_w[k - 12])
+            block = 2 * (k % 8) + (zl if k < 8 else 1 - zl)
+            at = pl.multiple_of(64 * block, 64)
+            [x] = opened(w, 64)
+            top = x.astype(BF16)
+            high[half, pl.ds(at, 64), :] = top
+            low[half, pl.ds(at, 64), :] = (x - top.astype(F32)).astype(BF16)
+    for seq in range(SEQS):
+        first, last = where[2 + seq], where[3 + seq]
+        acc[...] = jnp.zeros_like(acc)
+
+        def chunk(k, carry, first=first, last=last):
+            at = pl.multiple_of(256 * k, 256)
+            token = at + lax.broadcasted_iota(jnp.int32, (1, 256), 1)
+            inside = ((token >= first) & (token < last)).astype(F32).astype(BF16)
+            for p in range(2):
+                a_high = act_high[p, :, pl.ds(at, 256)] * inside
+                a_low = act_low[p, :, pl.ds(at, 256)] * inside
+                g_high, g_low = high[p, pl.ds(at, 256), :], low[p, pl.ds(at, 256), :]
+                acc[p] += (
                     jnp.dot(a_high, g_high, preferred_element_type=F32)
                     + jnp.dot(a_low, g_high, preferred_element_type=F32)
                     + jnp.dot(a_high, g_low, preferred_element_type=F32)
                 )
-                return carry
-
-            lax.fori_loop(first // 256, (last + 255) // 256, chunk, 0)
-            square = acc[...] * acc[...]
-            total[...] = square if seq == 0 else total[...] + square
-        out = (q_out, o_out)[p]
-        out[...] = total[...].T * (1.0 / SEQS)
+            return carry
+
+        lax.fori_loop(first // 256, (last + 255) // 256, chunk, 0)
+        square = acc[...] * acc[...]
+        total[...] = square if seq == 0 else total[...] + square
+    q_out[...] = total[0].T * (1.0 / SEQS)
+    o_out[...] = total[1].T * (1.0 / SEQS)
 
 
 def shape(*dims, dtype=S16):
@@ -210,16 +207,15 @@
     where = jnp.concatenate([jnp.stack([z, xh]).astype(jnp.int32), bounds, jnp.zeros(1, jnp.int32)])
 
     grads = jnp.stack([qg, og])
-    sent = jnp.transpose(grads.reshape(2, 2, 32, 256), (1, 0, 2, 3))
-    sent = jnp.broadcast_to(sent[:, None], (2, 16, 2, 32, 256)).reshape(32, 2, 32, 256)
+    sent = jnp.broadcast_to(grads[:, None], (2, 16, 64, 256)).reshape(32, 64, 256)
     got = lax.all_to_all(sent, PLANE, split_axis=0, concat_axis=0, tiled=True)
-    got = got.reshape(2, 16, 2, 32, 256)
-    grad_other = swap_half(jnp.stack([qb, ob]))
+    got = got.reshape(2, 16, 64, 256)
+    grad_other = swap_half(jnp.where(xh == 0, ob, qb))
     level = lax.all_gather(jnp.stack([qx, ox])[None], ZH, axis=0, tiled=True)
 
     keep, *sends = whole(
         rotate_grad_kernel,
-        [shape(4, 2, 32, 512, dtype=F32)] + [shape(4, 72, 512)] * 2 + [shape(2, 72, 512)] * 2,
+        [shape(4, 64, 512, dtype=F32)] + [shape(4, 72, 512)] * 2 + [shape(2, 72, 512)] * 2,
         [where, got, qb, ob, grad_other],
         flops=2 * 2 * 512 * 512 * 512,
     )
@@ -252,18 +248,18 @@
     [act_words] = whole(act_sum_kernel, [shape(2, 16, 72, 256)], [where, act_words])
     act_words = act_words.reshape(32, 72, 256)
     act_words = lax.all_to_all(act_words, PLANE, split_axis=0, concat_axis=0, tiled=True)
-    [act] = whole(open_act_kernel, [shape(2, 256, 1024, dtype=F32)], [act_words], scalars=0)
+    act = whole(open_act_kernel, [shape(2, 256, 1024, dtype=BF16)] * 2, [act_words], scalars=0)
 
     return tuple(
         whole(
             correct_kernel,
             [shape(512, 256, dtype=F32)] * 2,
-            [where, act] + mine + others,
+            [where] + list(act) + mine + others,
             scratch=[
-                pltpu.VMEM((1024, 512), BF16),
-                pltpu.VMEM((1024, 512), BF16),
-                pltpu.VMEM((256, 512), F32),
-                pltpu.VMEM((256, 512), F32),
+                pltpu.VMEM((2, 1024, 512), BF16),
+                pltpu.VMEM((2, 1024, 512), BF16),
+                pltpu.VMEM((2, 256, 512), F32),
+                pltpu.VMEM((2, 256, 512), F32),
             ],
             flops=2 * 2 * 7 * 3 * 256 * 512 * 256,
         )

time: 184 us -> 181 us (0.984)
  waiting for transfers between devices: 18.7 us -> 15.3 us
  blocking collectives: 56.4 us -> 58.3 us
    ppermute x12, waiting for transfers between devices: 16 us -> 12.7 us  [shift(): return lax.ppermute(x, Z, [(i, (i + by) % NZ) for i in range(NZ)])]
    all_gather x1, blocking collectives: 31.4 us -> 33.2 us  [per_device(): words = lax.all_gather(words, Z8, axis=0, tiled=True)]
  transfers between devices with their start and end apart: 19 -> 19, of which waited for: 6 -> 7; matrix products, arithmetic and copies ran while one was open for 1% -> 1% of each run, Pallas kernels for 3% -> 3%
where the time goes in v4:
time: 181 us; the launch traced here: 179 us
  starting transfers between devices  86.2 us (48%)
  blocking collectives  58.3 us (32%)
  waiting for transfers between devices  15.3 us (8%)
  Pallas kernels  14.5 us (8%)
  local copies, waits for them, and re-layouts  2.89 us (2%)
    ppermute x12, starting transfers between devices, shift(): return lax.ppermute(x, Z, [(i, (i + by) % NZ) for i in range(NZ)])  46.5 us
    all_gather x1, blocking collectives, per_device(): words = lax.all_gather(words, Z8, axis=0, tiled=True)  33.2 us
    all_gather x1, blocking collectives, per_device(): level = lax.all_gather(jnp.stack([qx, ox])[None], ZH, axis=0, tiled=True)  25.1 us
    pallas_call x7, Pallas kernels, whole(): pl.pallas_call(kernel, out_shape=outs, in_specs=specs, out_specs=[pl.Bloc...  14.5 us
    ppermute x12, waiting for transfers between devices, shift(): return lax.ppermute(x, Z, [(i, (i + by) % NZ) for i in range(NZ)])  12.7 us
    ppermute x3, starting transfers between devices, swap_half(): return lax.ppermute(x, 'xh', [(0, 1), (1, 0)])  10.6 us
    all_to_all x1, starting transfers between devices, per_device(): got = lax.all_to_all(sent, PLANE, split_axis=0, concat_axis=0, tiled=True)  9.73 us
    all_to_all x1, starting transfers between devices, per_device(): lax.all_to_all(act_words, PLANE, split_axis=0, concat_axis=0, tiled=True)  6.92 us
  transfers between devices with their start and end apart: 19, of which 7 were waited for; matrix products, arithmetic and copies ran while one was open for 1% of the time, Pallas kernels for 3%

profile of v4, /device:TPU:6, one launch (start us, length us, event | category | flops | bytes accessed | tf_op | source)
XLA Modules:
  0.0 179.1 jit_solution(11968754775592968370)
XLA Ops:
  0.6 0.8 pad_maximum_fusion.1
  1.4 1.1 broadcast_in_dim.4
  2.5 0.0 copy-start.6
  2.5 9.7 %all-to-all-start = ((bf16[32,64,256]{2,1,0:T(8,128)(2,1)}), bf16[32,64,256]{2,1,0:T(8,128)(2,1)S(1)}, u32[]{:S(2)}, u32[]{:S(2)}) async-start(bf16[32,64,256]{2,1,0:T(8,128)(2,1)} %bitcast.4), calls=%async_computation | async-start | bytes 2097152 | tf_op jit(solution)/shard_map/all_to_all | solution.py:211
  12.3 3.3 %collective-permute-start = (bf16[256,512]{1,0:T(8,128)(2,1)S(1)}, bf16[256,512]{1,0:T(8,128)(2,1)S(1)}, u32[]{:S(2)}, u32[]{:S(2)}) collective-permute-start(bf16[256,512]{1,0:T(8,128)(2,1)S(1)} %broadcast_select_fusion), channel_id=1, source_target_pairs={{0,16},{16,0},{1,17},{17,1},{2,18},{18,2},{3,19},{19,3},{4,20},{20... | collective-permute-start | bytes 786440 | tf_op jit(solution)/shard_map/ppermute | solution.py:26
  15.6 25.1 %all-gather = bf16[8,32,512]{2,1,0:T(8,128)(2,1)S(1)} all-gather(bf16[2,32,512]{2,1,0:T(8,128)(2,1)S(1)} %pad_maximum_fusion.2), channel_id=2, replica_groups=mesh['xl'=2,'y'=4,'c'=2,'xh'=2,'zh'=4,'zm'=2,'zl'=2] {'zh'}, dimensions={0}, use_global_device_ids=true | all-gather | bytes 327680 | tf_op jit(solution)/shard_map/all_gather | solution.py:214
  40.7 0.1 convert_reduce_fusion
  40.8 0.1 pad_add_fusion.where
  40.9 0.0 collective-permute-done.other
  40.9 0.0 all-to-all-done
  40.9 1.3 shard_map.104
  42.2 0.0 copy-start
  42.2 0.0 copy-start.1
  42.2 3.0 %collective-permute-start.1 = (s16[4,72,512]{2,1,0:T(8,128)(2,1)S(1)}, s16[4,72,512]{2,1,0:T(8,128)(2,1)S(1)}, u32[]{:S(2)}, u32[]{:S(2)}) collective-permute-start(s16[4,72,512]{2,1,0:T(8,128)(2,1)S(1)} %get-tuple-element.27), channel_id=1, source_target_pairs={{0,1},{1,2},{2,3},{3,4},{4,5},{5,6},{6,7},{7,8},{8,9},{9,10},{10,1... | collective-permute-start | bytes 884744 | tf_op jit(solution)/shard_map/ppermute | solution.py:22
  45.2 4.2 %collective-permute-start.2 = (s16[4,72,512]{2,1,0:T(8,128)(2,1)S(1)}, s16[4,72,512]{2,1,0:T(8,128)(2,1)S(1)}, u32[]{:S(2)}, u32[]{:S(2)}) collective-permute-start(s16[4,72,512]{2,1,0:T(8,128)(2,1)S(1)} %get-tuple-element.28), channel_id=1, source_target_pairs={{0,15},{1,0},{2,1},{3,2},{4,3},{5,4},{6,5},{7,6},{8,7},{9,8},{10,9... | collective-permute-start | bytes 884744 | tf_op jit(solution)/shard_map/ppermute | solution.py:22
  49.4 2.1 %collective-permute-start.3 = (s16[2,72,512]{2,1,0:T(8,128)(2,1)S(1)}, s16[2,72,512]{2,1,0:T(8,128)(2,1)S(1)}, u32[]{:S(2)}, u32[]{:S(2)}) collective-permute-start(s16[2,72,512]{2,1,0:T(8,128)(2,1)S(1)} %get-tuple-element.29), channel_id=1, source_target_pairs={{0,2},{1,3},{2,4},{3,5},{4,6},{5,7},{6,8},{7,9},{8,10},{9,11},{10,... | collective-permute-start | bytes 442376 | tf_op jit(solution)/shard_map/ppermute | solution.py:22
  51.5 5.8 %collective-permute-start.4 = (s16[2,72,512]{2,1,0:T(8,128)(2,1)S(1)}, s16[2,72,512]{2,1,0:T(8,128)(2,1)S(1)}, u32[]{:S(2)}, u32[]{:S(2)}) collective-permute-start(s16[2,72,512]{2,1,0:T(8,128)(2,1)S(1)} %get-tuple-element.30), channel_id=1, source_target_pairs={{0,14},{1,15},{2,0},{3,1},{4,2},{5,3},{6,4},{7,5},{8,6},{9,7},{10,... | collective-permute-start | bytes 442376 | tf_op jit(solution)/shard_map/ppermute | solution.py:22
  57.4 2.4 %collective-permute-done.3.up = s16[2,72,512]{2,1,0:T(8,128)(2,1)S(1)} collective-permute-done((s16[2,72,512]{2,1,0:T(8,128)(2,1)S(1)}, s16[2,72,512]{2,1,0:T(8,128)(2,1)S(1)}, u32[]{:S(2)}, u32[]{:S(2)}) %collective-permute-start.3) | collective-permute-done | bytes 147488 | tf_op jit(solution)/shard_map/ppermute | solution.py:22
  59.8 2.0 %collective-permute-done.4.down = s16[2,72,512]{2,1,0:T(8,128)(2,1)S(1)} collective-permute-done((s16[2,72,512]{2,1,0:T(8,128)(2,1)S(1)}, s16[2,72,512]{2,1,0:T(8,128)(2,1)S(1)}, u32[]{:S(2)}, u32[]{:S(2)}) %collective-permute-start.4) | collective-permute-done | bytes 147488 | tf_op jit(solution)/shard_map/ppermute | solution.py:22
  61.8 1.1 shard_map.105
  62.9 6.6 %all-to-all-start.1 = ((s16[4,72,512]{2,1,0:T(8,128)(2,1)}), s16[4,72,512]{2,1,0:T(8,128)(2,1)S(1)}, u32[]{:S(2)}, u32[]{:S(2)}) async-start(s16[4,72,512]{2,1,0:T(8,128)(2,1)} %shard_map.105), calls=%async_computation.1 | async-start | bytes 589824 | tf_op jit(solution)/shard_map/all_to_all | solution.py:230
  69.6 0.1 pad_maximum_fusion
  69.6 4.0 %collective-permute-start.9 = (bf16[2,512,256]{2,1,0:T(8,128)(2,1)S(1)}, bf16[2,512,256]{2,1,0:T(8,128)(2,1)S(1)}, u32[]{:S(2)}, u32[]{:S(2)}) collective-permute-start(bf16[2,512,256]{2,1,0:T(8,128)(2,1)S(1)} %pad_maximum_fusion), channel_id=1, source_target_pairs={{0,16},{16,0},{1,17},{17,1},{2,18},{18,2},{3,19},{19,3},{4,20},{20... | collective-permute-start | bytes 1572872 | tf_op jit(solution)/shard_map/ppermute | solution.py:26
  73.7 2.2 %collective-permute-start.5 = (bf16[4,2,32,512]{3,2,1,0:T(8,128)(2,1)S(1)}, bf16[4,2,32,512]{3,2,1,0:T(8,128)(2,1)S(1)}, u32[]{:S(2)}, u32[]{:S(2)}) collective-permute-start(bf16[4,2,32,512]{3,2,1,0:T(8,128)(2,1)S(1)} %bitcast.12), channel_id=1, source_target_pairs={{0,1},{1,2},{2,3},{3,4},{4,5},{5,6},{6,7},{7,8},{8,9},{9,10},{10,1... | collective-permute-start | bytes 786440 | tf_op jit(solution)/shard_map/ppermute | solution.py:22
  75.9 6.9 %collective-permute-start.6 = (bf16[4,2,32,512]{3,2,1,0:T(8,128)(2,1)S(1)}, bf16[4,2,32,512]{3,2,1,0:T(8,128)(2,1)S(1)}, u32[]{:S(2)}, u32[]{:S(2)}) collective-permute-start(bf16[4,2,32,512]{3,2,1,0:T(8,128)(2,1)S(1)} %bitcast.13), channel_id=1, source_target_pairs={{0,15},{1,0},{2,1},{3,2},{4,3},{5,4},{6,5},{7,6},{8,7},{9,8},{10,9... | collective-permute-start | bytes 786440 | tf_op jit(solution)/shard_map/ppermute | solution.py:22
  82.8 2.7 %collective-permute-start.7 = (bf16[2,2,32,512]{3,2,1,0:T(8,128)(2,1)S(1)}, bf16[2,2,32,512]{3,2,1,0:T(8,128)(2,1)S(1)}, u32[]{:S(2)}, u32[]{:S(2)}) collective-permute-start(bf16[2,2,32,512]{3,2,1,0:T(8,128)(2,1)S(1)} %get-tuple-element.47), channel_id=1, source_target_pairs={{0,2},{1,3},{2,4},{3,5},{4,6},{5,7},{6,8},{7,9},{8,10},{9,11},{10,... | collective-permute-start | bytes 393224 | tf_op jit(solution)/shard_map/ppermute | solution.py:22
  85.6 5.5 %collective-permute-start.8 = (bf16[2,2,32,512]{3,2,1,0:T(8,128)(2,1)S(1)}, bf16[2,2,32,512]{3,2,1,0:T(8,128)(2,1)S(1)}, u32[]{:S(2)}, u32[]{:S(2)}) collective-permute-start(bf16[2,2,32,512]{3,2,1,0:T(8,128)(2,1)S(1)} %get-tuple-element.46), channel_id=1, source_target_pairs={{0,14},{1,15},{2,0},{3,1},{4,2},{5,3},{6,4},{7,5},{8,6},{9,7},{10,... | collective-permute-start | bytes 393224 | tf_op jit(solution)/shard_map/ppermute | solution.py:22
  91.1 4.2 %collective-permute-done.7.up = bf16[2,2,32,512]{3,2,1,0:T(8,128)(2,1)S(1)} collective-permute-done((bf16[2,2,32,512]{3,2,1,0:T(8,128)(2,1)S(1)}, bf16[2,2,32,512]{3,2,1,0:T(8,128)(2,1)S(1)}, u32[]{:S(2)}, u32[]{:S(2)}) %collective-permute-start.7) | collective-permute-done | bytes 131104 | tf_op jit(solution)/shard_map/ppermute | solution.py:22
  95.2 0.2 collective-permute-done.8.down
  95.4 0.0 collective-permute-done.9.other
  95.4 2.5 %shard_map.107 = s16[16,72,512]{2,1,0:T(8,128)(2,1)} custom-call(s32[8]{0:T(128)S(1)} %pad_add_fusion.where, bf16[4,2,32,512]{3,2,1,0:T(8,128)(2,1)S(1)} %bitcast.15, bf16[4,2,32,512]{3,2,1,0:T(8,128)(2,1)S(1)} %collective-permute-done.5.x1, bf16[4,2,32,512]{3,2,1,0:T(8,128)(2,1)S(1)} %collective-permute-done.6.x3, ...), custom_call_target="tpu_custom_call" | custom-call | flops 536870912 | bytes 3276832 | tf_op jit(solution)/shard_map/pallas_call | solution.py:37
  97.9 0.2 shard_map.106
  98.1 5.7 %all-to-all-start.2 = ((s16[16,72,512]{2,1,0:T(8,128)(2,1)}), s16[16,72,512]{2,1,0:T(8,128)(2,1)S(1)}, u32[]{:S(2)}, u32[]{:S(2)}) async-start(s16[16,72,512]{2,1,0:T(8,128)(2,1)} %shard_map.107), calls=%async_computation.2 | async-start | bytes 2359296 | tf_op jit(solution)/shard_map/all_to_all | solution.py:240
  103.9 33.2 %all_gather.7.rest_0_ = s16[8,72,512]{2,1,0:T(8,128)(2,1)S(1)} all-gather(s16[1,72,512]{2,1,0:T(8,128)(2,1)S(1)} %shard_map.106), channel_id=1, replica_groups=mesh['xl'=2,'y'=4,'c'=2,'xh'=2,'zh'=4,'zm'=2,'zl'=2] {'zh','zm'}, dimensions={0}, use_global_device_ids=true | all-gather | bytes 663552 | tf_op jit(solution)/shard_map/all_gather | solution.py:242
  137.1 3.3 %collective-permute-start.12 = (s16[8,72,512]{2,1,0:T(8,128)(2,1)S(1)}, s16[8,72,512]{2,1,0:T(8,128)(2,1)S(1)}, u32[]{:S(2)}, u32[]{:S(2)}) collective-permute-start(s16[8,72,512]{2,1,0:T(8,128)(2,1)S(1)} %all_gather.7.rest_0_), channel_id=1, source_target_pairs={{0,16},{16,0},{1,17},{17,1},{2,18},{18,2},{3,19},{19,3},{4,20},{20... | collective-permute-start | bytes 1769480 | tf_op jit(solution)/shard_map/ppermute | solution.py:26
  140.4 2.1 %shard_map.108 = s16[2,16,72,256]{3,2,1,0:T(8,128)(2,1)} custom-call(s32[8]{0:T(128)S(1)} %pad_add_fusion.where, s16[16,72,512]{2,1,0:T(8,128)(2,1)S(1)} %all-to-all-done.2.w), custom_call_target="tpu_custom_call" | custom-call | bytes 2359328 | tf_op jit(solution)/shard_map/pallas_call | solution.py:37
  142.5 6.9 %all-to-all-start.3 = ((s16[32,72,256]{2,1,0:T(8,128)(2,1)}), s16[32,72,256]{2,1,0:T(8,128)(2,1)S(1)}, u32[]{:S(2)}, u32[]{:S(2)}) async-start(s16[32,72,256]{2,1,0:T(8,128)(2,1)} %bitcast.11), calls=%async_computation.3 | async-start | bytes 2359296 | tf_op jit(solution)/shard_map/all_to_all | solution.py:250
  149.4 2.6 %collective-permute-done.12.rest_3_ = s16[8,72,512]{2,1,0:T(8,128)(2,1)S(1)} collective-permute-done((s16[8,72,512]{2,1,0:T(8,128)(2,1)S(1)}, s16[8,72,512]{2,1,0:T(8,128)(2,1)S(1)}, u32[]{:S(2)}, u32[]{:S(2)}) %collective-permute-start.12) | collective-permute-done | bytes 589856 | tf_op jit(solution)/shard_map/ppermute | solution.py:26
  152.0 0.9 fusion
  152.9 4.0 %collective-permute-start.13 = (s16[4,72,512]{2,1,0:T(8,128)(2,1)}, s16[4,72,512]{2,1,0:T(8,128)(2,1)S(1)}, u32[]{:S(2)}, u32[]{:S(2)}) collective-permute-start(s16[4,72,512]{2,1,0:T(8,128)(2,1)} %get-tuple-element.43), channel_id=1, source_target_pairs={{0,1},{1,2},{2,3},{3,4},{4,5},{5,6},{6,7},{7,8},{8,9},{9,10},{10,1... | collective-permute-start | bytes 884744 | tf_op jit(solution)/shard_map/ppermute | solution.py:22
  156.9 3.0 %collective-permute-start.14 = (s16[4,72,512]{2,1,0:T(8,128)(2,1)}, s16[4,72,512]{2,1,0:T(8,128)(2,1)S(1)}, u32[]{:S(2)}, u32[]{:S(2)}) collective-permute-start(s16[4,72,512]{2,1,0:T(8,128)(2,1)} %get-tuple-element.42), channel_id=1, source_target_pairs={{0,15},{1,0},{2,1},{3,2},{4,3},{5,4},{6,5},{7,6},{8,7},{9,8},{10,9... | collective-permute-start | bytes 884744 | tf_op jit(solution)/shard_map/ppermute | solution.py:22
  159.9 0.9 fusion.1
  160.8 2.8 %collective-permute-start.10 = (s16[4,72,512]{2,1,0:T(8,128)(2,1)}, s16[4,72,512]{2,1,0:T(8,128)(2,1)S(1)}, u32[]{:S(2)}, u32[]{:S(2)}) collective-permute-start(s16[4,72,512]{2,1,0:T(8,128)(2,1)} %get-tuple-element.45), channel_id=1, source_target_pairs={{0,1},{1,2},{2,3},{3,4},{4,5},{5,6},{6,7},{7,8},{8,9},{9,10},{10,1... | collective-permute-start | bytes 884744 | tf_op jit(solution)/shard_map/ppermute | solution.py:22
  163.6 4.2 %collective-permute-start.11 = (s16[4,72,512]{2,1,0:T(8,128)(2,1)}, s16[4,72,512]{2,1,0:T(8,128)(2,1)S(1)}, u32[]{:S(2)}, u32[]{:S(2)}) collective-permute-start(s16[4,72,512]{2,1,0:T(8,128)(2,1)} %get-tuple-element.44), channel_id=1, source_target_pairs={{0,15},{1,0},{2,1},{3,2},{4,3},{5,4},{6,5},{7,6},{8,7},{9,8},{10,9... | collective-permute-start | bytes 884744 | tf_op jit(solution)/shard_map/ppermute | solution.py:22
  167.8 0.7 shard_map.109
  168.6 2.2 %collective-permute-done.10.rest_1_ = s16[4,72,512]{2,1,0:T(8,128)(2,1)S(1)} collective-permute-done((s16[4,72,512]{2,1,0:T(8,128)(2,1)}, s16[4,72,512]{2,1,0:T(8,128)(2,1)S(1)}, u32[]{:S(2)}, u32[]{:S(2)}) %collective-permute-start.10) | collective-permute-done | bytes 294944 | tf_op jit(solution)/shard_map/ppermute | solution.py:22
  170.8 1.6 collective-permute-done.11.rest_2_
  172.4 6.7 %shard_map.110 = (f32[512,256]{1,0:T(8,128)}, f32[512,256]{1,0:T(8,128)}) custom-call(s32[8]{0:T(128)S(1)} %pad_add_fusion.where, bf16[2,256,1024]{2,1,0:T(8,128)(2,1)S(1)} %get-tuple-element.39.act_high, bf16[2,256,1024]{2,1,0:T(8,128)(2,1)S(1)} %get-tuple-element.40.act_low, s16[8,72,512]{2,1,0:T(8,128)(2,1)S(1)} %all_gather.7.rest_0_, ...), custom_call_target="tpu_custom_call" | custom-call | flops 2818572288 | bytes 5505056 | tf_op jit(solution)/shard_map/pallas_call | solution.py:37
  (23 shorter events, 0.1 us)
Async XLA Ops:
  2.5 9.8 %copy-start.2 = (bf16[256,512]{1,0:T(8,128)(2,1)S(1)}, bf16[256,512]{1,0:T(8,128)(2,1)}, u32[]{:S(2)}) copy-start(bf16[256,512]{1,0:T(8,128)(2,1)} %qb.1) | copy-start | bytes 786436
  2.5 9.8 %copy-start.3 = (bf16[256,512]{1,0:T(8,128)(2,1)S(1)}, bf16[256,512]{1,0:T(8,128)(2,1)}, u32[]{:S(2)}) copy-start(bf16[256,512]{1,0:T(8,128)(2,1)} %ob.1) | copy-start | bytes 786436
  2.5 13.1 %copy-start.4 = (bf16[32,512]{1,0:T(8,128)(2,1)S(1)}, bf16[32,512]{1,0:T(8,128)(2,1)}, u32[]{:S(2)}) copy-start(bf16[32,512]{1,0:T(8,128)(2,1)} %param.14) | copy-start | bytes 98308
  2.5 13.1 %copy-start.5 = (bf16[32,512]{1,0:T(8,128)(2,1)S(1)}, bf16[32,512]{1,0:T(8,128)(2,1)}, u32[]{:S(2)}) copy-start(bf16[32,512]{1,0:T(8,128)(2,1)} %param.10) | copy-start | bytes 98308
  2.5 38.2 %copy-start.6 = (s32[1024]{0:T(1024)S(1)}, s32[1024]{0:T(1024)}, u32[]{:S(2)}) copy-start(s32[1024]{0:T(1024)} %param.9) | copy-start | bytes 12292
  2.5 38.4 %all-to-all-start = ((bf16[32,64,256]{2,1,0:T(8,128)(2,1)}), bf16[32,64,256]{2,1,0:T(8,128)(2,1)S(1)}, u32[]{:S(2)}, u32[]{:S(2)}) async-start(bf16[32,64,256]{2,1,0:T(8,128)(2,1)} %bitcast.4), calls=%async_computation | async-start | bytes 2097152 | tf_op jit(solution)/shard_map/all_to_all | solution.py:211
  12.3 28.6 %collective-permute-start = (bf16[256,512]{1,0:T(8,128)(2,1)S(1)}, bf16[256,512]{1,0:T(8,128)(2,1)S(1)}, u32[]{:S(2)}, u32[]{:S(2)}) collective-permute-start(bf16[256,512]{1,0:T(8,128)(2,1)S(1)} %broadcast_select_fusion), channel_id=1, source_target_pairs={{0,16},{16,0},{1,17},{17,1},{2,18},{18,2},{3,19},{19,3},{4,20},{20... | collective-permute-start | bytes 786440 | tf_op jit(solution)/shard_map/ppermute | solution.py:26
  42.2 27.4 %copy-start = (bf16[512,256]{1,0:T(8,128)(2,1)S(1)}, bf16[512,256]{1,0:T(8,128)(2,1)}, u32[]{:S(2)}) copy-start(bf16[512,256]{1,0:T(8,128)(2,1)} %qa) | copy-start | bytes 786436
  42.2 27.4 %copy-start.1 = (bf16[512,256]{1,0:T(8,128)(2,1)S(1)}, bf16[512,256]{1,0:T(8,128)(2,1)}, u32[]{:S(2)}) copy-start(bf16[512,256]{1,0:T(8,128)(2,1)} %oa) | copy-start | bytes 786436
  42.2 19.6 %collective-permute-start.1 = (s16[4,72,512]{2,1,0:T(8,128)(2,1)S(1)}, s16[4,72,512]{2,1,0:T(8,128)(2,1)S(1)}, u32[]{:S(2)}, u32[]{:S(2)}) collective-permute-start(s16[4,72,512]{2,1,0:T(8,128)(2,1)S(1)} %get-tuple-element.27), channel_id=1, source_target_pairs={{0,1},{1,2},{2,3},{3,4},{4,5},{5,6},{6,7},{7,8},{8,9},{9,10},{10,1... | collective-permute-start | bytes 884744 | tf_op jit(solution)/shard_map/ppermute | solution.py:22
  45.2 16.6 %collective-permute-start.2 = (s16[4,72,512]{2,1,0:T(8,128)(2,1)S(1)}, s16[4,72,512]{2,1,0:T(8,128)(2,1)S(1)}, u32[]{:S(2)}, u32[]{:S(2)}) collective-permute-start(s16[4,72,512]{2,1,0:T(8,128)(2,1)S(1)} %get-tuple-element.28), channel_id=1, source_target_pairs={{0,15},{1,0},{2,1},{3,2},{4,3},{5,4},{6,5},{7,6},{8,7},{9,8},{10,9... | collective-permute-start | bytes 884744 | tf_op jit(solution)/shard_map/ppermute | solution.py:22
  49.4 10.4 %collective-permute-start.3 = (s16[2,72,512]{2,1,0:T(8,128)(2,1)S(1)}, s16[2,72,512]{2,1,0:T(8,128)(2,1)S(1)}, u32[]{:S(2)}, u32[]{:S(2)}) collective-permute-start(s16[2,72,512]{2,1,0:T(8,128)(2,1)S(1)} %get-tuple-element.29), channel_id=1, source_target_pairs={{0,2},{1,3},{2,4},{3,5},{4,6},{5,7},{6,8},{7,9},{8,10},{9,11},{10,... | collective-permute-start | bytes 442376 | tf_op jit(solution)/shard_map/ppermute | solution.py:22
  51.5 10.3 %collective-permute-start.4 = (s16[2,72,512]{2,1,0:T(8,128)(2,1)S(1)}, s16[2,72,512]{2,1,0:T(8,128)(2,1)S(1)}, u32[]{:S(2)}, u32[]{:S(2)}) collective-permute-start(s16[2,72,512]{2,1,0:T(8,128)(2,1)S(1)} %get-tuple-element.30), channel_id=1, source_target_pairs={{0,14},{1,15},{2,0},{3,1},{4,2},{5,3},{6,4},{7,5},{8,6},{9,7},{10,... | collective-permute-start | bytes 442376 | tf_op jit(solution)/shard_map/ppermute | solution.py:22
  62.9 35.0 %all-to-all-start.1 = ((s16[4,72,512]{2,1,0:T(8,128)(2,1)}), s16[4,72,512]{2,1,0:T(8,128)(2,1)S(1)}, u32[]{:S(2)}, u32[]{:S(2)}) async-start(s16[4,72,512]{2,1,0:T(8,128)(2,1)} %shard_map.105), calls=%async_computation.1 | async-start | bytes 589824 | tf_op jit(solution)/shard_map/all_to_all | solution.py:230
  69.6 25.8 %collective-permute-start.9 = (bf16[2,512,256]{2,1,0:T(8,128)(2,1)S(1)}, bf16[2,512,256]{2,1,0:T(8,128)(2,1)S(1)}, u32[]{:S(2)}, u32[]{:S(2)}) collective-permute-start(bf16[2,512,256]{2,1,0:T(8,128)(2,1)S(1)} %pad_maximum_fusion), channel_id=1, source_target_pairs={{0,16},{16,0},{1,17},{17,1},{2,18},{18,2},{3,19},{19,3},{4,20},{20... | collective-permute-start | bytes 1572872 | tf_op jit(solution)/shard_map/ppermute | solution.py:26
  73.7 21.8 %collective-permute-start.5 = (bf16[4,2,32,512]{3,2,1,0:T(8,128)(2,1)S(1)}, bf16[4,2,32,512]{3,2,1,0:T(8,128)(2,1)S(1)}, u32[]{:S(2)}, u32[]{:S(2)}) collective-permute-start(bf16[4,2,32,512]{3,2,1,0:T(8,128)(2,1)S(1)} %bitcast.12), channel_id=1, source_target_pairs={{0,1},{1,2},{2,3},{3,4},{4,5},{5,6},{6,7},{7,8},{8,9},{9,10},{10,1... | collective-permute-start | bytes 786440 | tf_op jit(solution)/shard_map/ppermute | solution.py:22
  75.9 19.6 %collective-permute-start.6 = (bf16[4,2,32,512]{3,2,1,0:T(8,128)(2,1)S(1)}, bf16[4,2,32,512]{3,2,1,0:T(8,128)(2,1)S(1)}, u32[]{:S(2)}, u32[]{:S(2)}) collective-permute-start(bf16[4,2,32,512]{3,2,1,0:T(8,128)(2,1)S(1)} %bitcast.13), channel_id=1, source_target_pairs={{0,15},{1,0},{2,1},{3,2},{4,3},{5,4},{6,5},{7,6},{8,7},{9,8},{10,9... | collective-permute-start | bytes 786440 | tf_op jit(solution)/shard_map/ppermute | solution.py:22
  82.8 12.4 %collective-permute-start.7 = (bf16[2,2,32,512]{3,2,1,0:T(8,128)(2,1)S(1)}, bf16[2,2,32,512]{3,2,1,0:T(8,128)(2,1)S(1)}, u32[]{:S(2)}, u32[]{:S(2)}) collective-permute-start(bf16[2,2,32,512]{3,2,1,0:T(8,128)(2,1)S(1)} %get-tuple-element.47), channel_id=1, source_target_pairs={{0,2},{1,3},{2,4},{3,5},{4,6},{5,7},{6,8},{7,9},{8,10},{9,11},{10,... | collective-permute-start | bytes 393224 | tf_op jit(solution)/shard_map/ppermute | solution.py:22
  85.6 9.9 %collective-permute-start.8 = (bf16[2,2,32,512]{3,2,1,0:T(8,128)(2,1)S(1)}, bf16[2,2,32,512]{3,2,1,0:T(8,128)(2,1)S(1)}, u32[]{:S(2)}, u32[]{:S(2)}) collective-permute-start(bf16[2,2,32,512]{3,2,1,0:T(8,128)(2,1)S(1)} %get-tuple-element.46), channel_id=1, source_target_pairs={{0,14},{1,15},{2,0},{3,1},{4,2},{5,3},{6,4},{7,5},{8,6},{9,7},{10,... | collective-permute-start | bytes 393224 | tf_op jit(solution)/shard_map/ppermute | solution.py:22
  98.1 42.2 %all-to-all-start.2 = ((s16[16,72,512]{2,1,0:T(8,128)(2,1)}), s16[16,72,512]{2,1,0:T(8,128)(2,1)S(1)}, u32[]{:S(2)}, u32[]{:S(2)}) async-start(s16[16,72,512]{2,1,0:T(8,128)(2,1)} %shard_map.107), calls=%async_computation.2 | async-start | bytes 2359296 | tf_op jit(solution)/shard_map/all_to_all | solution.py:240
  137.1 14.9 %collective-permute-start.12 = (s16[8,72,512]{2,1,0:T(8,128)(2,1)S(1)}, s16[8,72,512]{2,1,0:T(8,128)(2,1)S(1)}, u32[]{:S(2)}, u32[]{:S(2)}) collective-permute-start(s16[8,72,512]{2,1,0:T(8,128)(2,1)S(1)} %all_gather.7.rest_0_), channel_id=1, source_target_pairs={{0,16},{16,0},{1,17},{17,1},{2,18},{18,2},{3,19},{19,3},{4,20},{20... | collective-permute-start | bytes 1769480 | tf_op jit(solution)/shard_map/ppermute | solution.py:26
  142.5 25.4 %all-to-all-start.3 = ((s16[32,72,256]{2,1,0:T(8,128)(2,1)}), s16[32,72,256]{2,1,0:T(8,128)(2,1)S(1)}, u32[]{:S(2)}, u32[]{:S(2)}) async-start(s16[32,72,256]{2,1,0:T(8,128)(2,1)} %bitcast.11), calls=%async_computation.3 | async-start | bytes 2359296 | tf_op jit(solution)/shard_map/all_to_all | solution.py:250
  152.9 15.7 %collective-permute-start.13 = (s16[4,72,512]{2,1,0:T(8,128)(2,1)}, s16[4,72,512]{2,1,0:T(8,128)(2,1)S(1)}, u32[]{:S(2)}, u32[]{:S(2)}) collective-permute-start(s16[4,72,512]{2,1,0:T(8,128)(2,1)} %get-tuple-element.43), channel_id=1, source_target_pairs={{0,1},{1,2},{2,3},{3,4},{4,5},{5,6},{6,7},{7,8},{8,9},{9,10},{10,1... | collective-permute-start | bytes 884744 | tf_op jit(solution)/shard_map/ppermute | solution.py:22
  156.9 11.7 %collective-permute-start.14 = (s16[4,72,512]{2,1,0:T(8,128)(2,1)}, s16[4,72,512]{2,1,0:T(8,128)(2,1)S(1)}, u32[]{:S(2)}, u32[]{:S(2)}) collective-permute-start(s16[4,72,512]{2,1,0:T(8,128)(2,1)} %get-tuple-element.42), channel_id=1, source_target_pairs={{0,15},{1,0},{2,1},{3,2},{4,3},{5,4},{6,5},{7,6},{8,7},{9,8},{10,9... | collective-permute-start | bytes 884744 | tf_op jit(solution)/shard_map/ppermute | solution.py:22
  160.8 10.0 %collective-permute-start.10 = (s16[4,72,512]{2,1,0:T(8,128)(2,1)}, s16[4,72,512]{2,1,0:T(8,128)(2,1)S(1)}, u32[]{:S(2)}, u32[]{:S(2)}) collective-permute-start(s16[4,72,512]{2,1,0:T(8,128)(2,1)} %get-tuple-element.45), channel_id=1, source_target_pairs={{0,1},{1,2},{2,3},{3,4},{4,5},{5,6},{6,7},{7,8},{8,9},{9,10},{10,1... | collective-permute-start | bytes 884744 | tf_op jit(solution)/shard_map/ppermute | solution.py:22
  163.6 8.8 %collective-permute-start.11 = (s16[4,72,512]{2,1,0:T(8,128)(2,1)}, s16[4,72,512]{2,1,0:T(8,128)(2,1)S(1)}, u32[]{:S(2)}, u32[]{:S(2)}) collective-permute-start(s16[4,72,512]{2,1,0:T(8,128)(2,1)} %get-tuple-element.44), channel_id=1, source_target_pairs={{0,15},{1,0},{2,1},{3,2},{4,3},{5,4},{6,5},{7,6},{8,7},{9,8},{10,9... | collective-permute-start | bytes 884744 | tf_op jit(solution)/shard_map/ppermute | solution.py:22

commit v5 on v4

--- a/solution.py
+++ b/solution.py
@@ -155,13 +155,15 @@
 
 
 def correct_kernel(where, act_high, act_low, *rest):
-    grads, (q_out, o_out, high, low, acc, total) = rest[:6], rest[6:]
+    grads, (q_out, o_out, high, low, acc, total) = rest[:5], rest[5:]
     zl, xh = lax.rem(where[0], 2), where[1]
     for side in range(2):
         half = xh if side == 0 else 1 - xh
-        level, first_w, last_w = grads[3 * side:3 * side + 3]
         for k in range(16):
-            w = level[k] if k < 8 else (first_w[k - 8] if k < 12 else last_w[k - 12])
+            if side == 0:
+                w = grads[k // 8][k % 8]
+            else:
+                w = grads[2][k] if k < 8 else grads[3 + (k - 8) // 4][k % 4]
             block = 2 * (k % 8) + (zl if k < 8 else 1 - zl)
             at = pl.multiple_of(64 * block, 64)
             [x] = opened(w, 64)
@@ -220,7 +222,8 @@
         flops=2 * 2 * 512 * 512 * 512,
     )
     *sends, qa, oa, level = lax.optimization_barrier((*sends, qa, oa, level))
-    sends = [shift(w, by) for w, by in zip(sends, (1, -1, 2, -2))]
+    ups = [shift(w, by) for w, by in zip(sends[2:], (2, -2))]
+    sends = [shift(w, by) for w, by in zip(sends[:2], (1, -1))] + ups
     act_other = swap_half(jnp.stack([qa, oa]))
     [words] = whole(near_sum_kernel, [shape(4, 72, 512)], [keep] + sends, scalars=0)
     words, level = lax.optimization_barrier((words, level))
@@ -242,7 +245,8 @@
     words = lax.all_gather(words, Z8, axis=0, tiled=True)
     other = swap_half(words)
     words, act_words = lax.optimization_barrier((words, act_words))
-    mine = [words, shift(words[:4], 1), shift(words[4:], -1)]
+    words, other = lax.optimization_barrier((words, other))
+    mine = [words, lax.ppermute(words, "zl", [(0, 1), (1, 0)])]
     others = [other, shift(other[:4], 1), shift(other[4:], -1)]
 
     [act_words] = whole(act_sum_kernel, [shape(2, 16, 72, 256)], [where, act_words])

time: 181 us -> 181 us (level)
  waiting for transfers between devices: 15.3 us -> 19.7 us
  starting transfers between devices: 86.2 us -> 83.2 us
    ppermute x12 -> x10, starting transfers between devices: 46.5 us -> 39.5 us  [shift(): return lax.ppermute(x, Z, [(i, (i + by) % NZ) for i in range(NZ)])]
    ppermute x0 -> x1, starting transfers between devices: none -> 4.03 us  [per_device(): mine = [words, lax.ppermute(words, 'zl', [(0, 1), (1, 0)])]]
    ppermute x12 -> x10, waiting for transfers between devices: 12.7 us -> 15.6 us  [shift(): return lax.ppermute(x, Z, [(i, (i + by) % NZ) for i in range(NZ)])]
  transfers between devices with their start and end apart: 19 -> 18, of which waited for: 7 -> 8; matrix products, arithmetic and copies ran while one was open for 1% -> 1% of each run, Pallas kernels for 3% -> 3%
where the time goes in v5:
time: 181 us; the launch traced here: 180 us
  starting transfers between devices  83.2 us (46%)
  blocking collectives  58.3 us (32%)
  waiting for transfers between devices  19.7 us (11%)
  Pallas kernels  14.5 us (8%)
  local copies, waits for them, and re-layouts  2.02 us (1%)
    ppermute x10, starting transfers between devices, shift(): return lax.ppermute(x, Z, [(i, (i + by) % NZ) for i in range(NZ)])  39.5 us
    all_gather x1, blocking collectives, per_device(): words = lax.all_gather(words, Z8, axis=0, tiled=True)  33.2 us
    all_gather x1, blocking collectives, per_device(): level = lax.all_gather(jnp.stack([qx, ox])[None], ZH, axis=0, tiled=True)  25.1 us
    ppermute x10, waiting for transfers between devices, shift(): return lax.ppermute(x, Z, [(i, (i + by) % NZ) for i in range(NZ)])  15.6 us
    pallas_call x7, Pallas kernels, whole(): pl.pallas_call(kernel, out_shape=outs, in_specs=specs, out_specs=[pl.Bloc...  14.5 us
    ppermute x3, starting transfers between devices, swap_half(): return lax.ppermute(x, 'xh', [(0, 1), (1, 0)])  10.6 us
    all_to_all x1, starting transfers between devices, per_device(): got = lax.all_to_all(sent, PLANE, split_axis=0, concat_axis=0, tiled=True)  9.73 us
    all_to_all x1, starting transfers between devices, per_device(): lax.all_to_all(act_words, PLANE, split_axis=0, concat_axis=0, tiled=True)  6.92 us
  transfers between devices with their start and end apart: 18, of which 8 were waited for; matrix products, arithmetic and copies ran while one was open for 1% of the time, Pallas kernels for 3%

profile of v5, /device:TPU:6, one launch (start us, length us, event | category | flops | bytes accessed | tf_op | source)
XLA Modules:
  0.0 179.7 jit_solution(18282564942583605535)
XLA Ops:
  0.6 0.8 pad_maximum_fusion.1
  1.4 1.1 broadcast_in_dim.4
  2.5 0.0 copy-start.6
  2.5 9.7 %all-to-all-start = ((bf16[32,64,256]{2,1,0:T(8,128)(2,1)}), bf16[32,64,256]{2,1,0:T(8,128)(2,1)S(1)}, u32[]{:S(2)}, u32[]{:S(2)}) async-start(bf16[32,64,256]{2,1,0:T(8,128)(2,1)} %bitcast.4), calls=%async_computation | async-start | bytes 2097152 | tf_op jit(solution)/shard_map/all_to_all | solution.py:213
  12.4 3.3 %collective-permute-start = (bf16[256,512]{1,0:T(8,128)(2,1)S(1)}, bf16[256,512]{1,0:T(8,128)(2,1)S(1)}, u32[]{:S(2)}, u32[]{:S(2)}) collective-permute-start(bf16[256,512]{1,0:T(8,128)(2,1)S(1)} %broadcast_select_fusion), channel_id=1, source_target_pairs={{0,16},{16,0},{1,17},{17,1},{2,18},{18,2},{3,19},{19,3},{4,20},{20... | collective-permute-start | bytes 786440 | tf_op jit(solution)/shard_map/ppermute | solution.py:26
  15.7 25.1 %all-gather = bf16[8,32,512]{2,1,0:T(8,128)(2,1)S(1)} all-gather(bf16[2,32,512]{2,1,0:T(8,128)(2,1)S(1)} %pad_maximum_fusion.2), channel_id=2, replica_groups=mesh['xl'=2,'y'=4,'c'=2,'xh'=2,'zh'=4,'zm'=2,'zl'=2] {'zh'}, dimensions={0}, use_global_device_ids=true | all-gather | bytes 327680 | tf_op jit(solution)/shard_map/all_gather | solution.py:216
  40.7 0.1 convert_reduce_fusion
  40.8 0.1 pad_add_fusion.where
  40.9 1.3 shard_map.104
  42.2 0.0 copy-start
  42.2 0.0 copy-start.1
  42.2 3.0 %collective-permute-start.1 = (s16[4,72,512]{2,1,0:T(8,128)(2,1)S(1)}, s16[4,72,512]{2,1,0:T(8,128)(2,1)S(1)}, u32[]{:S(2)}, u32[]{:S(2)}) collective-permute-start(s16[4,72,512]{2,1,0:T(8,128)(2,1)S(1)} %get-tuple-element.29), channel_id=1, source_target_pairs={{0,1},{1,2},{2,3},{3,4},{4,5},{5,6},{6,7},{7,8},{8,9},{9,10},{10,1... | collective-permute-start | bytes 884744 | tf_op jit(solution)/shard_map/ppermute | solution.py:22
  45.2 4.2 %collective-permute-start.2 = (s16[4,72,512]{2,1,0:T(8,128)(2,1)S(1)}, s16[4,72,512]{2,1,0:T(8,128)(2,1)S(1)}, u32[]{:S(2)}, u32[]{:S(2)}) collective-permute-start(s16[4,72,512]{2,1,0:T(8,128)(2,1)S(1)} %get-tuple-element.30), channel_id=1, source_target_pairs={{0,15},{1,0},{2,1},{3,2},{4,3},{5,4},{6,5},{7,6},{8,7},{9,8},{10,9... | collective-permute-start | bytes 884744 | tf_op jit(solution)/shard_map/ppermute | solution.py:22
  49.4 2.1 %collective-permute-start.3 = (s16[2,72,512]{2,1,0:T(8,128)(2,1)S(1)}, s16[2,72,512]{2,1,0:T(8,128)(2,1)S(1)}, u32[]{:S(2)}, u32[]{:S(2)}) collective-permute-start(s16[2,72,512]{2,1,0:T(8,128)(2,1)S(1)} %get-tuple-element.31), channel_id=1, source_target_pairs={{0,2},{1,3},{2,4},{3,5},{4,6},{5,7},{6,8},{7,9},{8,10},{9,11},{10,... | collective-permute-start | bytes 442376 | tf_op jit(solution)/shard_map/ppermute | solution.py:22
  51.6 5.8 %collective-permute-start.4 = (s16[2,72,512]{2,1,0:T(8,128)(2,1)S(1)}, s16[2,72,512]{2,1,0:T(8,128)(2,1)S(1)}, u32[]{:S(2)}, u32[]{:S(2)}) collective-permute-start(s16[2,72,512]{2,1,0:T(8,128)(2,1)S(1)} %get-tuple-element.32), channel_id=1, source_target_pairs={{0,14},{1,15},{2,0},{3,1},{4,2},{5,3},{6,4},{7,5},{8,6},{9,7},{10,... | collective-permute-start | bytes 442376 | tf_op jit(solution)/shard_map/ppermute | solution.py:22
  57.4 2.4 %collective-permute-done.3.up = s16[2,72,512]{2,1,0:T(8,128)(2,1)S(1)} collective-permute-done((s16[2,72,512]{2,1,0:T(8,128)(2,1)S(1)}, s16[2,72,512]{2,1,0:T(8,128)(2,1)S(1)}, u32[]{:S(2)}, u32[]{:S(2)}) %collective-permute-start.3) | collective-permute-done | bytes 147488 | tf_op jit(solution)/shard_map/ppermute | solution.py:22
  59.8 2.0 %collective-permute-done.4.down = s16[2,72,512]{2,1,0:T(8,128)(2,1)S(1)} collective-permute-done((s16[2,72,512]{2,1,0:T(8,128)(2,1)S(1)}, s16[2,72,512]{2,1,0:T(8,128)(2,1)S(1)}, u32[]{:S(2)}, u32[]{:S(2)}) %collective-permute-start.4) | collective-permute-done | bytes 147488 | tf_op jit(solution)/shard_map/ppermute | solution.py:22
  61.8 0.0 collective-permute-done.1.w1
  61.8 0.0 collective-permute-done.2.w3
  61.8 1.1 shard_map.105
  62.9 6.6 %all-to-all-start.1 = ((s16[4,72,512]{2,1,0:T(8,128)(2,1)}), s16[4,72,512]{2,1,0:T(8,128)(2,1)S(1)}, u32[]{:S(2)}, u32[]{:S(2)}) async-start(s16[4,72,512]{2,1,0:T(8,128)(2,1)} %shard_map.105), calls=%async_computation.1 | async-start | bytes 589824 | tf_op jit(solution)/shard_map/all_to_all | solution.py:233
  69.6 0.1 pad_maximum_fusion
  69.6 4.0 %collective-permute-start.9 = (bf16[2,512,256]{2,1,0:T(8,128)(2,1)S(1)}, bf16[2,512,256]{2,1,0:T(8,128)(2,1)S(1)}, u32[]{:S(2)}, u32[]{:S(2)}) collective-permute-start(bf16[2,512,256]{2,1,0:T(8,128)(2,1)S(1)} %pad_maximum_fusion), channel_id=1, source_target_pairs={{0,16},{16,0},{1,17},{17,1},{2,18},{18,2},{3,19},{19,3},{4,20},{20... | collective-permute-start | bytes 1572872 | tf_op jit(solution)/shard_map/ppermute | solution.py:26
  73.7 2.2 %collective-permute-start.5 = (bf16[4,2,32,512]{3,2,1,0:T(8,128)(2,1)S(1)}, bf16[4,2,32,512]{3,2,1,0:T(8,128)(2,1)S(1)}, u32[]{:S(2)}, u32[]{:S(2)}) collective-permute-start(bf16[4,2,32,512]{3,2,1,0:T(8,128)(2,1)S(1)} %bitcast.12), channel_id=1, source_target_pairs={{0,1},{1,2},{2,3},{3,4},{4,5},{5,6},{6,7},{7,8},{8,9},{9,10},{10,1... | collective-permute-start | bytes 786440 | tf_op jit(solution)/shard_map/ppermute | solution.py:22
  75.9 6.9 %collective-permute-start.6 = (bf16[4,2,32,512]{3,2,1,0:T(8,128)(2,1)S(1)}, bf16[4,2,32,512]{3,2,1,0:T(8,128)(2,1)S(1)}, u32[]{:S(2)}, u32[]{:S(2)}) collective-permute-start(bf16[4,2,32,512]{3,2,1,0:T(8,128)(2,1)S(1)} %bitcast.13), channel_id=1, source_target_pairs={{0,15},{1,0},{2,1},{3,2},{4,3},{5,4},{6,5},{7,6},{8,7},{9,8},{10,9... | collective-permute-start | bytes 786440 | tf_op jit(solution)/shard_map/ppermute | solution.py:22
  82.8 2.7 %collective-permute-start.7 = (bf16[2,2,32,512]{3,2,1,0:T(8,128)(2,1)S(1)}, bf16[2,2,32,512]{3,2,1,0:T(8,128)(2,1)S(1)}, u32[]{:S(2)}, u32[]{:S(2)}) collective-permute-start(bf16[2,2,32,512]{3,2,1,0:T(8,128)(2,1)S(1)} %get-tuple-element.49), channel_id=1, source_target_pairs={{0,2},{1,3},{2,4},{3,5},{4,6},{5,7},{6,8},{7,9},{8,10},{9,11},{10,... | collective-permute-start | bytes 393224 | tf_op jit(solution)/shard_map/ppermute | solution.py:22
  85.6 5.5 %collective-permute-start.8 = (bf16[2,2,32,512]{3,2,1,0:T(8,128)(2,1)S(1)}, bf16[2,2,32,512]{3,2,1,0:T(8,128)(2,1)S(1)}, u32[]{:S(2)}, u32[]{:S(2)}) collective-permute-start(bf16[2,2,32,512]{3,2,1,0:T(8,128)(2,1)S(1)} %get-tuple-element.48), channel_id=1, source_target_pairs={{0,14},{1,15},{2,0},{3,1},{4,2},{5,3},{6,4},{7,5},{8,6},{9,7},{10,... | collective-permute-start | bytes 393224 | tf_op jit(solution)/shard_map/ppermute | solution.py:22
  91.1 4.2 %collective-permute-done.7.up = bf16[2,2,32,512]{3,2,1,0:T(8,128)(2,1)S(1)} collective-permute-done((bf16[2,2,32,512]{3,2,1,0:T(8,128)(2,1)S(1)}, bf16[2,2,32,512]{3,2,1,0:T(8,128)(2,1)S(1)}, u32[]{:S(2)}, u32[]{:S(2)}) %collective-permute-start.7) | collective-permute-done | bytes 131104 | tf_op jit(solution)/shard_map/ppermute | solution.py:22
  95.2 0.2 collective-permute-done.8.down
  95.4 0.0 collective-permute-done.5.x1
  95.4 0.0 collective-permute-done.6.x3
  95.5 2.5 %shard_map.107 = s16[16,72,512]{2,1,0:T(8,128)(2,1)} custom-call(s32[8]{0:T(128)S(1)} %pad_add_fusion.where, bf16[4,2,32,512]{3,2,1,0:T(8,128)(2,1)S(1)} %bitcast.15, bf16[4,2,32,512]{3,2,1,0:T(8,128)(2,1)S(1)} %collective-permute-done.5.x1, bf16[4,2,32,512]{3,2,1,0:T(8,128)(2,1)S(1)} %collective-permute-done.6.x3, ...), custom_call_target="tpu_custom_call" | custom-call | flops 536870912 | bytes 3276832 | tf_op jit(solution)/shard_map/pallas_call | solution.py:37
  97.9 0.2 shard_map.106
  98.1 5.7 %all-to-all-start.2 = ((s16[16,72,512]{2,1,0:T(8,128)(2,1)}), s16[16,72,512]{2,1,0:T(8,128)(2,1)S(1)}, u32[]{:S(2)}, u32[]{:S(2)}) async-start(s16[16,72,512]{2,1,0:T(8,128)(2,1)} %shard_map.107), calls=%async_computation.2 | async-start | bytes 2359296 | tf_op jit(solution)/shard_map/all_to_all | solution.py:243
  103.9 33.2 %all_gather.7.rest_0_ = s16[8,72,512]{2,1,0:T(8,128)(2,1)S(1)} all-gather(s16[1,72,512]{2,1,0:T(8,128)(2,1)S(1)} %shard_map.106), channel_id=1, replica_groups=mesh['xl'=2,'y'=4,'c'=2,'xh'=2,'zh'=4,'zm'=2,'zl'=2] {'zh','zm'}, dimensions={0}, use_global_device_ids=true | all-gather | bytes 663552 | tf_op jit(solution)/shard_map/all_gather | solution.py:245
  137.1 3.3 %collective-permute-start.10 = (s16[8,72,512]{2,1,0:T(8,128)(2,1)S(1)}, s16[8,72,512]{2,1,0:T(8,128)(2,1)S(1)}, u32[]{:S(2)}, u32[]{:S(2)}) collective-permute-start(s16[8,72,512]{2,1,0:T(8,128)(2,1)S(1)} %all_gather.7.rest_0_), channel_id=1, source_target_pairs={{0,16},{16,0},{1,17},{17,1},{2,18},{18,2},{3,19},{19,3},{4,20},{20... | collective-permute-start | bytes 1769480 | tf_op jit(solution)/shard_map/ppermute | solution.py:26
  140.4 2.1 %shard_map.108 = s16[2,16,72,256]{3,2,1,0:T(8,128)(2,1)} custom-call(s32[8]{0:T(128)S(1)} %pad_add_fusion.where, s16[16,72,512]{2,1,0:T(8,128)(2,1)S(1)} %all-to-all-done.2.w), custom_call_target="tpu_custom_call" | custom-call | bytes 2359328 | tf_op jit(solution)/shard_map/pallas_call | solution.py:37
  142.5 6.9 %all-to-all-start.3 = ((s16[32,72,256]{2,1,0:T(8,128)(2,1)}), s16[32,72,256]{2,1,0:T(8,128)(2,1)S(1)}, u32[]{:S(2)}, u32[]{:S(2)}) async-start(s16[32,72,256]{2,1,0:T(8,128)(2,1)} %bitcast.11), calls=%async_computation.3 | async-start | bytes 2359296 | tf_op jit(solution)/shard_map/all_to_all | solution.py:254
  149.4 2.6 %collective-permute-done.10.rest_2_ = s16[8,72,512]{2,1,0:T(8,128)(2,1)S(1)} collective-permute-done((s16[8,72,512]{2,1,0:T(8,128)(2,1)S(1)}, s16[8,72,512]{2,1,0:T(8,128)(2,1)S(1)}, u32[]{:S(2)}, u32[]{:S(2)}) %collective-permute-start.10) | collective-permute-done | bytes 589856 | tf_op jit(solution)/shard_map/ppermute | solution.py:26
  152.0 4.0 %collective-permute-start.11 = (s16[8,72,512]{2,1,0:T(8,128)(2,1)S(1)}, s16[8,72,512]{2,1,0:T(8,128)(2,1)S(1)}, u32[]{:S(2)}, u32[]{:S(2)}) collective-permute-start(s16[8,72,512]{2,1,0:T(8,128)(2,1)S(1)} %all_gather.7.rest_0_), channel_id=1, source_target_pairs={{0,1},{1,0},{2,3},{3,2},{4,5},{5,4},{6,7},{7,6},{8,9},{9,8},{10,11... | collective-permute-start | bytes 1769480 | tf_op jit(solution)/shard_map/ppermute | solution.py:249
  156.0 0.9 fusion
  156.9 1.9 %collective-permute-start.12 = (s16[4,72,512]{2,1,0:T(8,128)(2,1)}, s16[4,72,512]{2,1,0:T(8,128)(2,1)S(1)}, u32[]{:S(2)}, u32[]{:S(2)}) collective-permute-start(s16[4,72,512]{2,1,0:T(8,128)(2,1)} %get-tuple-element.47), channel_id=1, source_target_pairs={{0,1},{1,2},{2,3},{3,4},{4,5},{5,6},{6,7},{7,8},{8,9},{9,10},{10,1... | collective-permute-start | bytes 884744 | tf_op jit(solution)/shard_map/ppermute | solution.py:22
  158.8 5.1 %collective-permute-start.13 = (s16[4,72,512]{2,1,0:T(8,128)(2,1)}, s16[4,72,512]{2,1,0:T(8,128)(2,1)S(1)}, u32[]{:S(2)}, u32[]{:S(2)}) collective-permute-start(s16[4,72,512]{2,1,0:T(8,128)(2,1)} %get-tuple-element.46), channel_id=1, source_target_pairs={{0,15},{1,0},{2,1},{3,2},{4,3},{5,4},{6,5},{7,6},{8,7},{9,8},{10,9... | collective-permute-start | bytes 884744 | tf_op jit(solution)/shard_map/ppermute | solution.py:22
  163.9 1.6 all-to-all-done.3.w
  165.5 0.7 shard_map.109
  166.3 4.7 %collective-permute-done.12.rest_3_ = s16[4,72,512]{2,1,0:T(8,128)(2,1)S(1)} collective-permute-done((s16[4,72,512]{2,1,0:T(8,128)(2,1)}, s16[4,72,512]{2,1,0:T(8,128)(2,1)S(1)}, u32[]{:S(2)}, u32[]{:S(2)}) %collective-permute-start.12) | collective-permute-done | bytes 294944 | tf_op jit(solution)/shard_map/ppermute | solution.py:22
  171.0 2.1 %collective-permute-done.13.rest_4_ = s16[4,72,512]{2,1,0:T(8,128)(2,1)S(1)} collective-permute-done((s16[4,72,512]{2,1,0:T(8,128)(2,1)}, s16[4,72,512]{2,1,0:T(8,128)(2,1)S(1)}, u32[]{:S(2)}, u32[]{:S(2)}) %collective-permute-start.13) | collective-permute-done | bytes 294944 | tf_op jit(solution)/shard_map/ppermute | solution.py:22
  173.0 6.7 %shard_map.110 = (f32[512,256]{1,0:T(8,128)}, f32[512,256]{1,0:T(8,128)}) custom-call(s32[8]{0:T(128)S(1)} %pad_add_fusion.where, bf16[2,256,1024]{2,1,0:T(8,128)(2,1)S(1)} %get-tuple-element.41.act_high, bf16[2,256,1024]{2,1,0:T(8,128)(2,1)S(1)} %get-tuple-element.42.act_low, s16[8,72,512]{2,1,0:T(8,128)(2,1)S(1)} %all_gather.7.rest_0_, ...), custom_call_target="tpu_custom_call" | custom-call | flops 2818572288 | bytes 5505056 | tf_op jit(solution)/shard_map/pallas_call | solution.py:37
  (20 shorter events, 0.1 us)
Async XLA Ops:
  2.5 9.8 %copy-start.2 = (bf16[256,512]{1,0:T(8,128)(2,1)S(1)}, bf16[256,512]{1,0:T(8,128)(2,1)}, u32[]{:S(2)}) copy-start(bf16[256,512]{1,0:T(8,128)(2,1)} %qb.1) | copy-start | bytes 786436
  2.5 9.8 %copy-start.3 = (bf16[256,512]{1,0:T(8,128)(2,1)S(1)}, bf16[256,512]{1,0:T(8,128)(2,1)}, u32[]{:S(2)}) copy-start(bf16[256,512]{1,0:T(8,128)(2,1)} %ob.1) | copy-start | bytes 786436
  2.5 13.1 %copy-start.4 = (bf16[32,512]{1,0:T(8,128)(2,1)S(1)}, bf16[32,512]{1,0:T(8,128)(2,1)}, u32[]{:S(2)}) copy-start(bf16[32,512]{1,0:T(8,128)(2,1)} %param.14) | copy-start | bytes 98308
  2.5 13.1 %copy-start.5 = (bf16[32,512]{1,0:T(8,128)(2,1)S(1)}, bf16[32,512]{1,0:T(8,128)(2,1)}, u32[]{:S(2)}) copy-start(bf16[32,512]{1,0:T(8,128)(2,1)} %param.10) | copy-start | bytes 98308
  2.5 38.2 %copy-start.6 = (s32[1024]{0:T(1024)S(1)}, s32[1024]{0:T(1024)}, u32[]{:S(2)}) copy-start(s32[1024]{0:T(1024)} %param.9) | copy-start | bytes 12292
  2.5 38.4 %all-to-all-start = ((bf16[32,64,256]{2,1,0:T(8,128)(2,1)}), bf16[32,64,256]{2,1,0:T(8,128)(2,1)S(1)}, u32[]{:S(2)}, u32[]{:S(2)}) async-start(bf16[32,64,256]{2,1,0:T(8,128)(2,1)} %bitcast.4), calls=%async_computation | async-start | bytes 2097152 | tf_op jit(solution)/shard_map/all_to_all | solution.py:213
  12.4 28.6 %collective-permute-start = (bf16[256,512]{1,0:T(8,128)(2,1)S(1)}, bf16[256,512]{1,0:T(8,128)(2,1)S(1)}, u32[]{:S(2)}, u32[]{:S(2)}) collective-permute-start(bf16[256,512]{1,0:T(8,128)(2,1)S(1)} %broadcast_select_fusion), channel_id=1, source_target_pairs={{0,16},{16,0},{1,17},{17,1},{2,18},{18,2},{3,19},{19,3},{4,20},{20... | collective-permute-start | bytes 786440 | tf_op jit(solution)/shard_map/ppermute | solution.py:26
  42.2 27.4 %copy-start = (bf16[512,256]{1,0:T(8,128)(2,1)S(1)}, bf16[512,256]{1,0:T(8,128)(2,1)}, u32[]{:S(2)}) copy-start(bf16[512,256]{1,0:T(8,128)(2,1)} %qa) | copy-start | bytes 786436
  42.2 27.4 %copy-start.1 = (bf16[512,256]{1,0:T(8,128)(2,1)S(1)}, bf16[512,256]{1,0:T(8,128)(2,1)}, u32[]{:S(2)}) copy-start(bf16[512,256]{1,0:T(8,128)(2,1)} %oa) | copy-start | bytes 786436
  42.2 19.6 %collective-permute-start.1 = (s16[4,72,512]{2,1,0:T(8,128)(2,1)S(1)}, s16[4,72,512]{2,1,0:T(8,128)(2,1)S(1)}, u32[]{:S(2)}, u32[]{:S(2)}) collective-permute-start(s16[4,72,512]{2,1,0:T(8,128)(2,1)S(1)} %get-tuple-element.29), channel_id=1, source_target_pairs={{0,1},{1,2},{2,3},{3,4},{4,5},{5,6},{6,7},{7,8},{8,9},{9,10},{10,1... | collective-permute-start | bytes 884744 | tf_op jit(solution)/shard_map/ppermute | solution.py:22
  45.2 16.6 %collective-permute-start.2 = (s16[4,72,512]{2,1,0:T(8,128)(2,1)S(1)}, s16[4,72,512]{2,1,0:T(8,128)(2,1)S(1)}, u32[]{:S(2)}, u32[]{:S(2)}) collective-permute-start(s16[4,72,512]{2,1,0:T(8,128)(2,1)S(1)} %get-tuple-element.30), channel_id=1, source_target_pairs={{0,15},{1,0},{2,1},{3,2},{4,3},{5,4},{6,5},{7,6},{8,7},{9,8},{10,9... | collective-permute-start | bytes 884744 | tf_op jit(solution)/shard_map/ppermute | solution.py:22
  49.4 10.4 %collective-permute-start.3 = (s16[2,72,512]{2,1,0:T(8,128)(2,1)S(1)}, s16[2,72,512]{2,1,0:T(8,128)(2,1)S(1)}, u32[]{:S(2)}, u32[]{:S(2)}) collective-permute-start(s16[2,72,512]{2,1,0:T(8,128)(2,1)S(1)} %get-tuple-element.31), channel_id=1, source_target_pairs={{0,2},{1,3},{2,4},{3,5},{4,6},{5,7},{6,8},{7,9},{8,10},{9,11},{10,... | collective-permute-start | bytes 442376 | tf_op jit(solution)/shard_map/ppermute | solution.py:22
  51.6 10.3 %collective-permute-start.4 = (s16[2,72,512]{2,1,0:T(8,128)(2,1)S(1)}, s16[2,72,512]{2,1,0:T(8,128)(2,1)S(1)}, u32[]{:S(2)}, u32[]{:S(2)}) collective-permute-start(s16[2,72,512]{2,1,0:T(8,128)(2,1)S(1)} %get-tuple-element.32), channel_id=1, source_target_pairs={{0,14},{1,15},{2,0},{3,1},{4,2},{5,3},{6,4},{7,5},{8,6},{9,7},{10,... | collective-permute-start | bytes 442376 | tf_op jit(solution)/shard_map/ppermute | solution.py:22
  62.9 35.0 %all-to-all-start.1 = ((s16[4,72,512]{2,1,0:T(8,128)(2,1)}), s16[4,72,512]{2,1,0:T(8,128)(2,1)S(1)}, u32[]{:S(2)}, u32[]{:S(2)}) async-start(s16[4,72,512]{2,1,0:T(8,128)(2,1)} %shard_map.105), calls=%async_computation.1 | async-start | bytes 589824 | tf_op jit(solution)/shard_map/all_to_all | solution.py:233
  69.6 25.8 %collective-permute-start.9 = (bf16[2,512,256]{2,1,0:T(8,128)(2,1)S(1)}, bf16[2,512,256]{2,1,0:T(8,128)(2,1)S(1)}, u32[]{:S(2)}, u32[]{:S(2)}) collective-permute-start(bf16[2,512,256]{2,1,0:T(8,128)(2,1)S(1)} %pad_maximum_fusion), channel_id=1, source_target_pairs={{0,16},{16,0},{1,17},{17,1},{2,18},{18,2},{3,19},{19,3},{4,20},{20... | collective-permute-start | bytes 1572872 | tf_op jit(solution)/shard_map/ppermute | solution.py:26
  73.7 21.8 %collective-permute-start.5 = (bf16[4,2,32,512]{3,2,1,0:T(8,128)(2,1)S(1)}, bf16[4,2,32,512]{3,2,1,0:T(8,128)(2,1)S(1)}, u32[]{:S(2)}, u32[]{:S(2)}) collective-permute-start(bf16[4,2,32,512]{3,2,1,0:T(8,128)(2,1)S(1)} %bitcast.12), channel_id=1, source_target_pairs={{0,1},{1,2},{2,3},{3,4},{4,5},{5,6},{6,7},{7,8},{8,9},{9,10},{10,1... | collective-permute-start | bytes 786440 | tf_op jit(solution)/shard_map/ppermute | solution.py:22
  75.9 19.6 %collective-permute-start.6 = (bf16[4,2,32,512]{3,2,1,0:T(8,128)(2,1)S(1)}, bf16[4,2,32,512]{3,2,1,0:T(8,128)(2,1)S(1)}, u32[]{:S(2)}, u32[]{:S(2)}) collective-permute-start(bf16[4,2,32,512]{3,2,1,0:T(8,128)(2,1)S(1)} %bitcast.13), channel_id=1, source_target_pairs={{0,15},{1,0},{2,1},{3,2},{4,3},{5,4},{6,5},{7,6},{8,7},{9,8},{10,9... | collective-permute-start | bytes 786440 | tf_op jit(solution)/shard_map/ppermute | solution.py:22
  82.8 12.4 %collective-permute-start.7 = (bf16[2,2,32,512]{3,2,1,0:T(8,128)(2,1)S(1)}, bf16[2,2,32,512]{3,2,1,0:T(8,128)(2,1)S(1)}, u32[]{:S(2)}, u32[]{:S(2)}) collective-permute-start(bf16[2,2,32,512]{3,2,1,0:T(8,128)(2,1)S(1)} %get-tuple-element.49), channel_id=1, source_target_pairs={{0,2},{1,3},{2,4},{3,5},{4,6},{5,7},{6,8},{7,9},{8,10},{9,11},{10,... | collective-permute-start | bytes 393224 | tf_op jit(solution)/shard_map/ppermute | solution.py:22
  85.6 9.9 %collective-permute-start.8 = (bf16[2,2,32,512]{3,2,1,0:T(8,128)(2,1)S(1)}, bf16[2,2,32,512]{3,2,1,0:T(8,128)(2,1)S(1)}, u32[]{:S(2)}, u32[]{:S(2)}) collective-permute-start(bf16[2,2,32,512]{3,2,1,0:T(8,128)(2,1)S(1)} %get-tuple-element.48), channel_id=1, source_target_pairs={{0,14},{1,15},{2,0},{3,1},{4,2},{5,3},{6,4},{7,5},{8,6},{9,7},{10,... | collective-permute-start | bytes 393224 | tf_op jit(solution)/shard_map/ppermute | solution.py:22
  98.1 42.2 %all-to-all-start.2 = ((s16[16,72,512]{2,1,0:T(8,128)(2,1)}), s16[16,72,512]{2,1,0:T(8,128)(2,1)S(1)}, u32[]{:S(2)}, u32[]{:S(2)}) async-start(s16[16,72,512]{2,1,0:T(8,128)(2,1)} %shard_map.107), calls=%async_computation.2 | async-start | bytes 2359296 | tf_op jit(solution)/shard_map/all_to_all | solution.py:243
  137.1 14.9 %collective-permute-start.10 = (s16[8,72,512]{2,1,0:T(8,128)(2,1)S(1)}, s16[8,72,512]{2,1,0:T(8,128)(2,1)S(1)}, u32[]{:S(2)}, u32[]{:S(2)}) collective-permute-start(s16[8,72,512]{2,1,0:T(8,128)(2,1)S(1)} %all_gather.7.rest_0_), channel_id=1, source_target_pairs={{0,16},{16,0},{1,17},{17,1},{2,18},{18,2},{3,19},{19,3},{4,20},{20... | collective-permute-start | bytes 1769480 | tf_op jit(solution)/shard_map/ppermute | solution.py:26
  142.5 23.0 %all-to-all-start.3 = ((s16[32,72,256]{2,1,0:T(8,128)(2,1)}), s16[32,72,256]{2,1,0:T(8,128)(2,1)S(1)}, u32[]{:S(2)}, u32[]{:S(2)}) async-start(s16[32,72,256]{2,1,0:T(8,128)(2,1)} %bitcast.11), calls=%async_computation.3 | async-start | bytes 2359296 | tf_op jit(solution)/shard_map/all_to_all | solution.py:254
  152.0 21.1 %collective-permute-start.11 = (s16[8,72,512]{2,1,0:T(8,128)(2,1)S(1)}, s16[8,72,512]{2,1,0:T(8,128)(2,1)S(1)}, u32[]{:S(2)}, u32[]{:S(2)}) collective-permute-start(s16[8,72,512]{2,1,0:T(8,128)(2,1)S(1)} %all_gather.7.rest_0_), channel_id=1, source_target_pairs={{0,1},{1,0},{2,3},{3,2},{4,5},{5,4},{6,7},{7,6},{8,9},{9,8},{10,11... | collective-permute-start | bytes 1769480 | tf_op jit(solution)/shard_map/ppermute | solution.py:249
  156.9 14.1 %collective-permute-start.12 = (s16[4,72,512]{2,1,0:T(8,128)(2,1)}, s16[4,72,512]{2,1,0:T(8,128)(2,1)S(1)}, u32[]{:S(2)}, u32[]{:S(2)}) collective-permute-start(s16[4,72,512]{2,1,0:T(8,128)(2,1)} %get-tuple-element.47), channel_id=1, source_target_pairs={{0,1},{1,2},{2,3},{3,4},{4,5},{5,6},{6,7},{7,8},{8,9},{9,10},{10,1... | collective-permute-start | bytes 884744 | tf_op jit(solution)/shard_map/ppermute | solution.py:22
  158.8 14.2 %collective-permute-start.13 = (s16[4,72,512]{2,1,0:T(8,128)(2,1)}, s16[4,72,512]{2,1,0:T(8,128)(2,1)S(1)}, u32[]{:S(2)}, u32[]{:S(2)}) collective-permute-start(s16[4,72,512]{2,1,0:T(8,128)(2,1)} %get-tuple-element.46), channel_id=1, source_target_pairs={{0,15},{1,0},{2,1},{3,2},{4,3},{5,4},{6,5},{7,6},{8,7},{9,8},{10,9... | collective-permute-start | bytes 884744 | tf_op jit(solution)/shard_map/ppermute | solution.py:22
